TPU v7x, 512 devices: a whole 4x4x16 slice. The times are simulated.
512 devices in a mesh: ctx: 32 (over y_hi, z), tp: 16 (over y_lo, x, core).
Axes of the slice: x: 4, y: 4 (y_hi: 2, y_lo: 2; y = y_hi * 2 + y_lo), z: 16, core: 2. Of those that a mesh axis runs over, the one named last changes fastest.
Arguments:
- query_rows: bfloat16 [4096, 1024], P('ctx', 'tp'), may hold values from -12 to 12
- key_rows: bfloat16 [4096, 1024], P('ctx', 'tp'), may hold values from -6 to 6
- value_rows: bfloat16 [4096, 1024], P('ctx', 'tp'), may hold values from -6 to 6
- valid_frames: int32 [1], replicated, may hold values from 3072 to 4096
- depth_kernel: float32 [32, 1024], P(None, 'tp'), may hold values from -1 to 1
- mix_weight: bfloat16 [1024, 1536], P('tp'), may hold values from -0.1875 to 0.1875
- out_grad: bfloat16 [4096, 1536], P(('ctx', 'tp')), may hold values from -6 to 6
Outputs:
- block_out: bfloat16 [4096, 1536], P(('ctx', 'tp'))
- query_grad: bfloat16 [4096, 1024], P('ctx', 'tp')
- key_grad: bfloat16 [4096, 1024], P('ctx', 'tp')
- value_grad: bfloat16 [4096, 1024], P('ctx', 'tp')
- mix_grad: float32 [1024, 1536], P('tp')
- kernel_grad: float32 [32, 1024], P(None, 'tp')
Inputs may be any that keep to these rules, and one draw needn't show every extreme that they name: Frames from valid_frames on are padding.
All inputs are finite; a program needn't handle non-finite values.
Results may differ from a plain program's by a relative error of at most 0.039.
Values may be sent and summed in bfloat16 or wider, within the bound.
No kernel may reach another device: no remote copies, remote signals or barrier semaphores. Data moves between devices by JAX's collectives and lax.ppermute only.
A program may use at most 64 MiB of HBM per device.

v0:
```python
import jax
import jax.numpy as jnp
from jax import lax
from jax.sharding import PartitionSpec as P

KSIZE = 32


def with_halo(block, sides, width):
    for axis, dim in sides:
        count = lax.axis_size(axis)
        forward = [(i, i + 1) for i in range(count - 1)]
        backward = [(target, source) for source, target in forward]
        low = lax.ppermute(
            lax.slice_in_dim(block, block.shape[dim] - width, None, axis=dim), axis, forward
        )
        high = lax.ppermute(lax.slice_in_dim(block, 0, width, axis=dim), axis, backward)
        block = jnp.concatenate([low, block, high], axis=dim)
    return block


def body(query_rows, key_rows, value_rows, valid_frames, depth_kernel, mix_weight, out_grad):
    frames_dev = query_rows.shape[0]
    head_width = query_rows.shape[1]
    score_scale = head_width ** (-0.5)
    total_frames = frames_dev * lax.axis_size("ctx")
    grad_norm = total_frames ** (-0.5)
    valid_count = valid_frames[0]
    own_ids = lax.axis_index("ctx") * frames_dev + jnp.arange(frames_dev, dtype=jnp.int32)
    own_live = own_ids < valid_count
    key_value = jnp.concatenate([key_rows, value_rows], axis=1)
    contract_last = (((1,), (1,)), ((), ()))
    key_piece = lax.all_gather(key_rows, "ctx", axis=0, tiled=True)
    run_max = jnp.full((frames_dev,), -1e30, jnp.float32)
    key_part = key_piece
    key_live = jnp.arange(key_piece.shape[0], dtype=jnp.int32) < valid_count
    scores = score_scale * lax.dot_general(
        query_rows, key_part, contract_last, preferred_element_type=jnp.float32
    )
    capped = jnp.where(key_live[None, :], scores, -1e30)
    new_max = jnp.maximum(run_max, jnp.max(capped, axis=1))
    weights = jnp.where(key_live[None, :], jnp.exp(capped - new_max[:, None]), 0.0)
    run_total = jnp.sum(weights, axis=1)
    run_max, run_total = (new_max, run_total)
    log_total = run_max + jnp.log(run_total)
    key_piece = lax.all_gather(key_value, "ctx", axis=0, tiled=True)
    key_part = key_piece[:, :head_width]
    value_part = key_piece[:, head_width:]
    key_live = jnp.arange(key_piece.shape[0], dtype=jnp.int32) < valid_count
    scores = score_scale * lax.dot_general(
        query_rows, key_part, contract_last, preferred_element_type=jnp.float32
    )
    capped = jnp.where(key_live[None, :], scores, -1e30)
    probs = jnp.where(key_live[None, :], jnp.exp(capped - log_total[:, None]), 0.0).astype(
        jnp.bfloat16
    )
    run_out = jnp.dot(probs, value_part, preferred_element_type=jnp.float32)
    attn = run_out.astype(jnp.bfloat16)
    masked = jnp.where(own_live[:, None], attn, jnp.zeros_like(attn))
    rim_width = KSIZE // 2
    padded_attn = with_halo(masked, (("ctx", 0),), rim_width)
    depth_out = jnp.zeros((frames_dev, head_width), jnp.float32)
    for offset in range(KSIZE):
        depth_out = depth_out + depth_kernel[offset][None, :] * padded_attn[
            offset : offset + frames_dev
        ].astype(jnp.float32)
    swished = (depth_out * jax.nn.sigmoid(depth_out)).astype(jnp.bfloat16)
    channel_rows = lax.all_to_all(swished, "tp", split_axis=0, concat_axis=1, tiled=True)
    full_weight = lax.all_gather(mix_weight, "tp", axis=0, tiled=True)
    block_out = jnp.dot(channel_rows, full_weight, preferred_element_type=jnp.float32).astype(
        jnp.bfloat16
    )
    grad_block = lax.all_gather(out_grad, "tp", axis=0, tiled=True)
    mix_back = lax.dot_general(
        grad_block, mix_weight, contract_last, preferred_element_type=jnp.float32
    )
    gate_sig = jax.nn.sigmoid(depth_out)
    depth_grad = (mix_back * gate_sig * (1.0 + depth_out * (1.0 - gate_sig))).astype(jnp.bfloat16)
    mix_part = lax.dot_general(
        swished, grad_block, (((0,), (0,)), ((), ())), preferred_element_type=jnp.float32
    )
    depth_grad_wide = depth_grad.astype(jnp.float32)
    kernel_rows = []
    for offset in range(KSIZE):
        kernel_rows.append(
            jnp.sum(
                padded_attn[offset : offset + frames_dev].astype(jnp.float32) * depth_grad_wide,
                axis=0,
            )
        )
    kernel_part = jnp.stack(kernel_rows, axis=0)
    mix_total, kernel_total = (
        lax.psum(mix_part.astype(jnp.bfloat16), "ctx").astype(jnp.float32),
        lax.psum(kernel_part.astype(jnp.bfloat16), "ctx").astype(jnp.float32),
    )
    mix_grad = grad_norm * mix_total
    kernel_grad = grad_norm * kernel_total
    padded_grad = with_halo(depth_grad, (("ctx", 0),), rim_width)
    back_sum = jnp.zeros((frames_dev, head_width), jnp.float32)
    for offset in range(KSIZE):
        first_row = 2 * rim_width - offset
        back_sum = back_sum + depth_kernel[offset][None, :] * padded_grad[
            first_row : first_row + frames_dev
        ].astype(jnp.float32)
    attn_grad = jnp.where(own_live[:, None], back_sum, jnp.zeros_like(back_sum)).astype(
        jnp.bfloat16
    )
    delta = jnp.sum(attn_grad.astype(jnp.float32) * attn.astype(jnp.float32), axis=1)
    key_piece = lax.all_gather(key_value, "ctx", axis=0, tiled=True)
    key_part = key_piece[:, :head_width]
    value_part = key_piece[:, head_width:]
    key_live = jnp.arange(key_piece.shape[0], dtype=jnp.int32) < valid_count
    scores = score_scale * lax.dot_general(
        query_rows, key_part, contract_last, preferred_element_type=jnp.float32
    )
    capped = jnp.where(key_live[None, :], scores, -1e30)
    weights = jnp.where(key_live[None, :], jnp.exp(capped - log_total[:, None]), 0.0)
    dprobs = lax.dot_general(
        attn_grad, value_part, contract_last, preferred_element_type=jnp.float32
    )
    dscores = (weights * (dprobs - delta[:, None])).astype(jnp.bfloat16)
    query_total = score_scale * jnp.dot(dscores, key_part, preferred_element_type=jnp.float32)
    query_grad = query_total.astype(jnp.bfloat16)
    query_and_grad = jnp.concatenate([query_rows, attn_grad], axis=1)
    row_stats = jnp.stack([log_total, delta], axis=1)
    all_stats = lax.all_gather(row_stats, "ctx", axis=0, tiled=True)
    rows_piece = lax.all_gather(query_and_grad, "ctx", axis=0, tiled=True)
    query_piece = rows_piece[:, :head_width]
    grad_piece = rows_piece[:, head_width:]
    total_piece = all_stats[:, 0]
    delta_piece = all_stats[:, 1]
    scores = score_scale * lax.dot_general(
        key_rows, query_piece, contract_last, preferred_element_type=jnp.float32
    )
    capped = jnp.where(own_live[:, None], scores, -1e30)
    weights = jnp.where(own_live[:, None], jnp.exp(capped - total_piece[None, :]), 0.0)
    dprobs = lax.dot_general(
        value_rows, grad_piece, contract_last, preferred_element_type=jnp.float32
    )
    dscores = (weights * (dprobs - delta_piece[None, :])).astype(jnp.bfloat16)
    key_total = score_scale * jnp.dot(dscores, query_piece, preferred_element_type=jnp.float32)
    value_total = jnp.dot(
        weights.astype(jnp.bfloat16), grad_piece, preferred_element_type=jnp.float32
    )
    key_total, value_total = (key_total, value_total)
    return (
        block_out,
        query_grad,
        key_total.astype(jnp.bfloat16),
        value_total.astype(jnp.bfloat16),
        mix_grad,
        kernel_grad,
    )


def solution(mesh):
    placed = (
        P("ctx", "tp"),
        P("ctx", "tp"),
        P("ctx", "tp"),
        P(),
        P(None, "tp"),
        P("tp", None),
        P(("ctx", "tp"), None),
    )
    return jax.shard_map(
        body,
        mesh=mesh,
        in_specs=placed,
        out_specs=(
            P(("ctx", "tp"), None),
            P("ctx", "tp"),
            P("ctx", "tp"),
            P("ctx", "tp"),
            P("tp", None),
            P(None, "tp"),
        ),
        check_vma=False,
    )
```

profile of v0, /device:TPU:1, one launch (start us, length us, event | category | flops | bytes accessed | tf_op | source)
XLA Modules:
  0.0 650.3 jit_solution(8706354773599395544)
XLA Ops:
  7.2 1.4 pad_maximum_fusion
  9.3 72.7 %all_gather.20 = bf16[4096,64]{0,1:T(8,128)(2,1)S(1)} all-gather(bf16[128,64]{0,1:T(8,128)(2,1)} %param.8), channel_id=1, replica_groups=mesh['ctx'=32,'tp'=16] {'ctx'}, dimensions={0}, use_global_device_ids=true | all-gather | bytes 540672 | tf_op jit(solution)/shard_map/all_gather | solution.py:33
  82.1 1.3 fusion.177
  83.4 0.5 select_reduce_fusion
  84.0 58.7 %all-gather.4.cloned.1.call-done = bf16[4096,128]{0,1:T(8,128)(2,1)} async-done(((bf16[128,128]{0,1:T(8,128)(2,1)}), bf16[4096,128]{0,1:T(8,128)(2,1)}) %all-gather.4.cloned.1.call-update) | async-done | bytes 1048592 | tf_op jit(solution)/shard_map/all_gather | solution.py:46
  142.7 3.0 fusion.8
  146.1 1.3 collective-permute-start.1
  147.4 4.0 collective-permute-start
  151.4 30.7 %all_gather.22 = bf16[128,1536]{1,0:T(8,128)(2,1)S(1)} all-gather(bf16[8,1536]{1,0:T(8,128)(2,1)S(1)} %copy-done.6), channel_id=1, replica_groups=mesh['ctx'=32,'tp'=16] {'tp'}, dimensions={0}, use_global_device_ids=true | all-gather | bytes 417792 | tf_op jit(solution)/shard_map/all_gather | solution.py:73
  182.1 0.6 multiply_convert_fusion
  182.7 0.5 fusion.97
  183.3 2.9 collective-permute-start.3
  186.2 1.3 collective-permute-start.2
  187.5 0.9 convolution_convert_fusion
  188.5 2.2 collective-permute-done.2
  190.7 0.6 multiply_reduce_fusion
  191.3 0.6 pad_maximum_fusion.1
  192.0 0.5 all-gather.6.cloned.1.call-update
  192.6 0.7 reshape.50
  193.3 4.9 all-to-all-start
  199.5 62.3 %psum.15 = bf16[32,64]{1,0:T(8,128)(2,1)S(1)} all-reduce(bf16[32,64]{1,0:T(8,128)(2,1)S(1)} %stack.170), channel_id=1, replica_groups=mesh['ctx'=32,'tp'=16] {'ctx'}, use_global_device_ids=true, to_apply=%region_36.37 | all-reduce | flops 2048 | bytes 8192 | tf_op jit(solution)/shard_map/psum | solution.py:94
  261.8 0.6 convert_multiply_fusion.66
  262.4 58.0 %all_gather.24 = f32[4096,2]{0,1:T(2,128)S(1)} all-gather(f32[128,2]{0,1:T(2,128)S(1)} %pad_maximum_fusion.6), channel_id=1, replica_groups=mesh['ctx'=32,'tp'=16] {'ctx'}, dimensions={0}, use_global_device_ids=true | all-gather | bytes 33792 | tf_op jit(solution)/shard_map/all_gather | solution.py:126
  320.4 1.4 fusion.21
  322.1 127.2 %all-reduce.2.cloned.1.call-done = bf16[64,1536]{1,0:T(8,128)(2,1)} async-done(((bf16[64,1536]{1,0:T(8,128)(2,1)}), bf16[64,1536]{1,0:T(8,128)(2,1)}) %all-reduce.2.cloned.1.call-update) | async-done | bytes 196624 | tf_op jit(solution)/shard_map/psum | solution.py:93
  449.3 1.7 convert_multiply_fusion
  451.0 139.8 %all-gather.8.cloned.1.call-done = bf16[4096,128]{0,1:T(8,128)(2,1)} async-done(((bf16[128,128]{0,1:T(8,128)(2,1)}), bf16[4096,128]{0,1:T(8,128)(2,1)}) %all-gather.8.cloned.1.call-update) | async-done | bytes 1048592 | tf_op jit(solution)/shard_map/all_gather | solution.py:127
  590.8 2.1 fusion.11
  592.9 0.9 convolution_convert_fusion.2
  593.8 1.7 fusion.20
  595.5 45.2 %all-gather.6.cloned.1.call-done = bf16[1024,1536]{1,0:T(8,128)(2,1)} async-done(((bf16[64,1536]{1,0:T(8,128)(2,1)}), bf16[1024,1536]{1,0:T(8,128)(2,1)}) %all-gather.6.cloned.1.call-update) | async-done | bytes 3145744 | tf_op jit(solution)/shard_map/all_gather | solution.py:69
  640.7 3.0 convolution_convert_fusion.1
  (46 shorter events, 2.3 us)
Async XLA Ops:
  7.2 135.6 %all-gather.4.cloned.1.call-start = ((), (), s32[]{:S(2)}) async-start(), calls=%async_computation.1 | async-start | bytes 1081344 | tf_op jit(solution)/shard_map/all_gather | solution.py:46
  8.6 440.7 %all-reduce.2.cloned.1.call-start = ((), (), s32[]{:S(2)}) async-start(), calls=%async_computation.4 | async-start | bytes 393216 | tf_op jit(solution)/shard_map/psum | solution.py:93
  82.1 1.9 copy-start.7
  82.1 60.7 %copy-start.3 = (bf16[128,64]{0,1:T(8,128)(2,1)S(1)}, bf16[128,64]{0,1:T(8,128)(2,1)}, u32[]{:S(2)}) copy-start(bf16[128,64]{0,1:T(8,128)(2,1)} %param.7) | copy-start | bytes 49156
  142.7 3.0 copy-start.1
  145.7 5.7 copy-start.6
  145.7 37.0 %copy-start.2 = (bf16[64,1536]{1,0:T(8,128)(2,1)S(1)}, bf16[64,1536]{1,0:T(8,128)(2,1)}, u32[]{:S(2)}) copy-start(bf16[64,1536]{1,0:T(8,128)(2,1)} %param.12) | copy-start | bytes 589828
  146.1 36.0 %collective-permute-start.1 = (bf16[16,64]{0,1:T(8,128)(2,1)S(1)}, bf16[16,64]{0,1:T(8,128)(2,1)S(1)}, u32[]{:S(2)}, u32[]{:S(2)}) collective-permute-start(bf16[16,64]{0,1:T(8,128)(2,1)S(1)} %get-tuple-element.79), channel_id=1, source_target_pairs={{16,0},{32,16},{48,32},{64,48},{80,64},{96,80},{112,96},{128,112},... | collective-permute-start | bytes 6152 | tf_op jit(solution)/shard_map/ppermute | solution.py:17
  147.4 34.7 %collective-permute-start = (bf16[16,64]{0,1:T(8,128)(2,1)S(1)}, bf16[16,64]{0,1:T(8,128)(2,1)S(1)}, u32[]{:S(2)}, u32[]{:S(2)}) collective-permute-start(bf16[16,64]{0,1:T(8,128)(2,1)S(1)} %get-tuple-element.78), channel_id=1, source_target_pairs={{0,16},{16,32},{32,48},{48,64},{64,80},{80,96},{96,112},{112,128},... | collective-permute-start | bytes 6152 | tf_op jit(solution)/shard_map/ppermute | solution.py:14
  183.3 5.2 collective-permute-start.3
  186.2 4.5 collective-permute-start.2
  188.4 402.4 %all-gather.8.cloned.1.call-start = ((), (), s32[]{:S(2)}) async-start(), calls=%async_computation.3 | async-start | bytes 1081344 | tf_op jit(solution)/shard_map/all_gather | solution.py:127
  191.9 448.8 %all-gather.6.cloned.1.call-start = ((), (), s32[]{:S(2)}) async-start(), calls=%async_computation.2 | async-start | bytes 3342336 | tf_op jit(solution)/shard_map/all_gather | solution.py:69
  193.3 128.5 %all-to-all-start = ((bf16[16,2,256]{2,1,0:T(2,128)(2,1)}), bf16[16,2,256]{2,1,0:T(2,128)(2,1)S(1)}, u32[]{:S(2)}, u32[]{:S(2)}) async-start(bf16[16,2,256]{2,1,0:T(2,128)(2,1)} %reshape.50), calls=%async_computation | async-start | bytes 32768 | tf_op jit(solution)/shard_map/all_to_all | solution.py:68
  199.3 391.5 %copy-start.5 = (bf16[128,64]{0,1:T(8,128)(2,1)S(1)}, bf16[128,64]{0,1:T(8,128)(2,1)}, u32[]{:S(2)}) copy-start(bf16[128,64]{0,1:T(8,128)(2,1)} %param.8) | copy-start | bytes 49156
  590.8 2.1 copy-start
  592.9 0.9 copy-start.4
Sparse Core Ops, SparseCore 0:
  11.5 131.2 all-gather.3
  188.5 260.7 all-reduce.1
  452.6 138.1 all-gather.7
  593.0 47.6 all-gather.5
where the time goes:
time: 651 us; the launch traced here: 650 us
  waiting for transfers between devices  374 us (57%)
  blocking collectives  224 us (34%)
  matrix products  15 us (2%)
  between operations  14.6 us (2%)
  starting transfers between devices  14.5 us (2%)
  other arithmetic  7.18 us (1%)
    all_gather x1, waiting for transfers between devices, body(): rows_piece = lax.all_gather(query_and_grad, 'ctx', axis=0, tiled=True)  140 us
    psum x1, waiting for transfers between devices, body(): lax.psum(mix_part.astype(jnp.bfloat16), 'ctx').astype(jnp.float32)  127 us
    all_gather x1, blocking collectives, body(): key_piece = lax.all_gather(key_rows, 'ctx', axis=0, tiled=True)  72.7 us
    psum x1, blocking collectives, body(): lax.psum(kernel_part.astype(jnp.bfloat16), 'ctx').astype(jnp.float32)  62.3 us
    all_gather x1, waiting for transfers between devices, body(): key_piece = lax.all_gather(key_value, 'ctx', axis=0, tiled=True)  58.7 us
    all_gather x1, blocking collectives, body(): all_stats = lax.all_gather(row_stats, 'ctx', axis=0, tiled=True)  58 us
    all_gather x1, waiting for transfers between devices, body(): full_weight = lax.all_gather(mix_weight, 'tp', axis=0, tiled=True)  45.2 us
    all_gather x1, blocking collectives, body(): grad_block = lax.all_gather(out_grad, 'tp', axis=0, tiled=True)  30.7 us
  transfers between devices with their start and end apart: 9, of which 5 were waited for; matrix products, arithmetic and copies ran while one was open for 2% of the time, Pallas kernels for 0%

commit v1 on v0

v1 whole, which is shorter than its diff:
```python
import functools

import jax
import jax.numpy as jnp
from jax import lax
from jax.experimental import pallas as pl
from jax.experimental.pallas import tpu as pltpu
from jax.sharding import Mesh, PartitionSpec as P

F32 = jnp.float32
BF16 = jnp.bfloat16
KSIZE = 32
RIM = KSIZE // 2
LOW = -1e30
VMEM_BYTES = 48 * 1024 * 1024


def dot00(a, b):
    return lax.dot_general(a, b, (((0,), (0,)), ((), ())), preferred_element_type=F32)


def dot10(a, b):
    return lax.dot_general(a, b, (((1,), (0,)), ((), ())), preferred_element_type=F32)


def dot11(a, b):
    return lax.dot_general(a, b, (((1,), (1,)), ((), ())), preferred_element_type=F32)


def rows_of(count, lanes, entries):
    index = lax.broadcasted_iota(jnp.int32, (count, lanes), 0)
    out = jnp.zeros((count, lanes), F32)
    for where, value in entries:
        out = jnp.where(index == where, value, out)
    return out


def split3(x):
    high = x.astype(BF16).astype(F32)
    rest = x - high
    mid = rest.astype(BF16).astype(F32)
    return high, mid, rest - mid


def call(kernel, out_shapes, flops, scratch=()):
    return pl.pallas_call(
        kernel,
        out_shape=out_shapes,
        scratch_shapes=list(scratch),
        compiler_params=pltpu.CompilerParams(vmem_limit_bytes=VMEM_BYTES),
        cost_estimate=pl.CostEstimate(flops=flops, bytes_accessed=2 ** 20, transcendentals=0),
    )


def attend(all_ref, own_ref, pair_ref, bias_ref, mine_ref, other_ref, score_ref):
    blocks = all_ref.shape[0]
    head = 64
    width = 128
    scale = head ** -0.5
    query = jnp.concatenate([own_ref[0:head], pair_ref[0:head]], axis=1).astype(F32) * scale
    query = jnp.concatenate([query, rows_of(16, 2 * width, [(6, 1.0)])], axis=0).astype(BF16)
    peak = jnp.full((1, 2 * width), LOW, F32)
    for b in range(blocks):
        key = jnp.concatenate(
            [all_ref[b, head : 2 * head], rows_of(16, width, [(6, bias_ref[b : b + 1])]).astype(BF16)], axis=0
        )
        score = dot00(key, query)
        score_ref[b] = score
        peak = jnp.maximum(peak, jnp.max(score, axis=0, keepdims=True))
    total = jnp.zeros((1, 2 * width), F32)
    out = jnp.zeros((head, 2 * width), F32)
    for b in range(blocks):
        weight = jnp.exp(score_ref[b] - peak)
        total = total + jnp.sum(weight, axis=0, keepdims=True)
        out = out + dot10(all_ref[b, 2 * head : 3 * head], weight.astype(BF16))
    out = out / total
    lse = peak + jnp.log(total)
    both = jnp.concatenate([out, jnp.broadcast_to(lse, (8, 2 * width))], axis=0)
    mine_ref[...] = both[:, :width]
    other_ref[...] = both[:, width:]


def combine(mine_ref, got_ref, live_ref, attn_ref, masked_ref, lse_ref):
    mine = mine_ref[64:65]
    got = got_ref[64:65]
    top = jnp.maximum(mine, got)
    lse = top + jnp.log(jnp.exp(mine - top) + jnp.exp(got - top))
    attn = mine_ref[0:64] * jnp.exp(mine - lse) + got_ref[0:64] * jnp.exp(got - lse)
    attn_ref[...] = attn.astype(BF16)
    masked_ref[...] = jnp.where(live_ref[...] > 0.0, attn, 0.0).astype(BF16)
    lse_ref[...] = jnp.broadcast_to(lse, lse_ref.shape)


def ring_of(own, low, high):
    lane = lax.broadcasted_iota(jnp.int32, own.shape, 1)
    side = jnp.where(lane < own.shape[1] // 2, high.astype(F32), low.astype(F32))
    return jnp.concatenate([own.astype(F32), side], axis=1)


def shifted(ring, offset):
    size = ring.shape[1]
    if offset % size == 0:
        return ring[:, : size // 2]
    return pltpu.roll(ring, (-offset) % size, 1)[:, : size // 2]


def convolve(masked_ref, low_ref, high_ref, taps_ref, weight_ref, grad_ref, swish_ref, mix_ref, dgrad_ref, tap_grad_ref):
    ring = ring_of(masked_ref[...], low_ref[...], high_ref[...])
    taps = taps_ref[...]
    depth = jnp.zeros((64, 128), F32)
    for t in range(KSIZE):
        depth = depth + taps[:, t : t + 1] * shifted(ring, t - RIM)
    gate = jax.nn.sigmoid(depth)
    swish = (depth * gate).astype(BF16)
    swish_ref[...] = (depth * gate).T.astype(BF16)
    grad = grad_ref[...]
    mix = dot10(swish, grad)
    for piece in range(mix_ref.shape[0]):
        mix_ref[piece] = mix[:, piece * 128 : (piece + 1) * 128].astype(BF16)
    back = dot11(weight_ref[...], grad)
    dgrad = (back * gate * (1.0 + depth * (1.0 - gate))).astype(BF16)
    dgrad_ref[...] = dgrad
    wide = dgrad.astype(F32)
    lane = lax.broadcasted_iota(jnp.int32, (64, 128), 1)
    sums = jnp.zeros((64, 128), F32)
    for t in range(KSIZE):
        column = jnp.sum(shifted(ring, t - RIM) * wide, axis=1, keepdims=True)
        sums = jnp.where(lane == t, column, sums)
    turned = sums.T
    tap_grad_ref[...] = jnp.concatenate([turned[0:16, 0:64], turned[16:32, 0:64]], axis=1).astype(BF16)


def deconvolve(dgrad_ref, low_ref, high_ref, taps_ref, attn_ref, live_ref, lse_ref, tap_grad_ref, pack_ref):
    ring = ring_of(dgrad_ref[...], low_ref[...], high_ref[...])
    taps = taps_ref[...]
    total = jnp.zeros((64, 128), F32)
    for t in range(KSIZE):
        total = total + taps[:, t : t + 1] * shifted(ring, RIM - t)
    grad = jnp.where(live_ref[...] > 0.0, total, 0.0).astype(BF16)
    delta = jnp.sum(grad.astype(F32) * attn_ref[...].astype(F32), axis=0, keepdims=True)
    lse = lse_ref[0:1]
    a, b, c = split3(-lse)
    d, e, f = split3(-delta)
    stats = rows_of(16, 128, [(0, a), (1, b), (2, c), (3, d), (4, e), (5, f), (6, 1.0)])
    pack_ref[...] = jnp.concatenate([grad, stats.astype(BF16), tap_grad_ref[...]], axis=0)


def backward(all_ref, packs_ref, own_ref, pair_ref, pack_own_ref, pack_pair_ref, bias_ref, pair_bias_ref, mine_ref, other_ref):
    blocks = all_ref.shape[0]
    head = 64
    width = 128
    scale = head ** -0.5
    both = jnp.concatenate([own_ref[...], pair_ref[...]], axis=1)
    packs = jnp.concatenate([pack_own_ref[0:80], pack_pair_ref[0:80]], axis=1)
    query = (both[0:head].astype(F32) * scale).astype(BF16)
    query = jnp.concatenate([query, packs[head : head + 16]], axis=0)
    ones = [(0, 1.0), (1, 1.0), (2, 1.0)]
    key_rows = rows_of(16, 2 * width, ones + [(6, pair_bias_ref[0:1])]).astype(BF16)
    key = jnp.concatenate([both[head : 2 * head], key_rows], axis=0)
    value_rows = rows_of(16, 2 * width, [(3, 1.0), (4, 1.0), (5, 1.0)]).astype(BF16)
    value = jnp.concatenate([both[2 * head : 3 * head], value_rows], axis=0)
    d_query = jnp.zeros((head, 2 * width), F32)
    d_key = jnp.zeros((head, 2 * width), F32)
    d_value = jnp.zeros((head, 2 * width), F32)
    tap_sum = jnp.zeros((16, width), F32)
    for b in range(blocks):
        key_b = all_ref[b, head : 2 * head]
        key_aug = jnp.concatenate([key_b, rows_of(16, width, ones + [(6, bias_ref[b : b + 1])]).astype(BF16)], axis=0)
        value_aug = jnp.concatenate([all_ref[b, 2 * head : 3 * head], value_rows[:, :width]], axis=0)
        weight = jnp.exp(dot00(key_aug, query))
        d_score = (weight * dot00(value_aug, packs)).astype(BF16)
        d_query = d_query + dot10(key_b, d_score)

        query_b = (all_ref[b, 0:head].astype(F32) * scale).astype(BF16)
        query_aug = jnp.concatenate([query_b, packs_ref[b, head : head + 16]], axis=0)
        weight = jnp.exp(dot00(query_aug, key))
        d_score = (weight * dot00(packs_ref[b, 0:80], value)).astype(BF16)
        d_key = d_key + dot10(query_b, d_score)
        d_value = d_value + dot10(packs_ref[b, 0:head], weight.astype(BF16))
        tap_sum = tap_sum + packs_ref[b, 80:96].astype(F32)
    d_query = d_query * scale
    for ref, at in ((mine_ref, 0), (other_ref, width)):
        ref[0:head] = d_query[:, at : at + width]
        ref[head : 2 * head] = d_key[:, at : at + width]
        ref[2 * head : 3 * head] = d_value[:, at : at + width]
        ref[3 * head : 3 * head + 16] = tap_sum


def finish(norm, mine_ref, got_ref, query_ref, key_ref, value_ref, taps_ref):
    total = mine_ref[...] + got_ref[...]
    query_ref[...] = total[0:64].astype(BF16)
    key_ref[...] = total[64:128].astype(BF16)
    value_ref[...] = total[128:192].astype(BF16)
    tap = total[192:208] * norm
    taps_ref[0:16] = tap[:, 0:64]
    taps_ref[16:32] = tap[:, 64:128]


def mix_sum(parts_ref, out_ref):
    total = jnp.zeros(out_ref.shape, F32)
    for j in range(parts_ref.shape[0]):
        total = total + parts_ref[j].astype(F32)
    out_ref[...] = total.astype(BF16)


def mix_place(norm, parts_ref, out_ref):
    for piece in range(parts_ref.shape[0]):
        out_ref[:, piece * 128 : (piece + 1) * 128] = parts_ref[piece].astype(F32) * norm


def body(query_rows, key_rows, value_rows, valid_frames, depth_kernel, mix_weight, out_grad):
    width, head = query_rows.shape
    depth = lax.axis_size("z")
    ctx = ("yh", "z")
    devices = 2 * depth
    lanes = lax.axis_size("tp")
    model = mix_weight.shape[1]
    rows8 = out_grad.shape[0]
    norm = (width * devices) ** -0.5
    valid = valid_frames[0]
    half = lax.axis_index("yh")
    spot = lax.axis_index("z")
    frame = jnp.arange(width, dtype=jnp.int32)
    half_ids = (half * depth + jnp.arange(depth, dtype=jnp.int32)[:, None]) * width + frame[None, :]
    key_bias = jnp.where(half_ids < valid, 0.0, LOW).astype(F32)
    own_ids = (half * depth + spot) * width + frame
    pair_ids = ((1 - half) * depth + spot) * width + frame
    pair_bias = jnp.where(jnp.concatenate([own_ids, pair_ids]) < valid, 0.0, LOW).astype(F32)[None, :]
    live = (own_ids < valid).astype(F32)[None, :]
    swap = [(0, 1), (1, 0)]
    up = [(i, i + 1) for i in range(devices - 1)]
    down = [(i + 1, i) for i in range(devices - 1)]
    taps = depth_kernel.T

    shared = lax.all_gather(jnp.concatenate([out_grad, mix_weight], axis=0), "tp", axis=0)
    own = jnp.concatenate([query_rows.T, key_rows.T, value_rows.T], axis=0)
    pair = lax.ppermute(own, "yh", swap)
    everyone = lax.all_gather(own, "z", axis=0)

    part = jax.ShapeDtypeStruct((head + 8, width), F32)
    block = jax.ShapeDtypeStruct((head, width), BF16)
    mine, other = call(
        attend, (part, part), 2 ** 28, [pltpu.VMEM((depth, width, 2 * width), F32)]
    )(everyone, own, pair, key_bias)
    got = lax.ppermute(other, "yh", swap)
    attn, masked, lse = call(combine, (block, block, jax.ShapeDtypeStruct((8, width), F32)), 2 ** 20)(mine, got, live)
    low = lax.ppermute(masked, ctx, up)
    high = lax.ppermute(masked, ctx, down)
    grad_block = shared[:, :rows8].reshape(lanes * rows8, model)
    swish, mix_parts, dgrad, tap_grad = call(
        convolve,
        (
            jax.ShapeDtypeStruct((width, head), BF16),
            jax.ShapeDtypeStruct((model // 128, head, 128), BF16),
            block,
            jax.ShapeDtypeStruct((16, 128), BF16),
        ),
        2 ** 26,
    )(masked, low, high, taps, mix_weight, grad_block)
    grad_low = lax.ppermute(dgrad, ctx, up)
    grad_high = lax.ppermute(dgrad, ctx, down)
    pack = call(deconvolve, jax.ShapeDtypeStruct((96, width), BF16), 2 ** 22)(
        dgrad, grad_low, grad_high, taps, attn, live, lse, tap_grad
    )
    pack_pair = lax.ppermute(pack, "yh", swap)
    packs = lax.all_gather(pack, "z", axis=0)
    result = jax.ShapeDtypeStruct((3 * head + 16, width), F32)
    mine, other = call(backward, (result, result), 2 ** 29)(
        everyone, packs, own, pair, pack, pack_pair, key_bias, pair_bias
    )
    got = lax.ppermute(other, "yh", swap)
    d_query, d_key, d_value, tap_total = call(
        functools.partial(finish, norm), (block, block, block, jax.ShapeDtypeStruct((KSIZE, head), F32)), 2 ** 20
    )(mine, got)

    chunk = head * model // 128 // devices
    mine = lax.all_to_all(mix_parts.reshape(devices, chunk, 128), ctx, 0, 0, tiled=True)
    total = call(mix_sum, jax.ShapeDtypeStruct((chunk, 128), BF16), 2 ** 20)(mine)
    spread = jnp.broadcast_to(total[None], (devices, chunk, 128))
    pieces = lax.all_to_all(spread, ctx, 0, 0, tiled=True).reshape(model // 128, head, 128)
    mix_grad = call(functools.partial(mix_place, norm), jax.ShapeDtypeStruct((head, model), F32), 2 ** 20)(pieces)

    channel = lax.all_to_all(swish.reshape(lanes, rows8, head), "tp", 0, 0, tiled=True)
    channel = channel.transpose(1, 0, 2).reshape(rows8, lanes * head)
    full_weight = shared[:, rows8:].reshape(lanes * head, model)
    block_out = jnp.dot(channel, full_weight, preferred_element_type=F32).astype(BF16)
    return block_out, d_query.T, d_key.T, d_value.T, mix_grad, tap_total


def solution(mesh):
    count = mesh.shape["ctx"]
    fine = Mesh(mesh.devices.reshape(2, count // 2, mesh.shape["tp"]), ("yh", "z", "tp"))
    ctx = ("yh", "z")
    every = ("yh", "z", "tp")
    return jax.shard_map(
        body,
        mesh=fine,
        in_specs=(
            P(ctx, "tp"),
            P(ctx, "tp"),
            P(ctx, "tp"),
            P(),
            P(None, "tp"),
            P("tp", None),
            P(every, None),
        ),
        out_specs=(
            P(every, None),
            P(ctx, "tp"),
            P(ctx, "tp"),
            P(ctx, "tp"),
            P("tp", None),
            P(None, "tp"),
        ),
        check_vma=False,
    )
```

time: 651 us -> 187 us (0.29)
  the two profiles are of different devices: /device:TPU:1 before, /device:TPU:32 now
where the time goes in v1:
time: 187 us; the launch traced here: 186 us
  blocking collectives  70.7 us (38%)
  starting transfers between devices  45.6 us (24%)
  waiting for transfers between devices  35.7 us (19%)
  between operations  14.9 us (8%)
  Pallas kernels  10.4 us (6%)
  local copies, waits for them, and re-layouts  3.33 us (2%)
  matrix products  3.06 us (2%)
  other arithmetic  2.52 us (1%)
    all_gather x1, blocking collectives, body(): everyone = lax.all_gather(own, 'z', axis=0)  37.7 us
    all_gather x1, blocking collectives, body(): packs = lax.all_gather(pack, 'z', axis=0)  32.9 us
    all_to_all x1, waiting for transfers between devices, body(): lax.all_to_all(mix_parts.reshape(devices, chunk, 128), ctx, 0, 0, tiled=T...  16.4 us
    all_to_all x1, starting transfers between devices, body(): lax.all_to_all(mix_parts.reshape(devices, chunk, 128), ctx, 0, 0, tiled=T...  9.08 us
    ppermute x2, waiting for transfers between devices, body(): got = lax.ppermute(other, 'yh', swap)  7.45 us
    all_to_all x1, waiting for transfers between devices, body(): lax.all_to_all(swish.reshape(lanes, rows8, head), 'tp', 0, 0, tiled=True)  6.02 us
    ppermute x1, starting transfers between devices, body(): pack_pair = lax.ppermute(pack, 'yh', swap)  5.27 us
    pallas_call x1, Pallas kernels, body(): call(backward, (result, result), 2 ** 29)  5.11 us
  transfers between devices with their start and end apart: 12, of which 7 were waited for; matrix products, arithmetic and copies ran while one was open for 4% of the time, Pallas kernels for 4%

profile of v1, /device:TPU:32, one launch (start us, length us, event | category | flops | bytes accessed | tf_op | source)
XLA Modules:
  0.0 186.1 jit_solution(11040329030198536812)
XLA Ops:
  7.2 1.7 pad_maximum_fusion
  8.9 0.8 pad_maximum_fusion.1.own_ref
  9.7 5.1 %collective-permute-start = (bf16[192,128]{1,0:T(8,128)(2,1)S(1)}, bf16[192,128]{1,0:T(8,128)(2,1)S(1)}, u32[]{:S(2)}, u32[]{:S(2)}) collective-permute-start(bf16[192,128]{1,0:T(8,128)(2,1)S(1)} %pad_maximum_fusion.1.own_ref), channel_id=1, source_target_pairs={{0,256},{256,0},{1,257},{257,1},{2,258},{258,2},{3,259},{259,3},{4... | collective-permute-start | bytes 147464 | tf_op jit(solution)/shard_map/ppermute | solution.py:237
  15.4 37.7 %all-gather = bf16[3072,128]{1,0:T(8,128)(2,1)S(1)} all-gather(bf16[192,128]{1,0:T(8,128)(2,1)S(1)} %pad_maximum_fusion.1.own_ref), channel_id=2, replica_groups=mesh['yh'=2,'z'=16,'tp'=16] {'z'}, dimensions={0}, use_global_device_ids=true | all-gather | bytes 835584 | tf_op jit(solution)/shard_map/all_gather | solution.py:238
  53.2 1.3 shard_map.118
  54.5 2.2 %collective-permute-start.1 = (f32[72,128]{1,0:T(8,128)S(1)}, f32[72,128]{1,0:T(8,128)S(1)}, u32[]{:S(2)}, u32[]{:S(2)}) collective-permute-start(f32[72,128]{1,0:T(8,128)S(1)} %get-tuple-element.22), channel_id=1, source_target_pairs={{0,256},{256,0},{1,257},{257,1},{2,258},{258,2},{3,259},{259,3},{4... | collective-permute-start | bytes 110600 | tf_op jit(solution)/shard_map/ppermute | solution.py:245
  56.8 0.8 copy.13
  57.6 4.3 %collective-permute-done.1.got_ref = f32[72,128]{1,0:T(8,128)S(1)} collective-permute-done((f32[72,128]{1,0:T(8,128)S(1)}, f32[72,128]{1,0:T(8,128)S(1)}, u32[]{:S(2)}, u32[]{:S(2)}) %collective-permute-start.1) | collective-permute-done | bytes 36896 | tf_op jit(solution)/shard_map/ppermute | solution.py:245
  61.9 4.6 %collective-permute-start.3 = (bf16[64,128]{1,0:T(8,128)(2,1)S(1)}, bf16[64,128]{1,0:T(8,128)(2,1)S(1)}, u32[]{:S(2)}, u32[]{:S(2)}) collective-permute-start(bf16[64,128]{1,0:T(8,128)(2,1)S(1)} %get-tuple-element.23.masked_ref), channel_id=1, source_target_pairs={{16,0},{32,16},{48,32},{64,48},{80,64},{96,80},{112,96},{128,112},... | collective-permute-start | bytes 49160 | tf_op jit(solution)/shard_map/ppermute | solution.py:248
  66.5 1.9 %collective-permute-start.2 = (bf16[64,128]{1,0:T(8,128)(2,1)S(1)}, bf16[64,128]{1,0:T(8,128)(2,1)S(1)}, u32[]{:S(2)}, u32[]{:S(2)}) collective-permute-start(bf16[64,128]{1,0:T(8,128)(2,1)S(1)} %get-tuple-element.23.masked_ref), channel_id=1, source_target_pairs={{0,16},{16,32},{32,48},{48,64},{64,80},{80,96},{96,112},{112,128},... | collective-permute-start | bytes 49160 | tf_op jit(solution)/shard_map/ppermute | solution.py:247
  68.4 1.0 slice_bitcast_fusion.grad_ref
  69.5 2.6 %collective-permute-done.2.low_ref = bf16[64,128]{1,0:T(8,128)(2,1)S(1)} collective-permute-done((bf16[64,128]{1,0:T(8,128)(2,1)S(1)}, bf16[64,128]{1,0:T(8,128)(2,1)S(1)}, u32[]{:S(2)}, u32[]{:S(2)}) %collective-permute-start.2) | collective-permute-done | bytes 16416 | tf_op jit(solution)/shard_map/ppermute | solution.py:247
  72.1 1.7 shard_map.120
  73.9 9.1 %all-to-all-start.1 = ((bf16[32,24,128]{2,1,0:T(8,128)(2,1)}), bf16[32,24,128]{2,1,0:T(8,128)(2,1)S(1)}, u32[]{:S(2)}, u32[]{:S(2)}) async-start(bf16[32,24,128]{2,1,0:T(8,128)(2,1)} %bitcast.17), calls=%async_computation.1 | async-start | bytes 393216 | tf_op jit(solution)/shard_map/all_to_all | solution.py:277
  82.9 0.7 reshape.81
  83.6 16.4 %all-to-all-done.1.parts_ref = bf16[32,24,128]{2,1,0:T(8,128)(2,1)S(1)} async-done(((bf16[32,24,128]{2,1,0:T(8,128)(2,1)}), bf16[32,24,128]{2,1,0:T(8,128)(2,1)S(1)}, u32[]{:S(2)}, u32[]{:S(2)}) %all-to-all-start.1) | async-done | bytes 196640 | tf_op jit(solution)/shard_map/all_to_all | solution.py:277
  100.0 5.0 %all-to-all-start = ((bf16[16,2,256]{2,1,0:T(2,128)(2,1)}), bf16[16,2,256]{2,1,0:T(2,128)(2,1)S(1)}, u32[]{:S(2)}, u32[]{:S(2)}) async-start(bf16[16,2,256]{2,1,0:T(2,128)(2,1)} %reshape.81), calls=%async_computation | async-start | bytes 32768 | tf_op jit(solution)/shard_map/all_to_all | solution.py:283
  105.1 6.0 %all-to-all-done = bf16[16,2,256]{2,1,0:T(2,128)(2,1)S(1)} async-done(((bf16[16,2,256]{2,1,0:T(2,128)(2,1)}), bf16[16,2,256]{2,1,0:T(2,128)(2,1)S(1)}, u32[]{:S(2)}, u32[]{:S(2)}) %all-to-all-start) | async-done | bytes 16416 | tf_op jit(solution)/shard_map/all_to_all | solution.py:283
  111.1 0.7 broadcast_in_dim.30
  111.8 4.7 %all-to-all-start.2 = ((bf16[32,24,128]{2,1,0:T(8,128)(2,1)}), bf16[32,24,128]{2,1,0:T(8,128)(2,1)S(1)}, u32[]{:S(2)}, u32[]{:S(2)}) async-start(bf16[32,24,128]{2,1,0:T(8,128)(2,1)} %broadcast_in_dim.30), calls=%async_computation.2 | async-start | bytes 393216 | tf_op jit(solution)/shard_map/all_to_all | solution.py:280
  116.5 2.3 %collective-permute-start.5 = (bf16[64,128]{1,0:T(8,128)(2,1)S(1)}, bf16[64,128]{1,0:T(8,128)(2,1)S(1)}, u32[]{:S(2)}, u32[]{:S(2)}) collective-permute-start(bf16[64,128]{1,0:T(8,128)(2,1)S(1)} %get-tuple-element.25.dgrad_ref), channel_id=1, source_target_pairs={{16,0},{32,16},{48,32},{64,48},{80,64},{96,80},{112,96},{128,112},... | collective-permute-start | bytes 49160 | tf_op jit(solution)/shard_map/ppermute | solution.py:261
  118.8 3.6 %collective-permute-start.4 = (bf16[64,128]{1,0:T(8,128)(2,1)S(1)}, bf16[64,128]{1,0:T(8,128)(2,1)S(1)}, u32[]{:S(2)}, u32[]{:S(2)}) collective-permute-start(bf16[64,128]{1,0:T(8,128)(2,1)S(1)} %get-tuple-element.25.dgrad_ref), channel_id=1, source_target_pairs={{0,16},{16,32},{32,48},{48,64},{64,80},{80,96},{96,112},{112,128},... | collective-permute-start | bytes 49160 | tf_op jit(solution)/shard_map/ppermute | solution.py:260
  122.5 2.0 %collective-permute-done.5.high_ref = bf16[64,128]{1,0:T(8,128)(2,1)S(1)} collective-permute-done((bf16[64,128]{1,0:T(8,128)(2,1)S(1)}, bf16[64,128]{1,0:T(8,128)(2,1)S(1)}, u32[]{:S(2)}, u32[]{:S(2)}) %collective-permute-start.5) | collective-permute-done | bytes 16416 | tf_op jit(solution)/shard_map/ppermute | solution.py:261
  124.5 1.2 collective-permute-done.4.low_ref
  125.7 0.7 shard_map.121.pack_own_ref
  126.4 5.3 %collective-permute-start.6 = (bf16[96,128]{1,0:T(8,128)(2,1)S(1)}, bf16[96,128]{1,0:T(8,128)(2,1)S(1)}, u32[]{:S(2)}, u32[]{:S(2)}) collective-permute-start(bf16[96,128]{1,0:T(8,128)(2,1)S(1)} %shard_map.121.pack_own_ref), channel_id=1, source_target_pairs={{0,256},{256,0},{1,257},{257,1},{2,258},{258,2},{3,259},{259,3},{4... | collective-permute-start | bytes 73736 | tf_op jit(solution)/shard_map/ppermute | solution.py:265
  131.7 32.9 %all-gather.2 = bf16[1536,128]{1,0:T(8,128)(2,1)S(1)} all-gather(bf16[96,128]{1,0:T(8,128)(2,1)S(1)} %shard_map.121.pack_own_ref), channel_id=4, replica_groups=mesh['yh'=2,'z'=16,'tp'=16] {'z'}, dimensions={0}, use_global_device_ids=true | all-gather | bytes 417792 | tf_op jit(solution)/shard_map/all_gather | solution.py:266
  164.6 5.1 %shard_map.122 = (f32[208,128]{1,0:T(8,128)S(1)}, f32[208,128]{1,0:T(8,128)S(1)}) custom-call(bf16[16,192,128]{2,1,0:T(8,128)(2,1)S(1)} %bitcast.31, bf16[16,96,128]{2,1,0:T(8,128)(2,1)S(1)} %bitcast.33, bf16[192,128]{1,0:T(8,128)(2,1)S(1)} %pad_maximum_fusion.1.own_ref, bf16[192,128]{1,0:T(8,128)(2,1)S(1)} %collective-permute-done.pair_ref, ...), custom_call_target="tpu_custom_call" | custom-call | flops 536870912 | bytes 1048576 | tf_op jit(solution)/shard_map/pallas_call | solution.py:268
  169.7 1.9 %collective-permute-start.7 = (f32[208,128]{1,0:T(8,128)S(1)}, f32[208,128]{1,0:T(8,128)S(1)}, u32[]{:S(2)}, u32[]{:S(2)}) collective-permute-start(f32[208,128]{1,0:T(8,128)S(1)} %get-tuple-element.30), channel_id=1, source_target_pairs={{0,256},{256,0},{1,257},{257,1},{2,258},{258,2},{3,259},{259,3},{4... | collective-permute-start | bytes 319496 | tf_op jit(solution)/shard_map/ppermute | solution.py:271
  171.7 3.1 %fusion.5 = bf16[8,1536]{1,0:T(8,128)(2,1)} fusion(bf16[16,72,1536]{2,1,0:T(8,128)(2,1)} %bitcast.38, bf16[16,8,64]{2,1,0:T(8,128)(2,1)S(1)} %reshape.82), kind=kOutput, calls=%fused_computation.3 | convolution fusion | flops 25178112 | bytes 3186688 | tf_op jit(solution)/shard_map/dot_general | solution.py:286
  174.7 3.1 %collective-permute-done.7.got_ref = f32[208,128]{1,0:T(8,128)S(1)} collective-permute-done((f32[208,128]{1,0:T(8,128)S(1)}, f32[208,128]{1,0:T(8,128)S(1)}, u32[]{:S(2)}, u32[]{:S(2)}) %collective-permute-start.7) | collective-permute-done | bytes 106528 | tf_op jit(solution)/shard_map/ppermute | solution.py:271
  178.5 0.8 shard_map.125
  (18 shorter events, 1.0 us)
Async XLA Ops:
  7.2 65.0 %copy-start = (bf16[64,1536]{1,0:T(8,128)(2,1)S(1)}, bf16[64,1536]{1,0:T(8,128)(2,1)}, u32[]{:S(2)}) copy-start(bf16[64,1536]{1,0:T(8,128)(2,1)} %weight_ref.1) | copy-start | bytes 589828
  7.2 61.3 %all-gather.5.cloned.1.call-start = ((), (), s32[]{:S(2)}) async-start(), calls=%async_computation.3 | async-start | bytes 3760128 | tf_op jit(solution)/shard_map/all_gather | solution.py:235
  9.7 43.6 %collective-permute-start = (bf16[192,128]{1,0:T(8,128)(2,1)S(1)}, bf16[192,128]{1,0:T(8,128)(2,1)S(1)}, u32[]{:S(2)}, u32[]{:S(2)}) collective-permute-start(bf16[192,128]{1,0:T(8,128)(2,1)S(1)} %pad_maximum_fusion.1.own_ref), channel_id=1, source_target_pairs={{0,256},{256,0},{1,257},{257,1},{2,258},{258,2},{3,259},{259,3},{4... | collective-permute-start | bytes 147464 | tf_op jit(solution)/shard_map/ppermute | solution.py:237
  54.5 7.4 %collective-permute-start.1 = (f32[72,128]{1,0:T(8,128)S(1)}, f32[72,128]{1,0:T(8,128)S(1)}, u32[]{:S(2)}, u32[]{:S(2)}) collective-permute-start(f32[72,128]{1,0:T(8,128)S(1)} %get-tuple-element.22), channel_id=1, source_target_pairs={{0,256},{256,0},{1,257},{257,1},{2,258},{258,2},{3,259},{259,3},{4... | collective-permute-start | bytes 110600 | tf_op jit(solution)/shard_map/ppermute | solution.py:245
  61.9 7.5 %collective-permute-start.3 = (bf16[64,128]{1,0:T(8,128)(2,1)S(1)}, bf16[64,128]{1,0:T(8,128)(2,1)S(1)}, u32[]{:S(2)}, u32[]{:S(2)}) collective-permute-start(bf16[64,128]{1,0:T(8,128)(2,1)S(1)} %get-tuple-element.23.masked_ref), channel_id=1, source_target_pairs={{16,0},{32,16},{48,32},{64,48},{80,64},{96,80},{112,96},{128,112},... | collective-permute-start | bytes 49160 | tf_op jit(solution)/shard_map/ppermute | solution.py:248
  66.5 5.6 %collective-permute-start.2 = (bf16[64,128]{1,0:T(8,128)(2,1)S(1)}, bf16[64,128]{1,0:T(8,128)(2,1)S(1)}, u32[]{:S(2)}, u32[]{:S(2)}) collective-permute-start(bf16[64,128]{1,0:T(8,128)(2,1)S(1)} %get-tuple-element.23.masked_ref), channel_id=1, source_target_pairs={{0,16},{16,32},{32,48},{48,64},{64,80},{80,96},{96,112},{112,128},... | collective-permute-start | bytes 49160 | tf_op jit(solution)/shard_map/ppermute | solution.py:247
  73.9 26.2 %all-to-all-start.1 = ((bf16[32,24,128]{2,1,0:T(8,128)(2,1)}), bf16[32,24,128]{2,1,0:T(8,128)(2,1)S(1)}, u32[]{:S(2)}, u32[]{:S(2)}) async-start(bf16[32,24,128]{2,1,0:T(8,128)(2,1)} %bitcast.17), calls=%async_computation.1 | async-start | bytes 393216 | tf_op jit(solution)/shard_map/all_to_all | solution.py:277
  100.0 11.1 %all-to-all-start = ((bf16[16,2,256]{2,1,0:T(2,128)(2,1)}), bf16[16,2,256]{2,1,0:T(2,128)(2,1)S(1)}, u32[]{:S(2)}, u32[]{:S(2)}) async-start(bf16[16,2,256]{2,1,0:T(2,128)(2,1)} %reshape.81), calls=%async_computation | async-start | bytes 32768 | tf_op jit(solution)/shard_map/all_to_all | solution.py:283
  111.8 66.7 %all-to-all-start.2 = ((bf16[32,24,128]{2,1,0:T(8,128)(2,1)}), bf16[32,24,128]{2,1,0:T(8,128)(2,1)S(1)}, u32[]{:S(2)}, u32[]{:S(2)}) async-start(bf16[32,24,128]{2,1,0:T(8,128)(2,1)} %broadcast_in_dim.30), calls=%async_computation.2 | async-start | bytes 393216 | tf_op jit(solution)/shard_map/all_to_all | solution.py:280
  116.5 8.0 %collective-permute-start.5 = (bf16[64,128]{1,0:T(8,128)(2,1)S(1)}, bf16[64,128]{1,0:T(8,128)(2,1)S(1)}, u32[]{:S(2)}, u32[]{:S(2)}) collective-permute-start(bf16[64,128]{1,0:T(8,128)(2,1)S(1)} %get-tuple-element.25.dgrad_ref), channel_id=1, source_target_pairs={{16,0},{32,16},{48,32},{64,48},{80,64},{96,80},{112,96},{128,112},... | collective-permute-start | bytes 49160 | tf_op jit(solution)/shard_map/ppermute | solution.py:261
  118.8 6.9 %collective-permute-start.4 = (bf16[64,128]{1,0:T(8,128)(2,1)S(1)}, bf16[64,128]{1,0:T(8,128)(2,1)S(1)}, u32[]{:S(2)}, u32[]{:S(2)}) collective-permute-start(bf16[64,128]{1,0:T(8,128)(2,1)S(1)} %get-tuple-element.25.dgrad_ref), channel_id=1, source_target_pairs={{0,16},{16,32},{32,48},{48,64},{64,80},{80,96},{96,112},{112,128},... | collective-permute-start | bytes 49160 | tf_op jit(solution)/shard_map/ppermute | solution.py:260
  126.4 38.2 %collective-permute-start.6 = (bf16[96,128]{1,0:T(8,128)(2,1)S(1)}, bf16[96,128]{1,0:T(8,128)(2,1)S(1)}, u32[]{:S(2)}, u32[]{:S(2)}) collective-permute-start(bf16[96,128]{1,0:T(8,128)(2,1)S(1)} %shard_map.121.pack_own_ref), channel_id=1, source_target_pairs={{0,256},{256,0},{1,257},{257,1},{2,258},{258,2},{3,259},{259,3},{4... | collective-permute-start | bytes 73736 | tf_op jit(solution)/shard_map/ppermute | solution.py:265
  169.7 8.1 %collective-permute-start.7 = (f32[208,128]{1,0:T(8,128)S(1)}, f32[208,128]{1,0:T(8,128)S(1)}, u32[]{:S(2)}, u32[]{:S(2)}) collective-permute-start(f32[208,128]{1,0:T(8,128)S(1)} %get-tuple-element.30), channel_id=1, source_target_pairs={{0,256},{256,0},{1,257},{257,1},{2,258},{258,2},{3,259},{259,3},{4... | collective-permute-start | bytes 319496 | tf_op jit(solution)/shard_map/ppermute | solution.py:271
Sparse Core Ops, SparseCore 0:
  10.7 48.2 all-gather.4

commit v2 on v1

--- a/solution.py
+++ b/solution.py
@@ -42,24 +42,47 @@
     return high, mid, rest - mid
 
 
-def call(kernel, out_shapes, flops, scratch=()):
+def call(kernel, out_shapes, flops, scratch=(), scalars=0):
+    specs = {}
+    if scalars:
+        count = kernel.__code__.co_argcount - len(scratch) - len(jax.tree.leaves(out_shapes))
+        specs["in_specs"] = [pl.BlockSpec(memory_space=pltpu.SMEM)] + [pl.BlockSpec(memory_space=pltpu.VMEM)] * (count - 1)
     return pl.pallas_call(
         kernel,
         out_shape=out_shapes,
+        **specs,
         scratch_shapes=list(scratch),
         compiler_params=pltpu.CompilerParams(vmem_limit_bytes=VMEM_BYTES),
         cost_estimate=pl.CostEstimate(flops=flops, bytes_accessed=2 ** 20, transcendentals=0),
     )
 
 
-def attend(all_ref, own_ref, pair_ref, bias_ref, mine_ref, other_ref, score_ref):
+def side_of(low, high):
+    lane = lax.broadcasted_iota(jnp.int32, low.shape, 1)
+    return jnp.where(lane < low.shape[1] // 2, high, low)
+
+
+def attend(place_ref, all_ref, own_ref, pair_ref, low_ref, high_ref, bias_ref, mine_ref, other_ref, score_ref):
     blocks = all_ref.shape[0]
     head = 64
     width = 128
+    lanes = 3 * width
     scale = head ** -0.5
-    query = jnp.concatenate([own_ref[0:head], pair_ref[0:head]], axis=1).astype(F32) * scale
-    query = jnp.concatenate([query, rows_of(16, 2 * width, [(6, 1.0)])], axis=0).astype(BF16)
-    peak = jnp.full((1, 2 * width), LOW, F32)
+    spot = place_ref[0]
+    first = spot == 0
+    last = spot == blocks - 1
+    low_here = all_ref[lax.rem(spot + blocks - 1, blocks), 0:head].astype(F32)
+    high_here = all_ref[lax.rem(spot + 1, blocks), 0:head].astype(F32)
+    low_there = low_ref[...].astype(F32)
+    high_there = high_ref[...].astype(F32)
+    side_own = side_of(jnp.where(first, low_there, low_here), jnp.where(last, high_there, high_here))
+    side_pair = side_of(jnp.where(first, low_here, low_there), jnp.where(last, high_here, high_there))
+    lane = lax.broadcasted_iota(jnp.int32, (head, width), 1)
+    middle = (lane >= 32) & (lane < 96)
+    edges = jnp.where(middle, pltpu.roll(side_pair, width // 2, 1), side_own)
+    query = jnp.concatenate([own_ref[0:head].astype(F32), pair_ref[0:head].astype(F32), edges], axis=1) * scale
+    query = jnp.concatenate([query, rows_of(16, lanes, [(6, 1.0)])], axis=0).astype(BF16)
+    peak = jnp.full((1, lanes), LOW, F32)
     for b in range(blocks):
         key = jnp.concatenate(
             [all_ref[b, head : 2 * head], rows_of(16, width, [(6, bias_ref[b : b + 1])]).astype(BF16)], axis=0
@@ -67,82 +90,77 @@
         score = dot00(key, query)
         score_ref[b] = score
         peak = jnp.maximum(peak, jnp.max(score, axis=0, keepdims=True))
-    total = jnp.zeros((1, 2 * width), F32)
-    out = jnp.zeros((head, 2 * width), F32)
+    total = jnp.zeros((1, lanes), F32)
+    out = jnp.zeros((head, lanes), F32)
     for b in range(blocks):
         weight = jnp.exp(score_ref[b] - peak)
         total = total + jnp.sum(weight, axis=0, keepdims=True)
         out = out + dot10(all_ref[b, 2 * head : 3 * head], weight.astype(BF16))
     out = out / total
     lse = peak + jnp.log(total)
-    both = jnp.concatenate([out, jnp.broadcast_to(lse, (8, 2 * width))], axis=0)
-    mine_ref[...] = both[:, :width]
-    other_ref[...] = both[:, width:]
-
-
-def combine(mine_ref, got_ref, live_ref, attn_ref, masked_ref, lse_ref):
+    both = jnp.concatenate([out, jnp.broadcast_to(lse, (8, lanes))], axis=0)
+    edges = both[:, 2 * width :]
+    mine_ref[:, 0:width] = both[:, 0:width]
+    mine_ref[:, width:] = edges
+    other_ref[:, 0:width] = both[:, width : 2 * width]
+    other_ref[:, width:] = pltpu.roll(edges, width // 2, 1)
+
+
+def shifted(ring, offset):
+    if offset == 0:
+        return ring
+    return pltpu.roll(ring, (-offset) % ring.shape[1], 1)
+
+
+def middle_part(place_ref, mine_ref, got_ref, taps_ref, weight_ref, grad_ref, low_ref, high_ref, partial_ref, mix_ref, pack_ref):
+    width = 128
+    ring = 2 * width
+    start = place_ref[1]
+    valid = place_ref[2]
+    frames = place_ref[3]
     mine = mine_ref[64:65]
     got = got_ref[64:65]
     top = jnp.maximum(mine, got)
     lse = top + jnp.log(jnp.exp(mine - top) + jnp.exp(got - top))
     attn = mine_ref[0:64] * jnp.exp(mine - lse) + got_ref[0:64] * jnp.exp(got - lse)
-    attn_ref[...] = attn.astype(BF16)
-    masked_ref[...] = jnp.where(live_ref[...] > 0.0, attn, 0.0).astype(BF16)
-    lse_ref[...] = jnp.broadcast_to(lse, lse_ref.shape)
-
-
-def ring_of(own, low, high):
-    lane = lax.broadcasted_iota(jnp.int32, own.shape, 1)
-    side = jnp.where(lane < own.shape[1] // 2, high.astype(F32), low.astype(F32))
-    return jnp.concatenate([own.astype(F32), side], axis=1)
-
-
-def shifted(ring, offset):
-    size = ring.shape[1]
-    if offset % size == 0:
-        return ring[:, : size // 2]
-    return pltpu.roll(ring, (-offset) % size, 1)[:, : size // 2]
-
-
-def convolve(masked_ref, low_ref, high_ref, taps_ref, weight_ref, grad_ref, swish_ref, mix_ref, dgrad_ref, tap_grad_ref):
-    ring = ring_of(masked_ref[...], low_ref[...], high_ref[...])
+    attn = attn.astype(BF16).astype(F32)
+    lane = lax.broadcasted_iota(jnp.int32, (1, ring), 1)
+    frame = start + jnp.where(lane < ring - width // 2, lane, lane - ring)
+    inside = (frame >= 0) & (frame < frames) & ((lane < width + 32) | (lane >= ring - 32))
+    live = inside & (frame < valid)
+    masked = jnp.where(live, attn, 0.0)
     taps = taps_ref[...]
-    depth = jnp.zeros((64, 128), F32)
+    depth = jnp.zeros((64, ring), F32)
     for t in range(KSIZE):
-        depth = depth + taps[:, t : t + 1] * shifted(ring, t - RIM)
+        depth = depth + taps[:, t : t + 1] * shifted(masked, t - RIM)
     gate = jax.nn.sigmoid(depth)
-    swish = (depth * gate).astype(BF16)
-    swish_ref[...] = (depth * gate).T.astype(BF16)
+    swish = (depth[:, :width] * gate[:, :width]).astype(BF16)
     grad = grad_ref[...]
     mix = dot10(swish, grad)
     for piece in range(mix_ref.shape[0]):
         mix_ref[piece] = mix[:, piece * 128 : (piece + 1) * 128].astype(BF16)
-    back = dot11(weight_ref[...], grad)
-    dgrad = (back * gate * (1.0 + depth * (1.0 - gate))).astype(BF16)
-    dgrad_ref[...] = dgrad
-    wide = dgrad.astype(F32)
-    lane = lax.broadcasted_iota(jnp.int32, (64, 128), 1)
-    sums = jnp.zeros((64, 128), F32)
+    weight = weight_ref[...]
+    partial_ref[...] = dot00(swish, weight)
+    gap = jnp.zeros((width - 2 * RIM, grad.shape[1]), BF16)
+    side = jnp.concatenate([high_ref[...], gap, low_ref[...]], axis=0)
+    back = jnp.concatenate([dot11(weight, grad), dot11(weight, side)], axis=1)
+    dgrad = back * gate * (1.0 + depth * (1.0 - gate))
+    dgrad = jnp.where(inside, dgrad, 0.0).astype(BF16).astype(F32)
+    row = lax.broadcasted_iota(jnp.int32, (64, width), 1)
+    sums = jnp.zeros((64, width), F32)
+    total = jnp.zeros((64, width), F32)
     for t in range(KSIZE):
-        column = jnp.sum(shifted(ring, t - RIM) * wide, axis=1, keepdims=True)
-        sums = jnp.where(lane == t, column, sums)
+        column = jnp.sum(shifted(masked, t - RIM)[:, :width] * dgrad[:, :width], axis=1, keepdims=True)
+        sums = jnp.where(row == t, column, sums)
+        total = total + taps[:, t : t + 1] * shifted(dgrad, RIM - t)[:, :width]
     turned = sums.T
-    tap_grad_ref[...] = jnp.concatenate([turned[0:16, 0:64], turned[16:32, 0:64]], axis=1).astype(BF16)
-
-
-def deconvolve(dgrad_ref, low_ref, high_ref, taps_ref, attn_ref, live_ref, lse_ref, tap_grad_ref, pack_ref):
-    ring = ring_of(dgrad_ref[...], low_ref[...], high_ref[...])
-    taps = taps_ref[...]
-    total = jnp.zeros((64, 128), F32)
-    for t in range(KSIZE):
-        total = total + taps[:, t : t + 1] * shifted(ring, RIM - t)
-    grad = jnp.where(live_ref[...] > 0.0, total, 0.0).astype(BF16)
-    delta = jnp.sum(grad.astype(F32) * attn_ref[...].astype(F32), axis=0, keepdims=True)
-    lse = lse_ref[0:1]
-    a, b, c = split3(-lse)
+    tap_grad = jnp.concatenate([turned[0:16, 0:64], turned[16:32, 0:64]], axis=1).astype(BF16)
+    grad_out = jnp.where(live[:, :width], total, 0.0).astype(BF16)
+    delta = jnp.sum(grad_out.astype(F32) * attn[:, :width], axis=0, keepdims=True)
+    a, b, c = split3(-lse[:, :width])
     d, e, f = split3(-delta)
-    stats = rows_of(16, 128, [(0, a), (1, b), (2, c), (3, d), (4, e), (5, f), (6, 1.0)])
-    pack_ref[...] = jnp.concatenate([grad, stats.astype(BF16), tap_grad_ref[...]], axis=0)
+    stats = rows_of(16, width, [(0, a), (1, b), (2, c), (3, d), (4, e), (5, f), (6, 1.0)])
+    pack_ref[...] = jnp.concatenate([grad_out, stats.astype(BF16), tap_grad], axis=0)
 
 
 def backward(all_ref, packs_ref, own_ref, pair_ref, pack_own_ref, pack_pair_ref, bias_ref, pair_bias_ref, mine_ref, other_ref):
@@ -226,44 +244,52 @@
     own_ids = (half * depth + spot) * width + frame
     pair_ids = ((1 - half) * depth + spot) * width + frame
     pair_bias = jnp.where(jnp.concatenate([own_ids, pair_ids]) < valid, 0.0, LOW).astype(F32)[None, :]
-    live = (own_ids < valid).astype(F32)[None, :]
+    place = jnp.stack([spot, (half * depth + spot) * width, valid, jnp.int32(width * devices)]).astype(jnp.int32)
     swap = [(0, 1), (1, 0)]
-    up = [(i, i + 1) for i in range(devices - 1)]
-    down = [(i + 1, i) for i in range(devices - 1)]
     taps = depth_kernel.T
-
-    shared = lax.all_gather(jnp.concatenate([out_grad, mix_weight], axis=0), "tp", axis=0)
-    own = jnp.concatenate([query_rows.T, key_rows.T, value_rows.T], axis=0)
+    over_up = [(h * depth + z, (1 - h) * depth + (z + 1) % depth) for h in range(2) for z in range(depth)]
+    over_down = [(h * depth + z, (1 - h) * depth + (z - 1) % depth) for h in range(2) for z in range(depth)]
+    rim_pairs = []
+    sides = RIM // rows8
+    for i in range(devices - 1):
+        for k in range(sides):
+            rim_pairs.append((i * lanes + lanes - sides + k, (i + 1) * lanes + k))
+            rim_pairs.append(((i + 1) * lanes + k, i * lanes + lanes - sides + k))
+
+    rim_rows = lax.ppermute(out_grad, ("yh", "z", "tp"), rim_pairs)
+    shared = lax.all_gather(jnp.concatenate([out_grad, rim_rows, mix_weight], axis=0), "tp", axis=0)
+    query_turned = query_rows.T
+    low = lax.ppermute(query_turned, ctx, over_up)
+    high = lax.ppermute(query_turned, ctx, over_down)
+    own = jnp.concatenate([query_turned, key_rows.T, value_rows.T], axis=0)
     pair = lax.ppermute(own, "yh", swap)
     everyone = lax.all_gather(own, "z", axis=0)
 
-    part = jax.ShapeDtypeStruct((head + 8, width), F32)
+    part = jax.ShapeDtypeStruct((head + 8, 2 * width), F32)
     block = jax.ShapeDtypeStruct((head, width), BF16)
     mine, other = call(
-        attend, (part, part), 2 ** 28, [pltpu.VMEM((depth, width, 2 * width), F32)]
-    )(everyone, own, pair, key_bias)
+        attend, (part, part), 2 ** 28, [pltpu.VMEM((depth, width, 3 * width), F32)], scalars=1
+    )(place, everyone, own, pair, low, high, key_bias)
     got = lax.ppermute(other, "yh", swap)
-    attn, masked, lse = call(combine, (block, block, jax.ShapeDtypeStruct((8, width), F32)), 2 ** 20)(mine, got, live)
-    low = lax.ppermute(masked, ctx, up)
-    high = lax.ppermute(masked, ctx, down)
     grad_block = shared[:, :rows8].reshape(lanes * rows8, model)
-    swish, mix_parts, dgrad, tap_grad = call(
-        convolve,
+    grad_low = shared[:sides, rows8 : 2 * rows8].reshape(RIM, model)
+    grad_high = shared[lanes - sides :, rows8 : 2 * rows8].reshape(RIM, model)
+    partial, mix_parts, pack = call(
+        middle_part,
         (
-            jax.ShapeDtypeStruct((width, head), BF16),
+            jax.ShapeDtypeStruct((width, model), F32),
             jax.ShapeDtypeStruct((model // 128, head, 128), BF16),
-            block,
-            jax.ShapeDtypeStruct((16, 128), BF16),
+            jax.ShapeDtypeStruct((96, width), BF16),
         ),
-        2 ** 26,
-    )(masked, low, high, taps, mix_weight, grad_block)
-    grad_low = lax.ppermute(dgrad, ctx, up)
-    grad_high = lax.ppermute(dgrad, ctx, down)
-    pack = call(deconvolve, jax.ShapeDtypeStruct((96, width), BF16), 2 ** 22)(
-        dgrad, grad_low, grad_high, taps, attn, live, lse, tap_grad
-    )
+        2 ** 27,
+        scalars=1,
+    )(place, mine, got, taps, mix_weight, grad_block, grad_low, grad_high)
+    block_out = lax.psum_scatter(partial, "tp", scatter_dimension=0, tiled=True).astype(BF16)
+    chunk = head * model // 128 // devices
+    mix_mine = lax.all_to_all(mix_parts.reshape(devices, chunk, 128), ctx, 0, 0, tiled=True)
     pack_pair = lax.ppermute(pack, "yh", swap)
     packs = lax.all_gather(pack, "z", axis=0)
+    mix_mine, packs = lax.optimization_barrier((mix_mine, packs))
     result = jax.ShapeDtypeStruct((3 * head + 16, width), F32)
     mine, other = call(backward, (result, result), 2 ** 29)(
         everyone, packs, own, pair, pack, pack_pair, key_bias, pair_bias
@@ -273,17 +299,10 @@
         functools.partial(finish, norm), (block, block, block, jax.ShapeDtypeStruct((KSIZE, head), F32)), 2 ** 20
     )(mine, got)
 
-    chunk = head * model // 128 // devices
-    mine = lax.all_to_all(mix_parts.reshape(devices, chunk, 128), ctx, 0, 0, tiled=True)
-    total = call(mix_sum, jax.ShapeDtypeStruct((chunk, 128), BF16), 2 ** 20)(mine)
-    spread = jnp.broadcast_to(total[None], (devices, chunk, 128))
+    mix_total = call(mix_sum, jax.ShapeDtypeStruct((chunk, 128), BF16), 2 ** 20)(mix_mine)
+    spread = jnp.broadcast_to(mix_total[None], (devices, chunk, 128))
     pieces = lax.all_to_all(spread, ctx, 0, 0, tiled=True).reshape(model // 128, head, 128)
     mix_grad = call(functools.partial(mix_place, norm), jax.ShapeDtypeStruct((head, model), F32), 2 ** 20)(pieces)
-
-    channel = lax.all_to_all(swish.reshape(lanes, rows8, head), "tp", 0, 0, tiled=True)
-    channel = channel.transpose(1, 0, 2).reshape(rows8, lanes * head)
-    full_weight = shared[:, rows8:].reshape(lanes * head, model)
-    block_out = jnp.dot(channel, full_weight, preferred_element_type=F32).astype(BF16)
     return block_out, d_query.T, d_key.T, d_value.T, mix_grad, tap_total
 
 

time: 187 us -> 176 us (0.941)
  the two profiles are of different devices: /device:TPU:32 before, /device:TPU:30 now
where the time goes in v2:
time: 176 us; the launch traced here: 175 us
  blocking collectives  70 us (40%)
  starting transfers between devices  50.9 us (29%)
  waiting for transfers between devices  18.8 us (11%)
  between operations  14.8 us (8%)
  Pallas kernels  12.3 us (7%)
  local copies, waits for them, and re-layouts  4.28 us (2%)
  other arithmetic  3.98 us (2%)
    all_gather x1, blocking collectives, body(): everyone = lax.all_gather(own, 'z', axis=0)  36.6 us
    all_gather x1, blocking collectives, body(): packs = lax.all_gather(pack, 'z', axis=0)  33.3 us
    all_to_all x1, starting transfers between devices, body(): lax.all_to_all(spread, ctx, 0, 0, tiled=True)  13.4 us
    ppermute x1, starting transfers between devices, body(): high = lax.ppermute(query_turned, ctx, over_down)  13.3 us
    all_to_all x1, starting transfers between devices, body(): lax.all_to_all(mix_parts.reshape(devices, chunk, 128), ctx, 0, 0, tiled=T...  8.85 us
    ppermute x2, waiting for transfers between devices, body(): got = lax.ppermute(other, 'yh', swap)  8.57 us
    ppermute x2, starting transfers between devices, body(): got = lax.ppermute(other, 'yh', swap)  5.38 us
    ppermute x1, waiting for transfers between devices, body(): pack_pair = lax.ppermute(pack, 'yh', swap)  5.11 us
  transfers between devices with their start and end apart: 11, of which 4 were waited for; matrix products, arithmetic and copies ran while one was open for 2% of the time, Pallas kernels for 5%

profile of v2, /device:TPU:30, one launch (start us, length us, event | category | flops | bytes accessed | tf_op | source)
XLA Modules:
  0.0 175.0 jit_solution(12459674018442554685)
XLA Ops:
  7.2 0.0 all-gather.5.cloned.1.call-start
  7.2 3.9 %collective-permute-start.4 = (bf16[8,1536]{1,0:T(8,128)(2,1)}, bf16[8,1536]{1,0:T(8,128)(2,1)S(1)}, u32[]{:S(2)}, u32[]{:S(2)}) collective-permute-start(bf16[8,1536]{1,0:T(8,128)(2,1)} %param.13), channel_id=1, source_target_pairs={{14,16},{16,14},{15,17},{17,15},{30,32},{32,30},{31,33},{33,31},{4... | collective-permute-start | bytes 73736 | tf_op jit(solution)/shard_map/ppermute | solution.py:259
  11.1 5.0 %collective-permute-done.4 = bf16[8,1536]{1,0:T(8,128)(2,1)S(1)} collective-permute-done((bf16[8,1536]{1,0:T(8,128)(2,1)}, bf16[8,1536]{1,0:T(8,128)(2,1)S(1)}, u32[]{:S(2)}, u32[]{:S(2)}) %collective-permute-start.4) | collective-permute-done | bytes 24608 | tf_op jit(solution)/shard_map/ppermute | solution.py:259
  16.1 1.6 pad_maximum_fusion
  17.8 0.0 reduce-scatter.2.cloned.1.call-start
  17.9 13.3 %collective-permute-start.2 = (bf16[64,128]{1,0:T(8,128)(2,1)}, bf16[64,128]{1,0:T(8,128)(2,1)S(1)}, u32[]{:S(2)}, u32[]{:S(2)}) collective-permute-start(bf16[64,128]{1,0:T(8,128)(2,1)} %bitcast.36), channel_id=1, source_target_pairs={{0,496},{16,256},{32,272},{48,288},{64,304},{80,320},{96,336},{112... | collective-permute-start | bytes 49160 | tf_op jit(solution)/shard_map/ppermute | solution.py:263
  31.2 1.9 %collective-permute-start.1 = (bf16[64,128]{1,0:T(8,128)(2,1)}, bf16[64,128]{1,0:T(8,128)(2,1)S(1)}, u32[]{:S(2)}, u32[]{:S(2)}) collective-permute-start(bf16[64,128]{1,0:T(8,128)(2,1)} %bitcast.37), channel_id=1, source_target_pairs={{0,272},{16,288},{32,304},{48,320},{64,336},{80,352},{96,368},{112... | collective-permute-start | bytes 49160 | tf_op jit(solution)/shard_map/ppermute | solution.py:262
  33.1 0.8 pad_maximum_fusion.1.own_ref
  33.9 1.9 %collective-permute-start = (bf16[192,128]{1,0:T(8,128)(2,1)S(1)}, bf16[192,128]{1,0:T(8,128)(2,1)S(1)}, u32[]{:S(2)}, u32[]{:S(2)}) collective-permute-start(bf16[192,128]{1,0:T(8,128)(2,1)S(1)} %pad_maximum_fusion.1.own_ref), channel_id=1, source_target_pairs={{0,256},{256,0},{1,257},{257,1},{2,258},{258,2},{3,259},{259,3},{4... | collective-permute-start | bytes 147464 | tf_op jit(solution)/shard_map/ppermute | solution.py:265
  36.4 0.1 fusion.bias_ref
  36.5 36.6 %all-gather = bf16[3072,128]{1,0:T(8,128)(2,1)S(1)} all-gather(bf16[192,128]{1,0:T(8,128)(2,1)S(1)} %pad_maximum_fusion.1.own_ref), channel_id=2, replica_groups=mesh['yh'=2,'z'=16,'tp'=16] {'z'}, dimensions={0}, use_global_device_ids=true | all-gather | bytes 835584 | tf_op jit(solution)/shard_map/all_gather | solution.py:266
  73.2 0.1 pad_add_fusion.place_ref
  73.2 0.8 copy.13
  74.1 2.1 %shard_map.118 = (f32[72,256]{1,0:T(8,128)S(1)}, f32[72,256]{1,0:T(8,128)S(1)}) custom-call(s32[4]{0:T(128)S(1)} %pad_add_fusion.place_ref, bf16[16,192,128]{2,1,0:T(8,128)(2,1)S(1)} %bitcast.27, bf16[192,128]{1,0:T(8,128)(2,1)S(1)} %pad_maximum_fusion.1.own_ref, bf16[192,128]{1,0:T(8,128)(2,1)S(1)} %collective-permute-done.pair_ref, ...), custom_call_target="tpu_custom_call" | custom-call | flops 268435456 | bytes 1048576 | tf_op jit(solution)/shard_map/pallas_call | solution.py:270
  76.2 3.2 %collective-permute-start.3 = (f32[72,256]{1,0:T(8,128)S(1)}, f32[72,256]{1,0:T(8,128)S(1)}, u32[]{:S(2)}, u32[]{:S(2)}) collective-permute-start(f32[72,256]{1,0:T(8,128)S(1)} %get-tuple-element.20), channel_id=1, source_target_pairs={{0,256},{256,0},{1,257},{257,1},{2,258},{258,2},{3,259},{259,3},{4... | collective-permute-start | bytes 221192 | tf_op jit(solution)/shard_map/ppermute | solution.py:273
  79.4 1.0 slice_bitcast_fusion.grad_ref
  80.4 0.8 slice_bitcast_fusion.1
  81.3 2.7 %collective-permute-done.3.got_ref = f32[72,256]{1,0:T(8,128)S(1)} collective-permute-done((f32[72,256]{1,0:T(8,128)S(1)}, f32[72,256]{1,0:T(8,128)S(1)}, u32[]{:S(2)}, u32[]{:S(2)}) %collective-permute-start.3) | collective-permute-done | bytes 73760 | tf_op jit(solution)/shard_map/ppermute | solution.py:273
  83.9 0.9 copy-done
  84.9 3.5 %shard_map.119 = (f32[128,1536]{1,0:T(8,128)}, bf16[12,64,128]{2,1,0:T(8,128)(2,1)}, bf16[96,128]{1,0:T(8,128)(2,1)S(1)}) custom-call(s32[4]{0:T(128)S(1)} %pad_add_fusion.place_ref, f32[72,256]{1,0:T(8,128)S(1)} %get-tuple-element.19.mine_ref, f32[72,256]{1,0:T(8,128)S(1)} %collective-permute-done.3.got_ref, f32[64,32]{1,0:T(8,128)S(1)} %bitcast.31, ...), custom_call_target="tpu_custom_call" | custom-call | flops 134217728 | bytes 1048576 | tf_op jit(solution)/shard_map/pallas_call | solution.py:277
  88.4 8.9 %all-to-all-start = ((bf16[32,24,128]{2,1,0:T(8,128)(2,1)}), bf16[32,24,128]{2,1,0:T(8,128)(2,1)S(1)}, u32[]{:S(2)}, u32[]{:S(2)}) async-start(bf16[32,24,128]{2,1,0:T(8,128)(2,1)} %bitcast.12), calls=%async_computation.1 | async-start | bytes 393216 | tf_op jit(solution)/shard_map/all_to_all | solution.py:289
  97.3 33.3 %all-gather.2 = bf16[1536,128]{1,0:T(8,128)(2,1)S(1)} all-gather(bf16[96,128]{1,0:T(8,128)(2,1)S(1)} %get-tuple-element.23.pack_own_ref), channel_id=4, replica_groups=mesh['yh'=2,'z'=16,'tp'=16] {'z'}, dimensions={0}, use_global_device_ids=true | all-gather | bytes 417792 | tf_op jit(solution)/shard_map/all_gather | solution.py:291
  130.7 0.7 broadcast_in_dim.29
  131.4 13.4 %all-to-all-start.1 = ((bf16[32,24,128]{2,1,0:T(8,128)(2,1)}), bf16[32,24,128]{2,1,0:T(8,128)(2,1)S(1)}, u32[]{:S(2)}, u32[]{:S(2)}) async-start(bf16[32,24,128]{2,1,0:T(8,128)(2,1)} %broadcast_in_dim.29), calls=%async_computation.2 | async-start | bytes 393216 | tf_op jit(solution)/shard_map/all_to_all | solution.py:304
  144.8 2.1 %collective-permute-start.5 = (bf16[96,128]{1,0:T(8,128)(2,1)S(1)}, bf16[96,128]{1,0:T(8,128)(2,1)S(1)}, u32[]{:S(2)}, u32[]{:S(2)}) collective-permute-start(bf16[96,128]{1,0:T(8,128)(2,1)S(1)} %get-tuple-element.23.pack_own_ref), channel_id=1, source_target_pairs={{0,256},{256,0},{1,257},{257,1},{2,258},{258,2},{3,259},{259,3},{4... | collective-permute-start | bytes 73736 | tf_op jit(solution)/shard_map/ppermute | solution.py:290
  147.0 5.1 %collective-permute-done.5.pack_pair_ref = bf16[96,128]{1,0:T(8,128)(2,1)S(1)} collective-permute-done((bf16[96,128]{1,0:T(8,128)(2,1)S(1)}, bf16[96,128]{1,0:T(8,128)(2,1)S(1)}, u32[]{:S(2)}, u32[]{:S(2)}) %collective-permute-start.5) | collective-permute-done | bytes 24608 | tf_op jit(solution)/shard_map/ppermute | solution.py:290
  152.1 5.1 %shard_map.120 = (f32[208,128]{1,0:T(8,128)S(1)}, f32[208,128]{1,0:T(8,128)S(1)}) custom-call(bf16[16,192,128]{2,1,0:T(8,128)(2,1)S(1)} %bitcast.28, bf16[16,96,128]{2,1,0:T(8,128)(2,1)S(1)} %bitcast.30, bf16[192,128]{1,0:T(8,128)(2,1)S(1)} %pad_maximum_fusion.1.own_ref, bf16[192,128]{1,0:T(8,128)(2,1)S(1)} %collective-permute-done.pair_ref, ...), custom_call_target="tpu_custom_call" | custom-call | flops 536870912 | bytes 1048576 | tf_op jit(solution)/shard_map/pallas_call | solution.py:294
  157.2 2.2 %collective-permute-start.6 = (f32[208,128]{1,0:T(8,128)S(1)}, f32[208,128]{1,0:T(8,128)S(1)}, u32[]{:S(2)}, u32[]{:S(2)}) collective-permute-start(f32[208,128]{1,0:T(8,128)S(1)} %get-tuple-element.26), channel_id=1, source_target_pairs={{0,256},{256,0},{1,257},{257,1},{2,258},{258,2},{3,259},{259,3},{4... | collective-permute-start | bytes 319496 | tf_op jit(solution)/shard_map/ppermute | solution.py:297
  159.4 5.9 %collective-permute-done.6.got_ref = f32[208,128]{1,0:T(8,128)S(1)} collective-permute-done((f32[208,128]{1,0:T(8,128)S(1)}, f32[208,128]{1,0:T(8,128)S(1)}, u32[]{:S(2)}, u32[]{:S(2)}) %collective-permute-start.6) | collective-permute-done | bytes 106528 | tf_op jit(solution)/shard_map/ppermute | solution.py:297
  165.3 0.7 shard_map.121
  166.0 0.8 shard_map.123
  166.7 1.4 convert_element_type.3
  (14 shorter events, 0.1 us)
Async XLA Ops:
  7.2 72.2 %all-gather.5.cloned.1.call-start = ((), (), s32[]{:S(2)}) async-start(), calls=%async_computation.4 | async-start | bytes 4177920 | tf_op jit(solution)/shard_map/all_gather | solution.py:260
  7.2 8.9 %collective-permute-start.4 = (bf16[8,1536]{1,0:T(8,128)(2,1)}, bf16[8,1536]{1,0:T(8,128)(2,1)S(1)}, u32[]{:S(2)}, u32[]{:S(2)}) collective-permute-start(bf16[8,1536]{1,0:T(8,128)(2,1)} %param.13), channel_id=1, source_target_pairs={{14,16},{16,14},{15,17},{17,15},{30,32},{32,30},{31,33},{33,31},{4... | collective-permute-start | bytes 73736 | tf_op jit(solution)/shard_map/ppermute | solution.py:259
  17.8 148.9 %reduce-scatter.2.cloned.1.call-start = ((), (), s32[]{:S(2)}) async-start(), calls=%async_computation.3 | async-start | bytes 835584 | tf_op jit(solution)/shard_map/reduce_scatter | solution.py:287
  17.9 56.2 %collective-permute-start.2 = (bf16[64,128]{1,0:T(8,128)(2,1)}, bf16[64,128]{1,0:T(8,128)(2,1)S(1)}, u32[]{:S(2)}, u32[]{:S(2)}) collective-permute-start(bf16[64,128]{1,0:T(8,128)(2,1)} %bitcast.36), channel_id=1, source_target_pairs={{0,496},{16,256},{32,272},{48,288},{64,304},{80,320},{96,336},{112... | collective-permute-start | bytes 49160 | tf_op jit(solution)/shard_map/ppermute | solution.py:263
  31.2 42.9 %collective-permute-start.1 = (bf16[64,128]{1,0:T(8,128)(2,1)}, bf16[64,128]{1,0:T(8,128)(2,1)S(1)}, u32[]{:S(2)}, u32[]{:S(2)}) collective-permute-start(bf16[64,128]{1,0:T(8,128)(2,1)} %bitcast.37), channel_id=1, source_target_pairs={{0,272},{16,288},{32,304},{48,320},{64,336},{80,352},{96,368},{112... | collective-permute-start | bytes 49160 | tf_op jit(solution)/shard_map/ppermute | solution.py:262
  33.9 40.2 %collective-permute-start = (bf16[192,128]{1,0:T(8,128)(2,1)S(1)}, bf16[192,128]{1,0:T(8,128)(2,1)S(1)}, u32[]{:S(2)}, u32[]{:S(2)}) collective-permute-start(bf16[192,128]{1,0:T(8,128)(2,1)S(1)} %pad_maximum_fusion.1.own_ref), channel_id=1, source_target_pairs={{0,256},{256,0},{1,257},{257,1},{2,258},{258,2},{3,259},{259,3},{4... | collective-permute-start | bytes 147464 | tf_op jit(solution)/shard_map/ppermute | solution.py:265
  76.2 7.7 %collective-permute-start.3 = (f32[72,256]{1,0:T(8,128)S(1)}, f32[72,256]{1,0:T(8,128)S(1)}, u32[]{:S(2)}, u32[]{:S(2)}) collective-permute-start(f32[72,256]{1,0:T(8,128)S(1)} %get-tuple-element.20), channel_id=1, source_target_pairs={{0,256},{256,0},{1,257},{257,1},{2,258},{258,2},{3,259},{259,3},{4... | collective-permute-start | bytes 221192 | tf_op jit(solution)/shard_map/ppermute | solution.py:273
  83.9 0.9 copy-start
  88.4 42.2 %all-to-all-start = ((bf16[32,24,128]{2,1,0:T(8,128)(2,1)}), bf16[32,24,128]{2,1,0:T(8,128)(2,1)S(1)}, u32[]{:S(2)}, u32[]{:S(2)}) async-start(bf16[32,24,128]{2,1,0:T(8,128)(2,1)} %bitcast.12), calls=%async_computation.1 | async-start | bytes 393216 | tf_op jit(solution)/shard_map/all_to_all | solution.py:289
  131.4 34.6 %all-to-all-start.1 = ((bf16[32,24,128]{2,1,0:T(8,128)(2,1)}), bf16[32,24,128]{2,1,0:T(8,128)(2,1)S(1)}, u32[]{:S(2)}, u32[]{:S(2)}) async-start(bf16[32,24,128]{2,1,0:T(8,128)(2,1)} %broadcast_in_dim.29), calls=%async_computation.2 | async-start | bytes 393216 | tf_op jit(solution)/shard_map/all_to_all | solution.py:304
  144.8 7.3 %collective-permute-start.5 = (bf16[96,128]{1,0:T(8,128)(2,1)S(1)}, bf16[96,128]{1,0:T(8,128)(2,1)S(1)}, u32[]{:S(2)}, u32[]{:S(2)}) collective-permute-start(bf16[96,128]{1,0:T(8,128)(2,1)S(1)} %get-tuple-element.23.pack_own_ref), channel_id=1, source_target_pairs={{0,256},{256,0},{1,257},{257,1},{2,258},{258,2},{3,259},{259,3},{4... | collective-permute-start | bytes 73736 | tf_op jit(solution)/shard_map/ppermute | solution.py:290
  157.2 8.1 %collective-permute-start.6 = (f32[208,128]{1,0:T(8,128)S(1)}, f32[208,128]{1,0:T(8,128)S(1)}, u32[]{:S(2)}, u32[]{:S(2)}) collective-permute-start(f32[208,128]{1,0:T(8,128)S(1)} %get-tuple-element.26), channel_id=1, source_target_pairs={{0,256},{256,0},{1,257},{257,1},{2,258},{258,2},{3,259},{259,3},{4... | collective-permute-start | bytes 319496 | tf_op jit(solution)/shard_map/ppermute | solution.py:297
Sparse Core Ops, SparseCore 0:
  17.9 46.6 all-gather.4
  88.6 59.7 reduce-scatter.1

commit v3 on v2

--- a/solution.py
+++ b/solution.py
@@ -62,7 +62,44 @@
     return jnp.where(lane < low.shape[1] // 2, high, low)
 
 
-def attend(place_ref, all_ref, own_ref, pair_ref, low_ref, high_ref, bias_ref, mine_ref, other_ref, score_ref):
+def bias_of(place_ref, block, base):
+    lane = lax.broadcasted_iota(jnp.int32, (1, 128), 1)
+    return jnp.where((base + block) * 128 + lane < place_ref[2], 0.0, LOW)
+
+
+def edges_of(packed):
+    packed = packed.astype(F32)
+    return jnp.concatenate([packed, pltpu.roll(packed, 64, 1)], axis=0)
+
+
+def first_pack(place_ref, both_ref, pack_ref, pair_ref):
+    own = both_ref[place_ref[4]]
+    pair = both_ref[1 - place_ref[4]]
+    query = pair[0:64].astype(F32)
+    lane = lax.broadcasted_iota(jnp.int32, query.shape, 1)
+    edge = jnp.where(lane < 32, query, pltpu.roll(query, 64, 1))
+    edge = jnp.where(lane[0:32] < 64, edge[0:32], pltpu.roll(edge[32:64], 64, 1))
+    pair_ref[...] = pair
+    pack_ref[0:192] = own
+    pack_ref[192:224] = edge.astype(BF16)
+
+
+def lay_grads(shared_ref, grad_ref, low_ref, high_ref, turned_ref):
+    lanes = shared_ref.shape[0]
+    for i in range(lanes // 2):
+        even = shared_ref[2 * i].astype(F32)
+        odd = shared_ref[2 * i + 1].astype(F32)
+        grad_ref[16 * i : 16 * i + 16] = jnp.concatenate([even[0:8], odd[0:8]], axis=0).astype(BF16)
+        if i == 0:
+            low_ref[...] = jnp.concatenate([even[8:16], odd[8:16]], axis=0).astype(BF16)
+        if i == lanes // 2 - 1:
+            high_ref[...] = jnp.concatenate([even[8:16], odd[8:16]], axis=0).astype(BF16)
+    for piece in range(grad_ref.shape[1] // 128):
+        columns = slice(128 * piece, 128 * piece + 128)
+        turned_ref[columns] = grad_ref[:, columns].astype(F32).T.astype(BF16)
+
+
+def attend(place_ref, all_ref, own_ref, pair_ref, mine_ref, other_ref, score_ref):
     blocks = all_ref.shape[0]
     head = 64
     width = 128
@@ -70,11 +107,14 @@
     scale = head ** -0.5
     spot = place_ref[0]
     first = spot == 0
+    spot_rows = place_ref[4] * blocks
     last = spot == blocks - 1
-    low_here = all_ref[lax.rem(spot + blocks - 1, blocks), 0:head].astype(F32)
-    high_here = all_ref[lax.rem(spot + 1, blocks), 0:head].astype(F32)
-    low_there = low_ref[...].astype(F32)
-    high_there = high_ref[...].astype(F32)
+    before = lax.rem(spot + blocks - 1, blocks)
+    after = lax.rem(spot + 1, blocks)
+    low_here = all_ref[before, 0:head].astype(F32)
+    high_here = all_ref[after, 0:head].astype(F32)
+    low_there = pltpu.roll(edges_of(all_ref[before, 3 * head : 3 * head + 32]), width // 2, 1)
+    high_there = edges_of(all_ref[after, 3 * head : 3 * head + 32])
     side_own = side_of(jnp.where(first, low_there, low_here), jnp.where(last, high_there, high_here))
     side_pair = side_of(jnp.where(first, low_here, low_there), jnp.where(last, high_here, high_there))
     lane = lax.broadcasted_iota(jnp.int32, (head, width), 1)
@@ -85,7 +125,7 @@
     peak = jnp.full((1, lanes), LOW, F32)
     for b in range(blocks):
         key = jnp.concatenate(
-            [all_ref[b, head : 2 * head], rows_of(16, width, [(6, bias_ref[b : b + 1])]).astype(BF16)], axis=0
+            [all_ref[b, head : 2 * head], rows_of(16, width, [(6, bias_of(place_ref, b, spot_rows))]).astype(BF16)], axis=0
         )
         score = dot00(key, query)
         score_ref[b] = score
@@ -112,7 +152,7 @@
     return pltpu.roll(ring, (-offset) % ring.shape[1], 1)
 
 
-def middle_part(place_ref, mine_ref, got_ref, taps_ref, weight_ref, grad_ref, low_ref, high_ref, partial_ref, mix_ref, pack_ref):
+def middle_part(place_ref, mine_ref, got_ref, taps_ref, weight_ref, grad_ref, low_ref, high_ref, partial_ref, pack_ref):
     width = 128
     ring = 2 * width
     start = place_ref[1]
@@ -136,11 +176,8 @@
     gate = jax.nn.sigmoid(depth)
     swish = (depth[:, :width] * gate[:, :width]).astype(BF16)
     grad = grad_ref[...]
-    mix = dot10(swish, grad)
-    for piece in range(mix_ref.shape[0]):
-        mix_ref[piece] = mix[:, piece * 128 : (piece + 1) * 128].astype(BF16)
     weight = weight_ref[...]
-    partial_ref[...] = dot00(swish, weight)
+    partial_ref[...] = dot00(swish, weight).astype(BF16)
     gap = jnp.zeros((width - 2 * RIM, grad.shape[1]), BF16)
     side = jnp.concatenate([high_ref[...], gap, low_ref[...]], axis=0)
     back = jnp.concatenate([dot11(weight, grad), dot11(weight, side)], axis=1)
@@ -160,11 +197,14 @@
     a, b, c = split3(-lse[:, :width])
     d, e, f = split3(-delta)
     stats = rows_of(16, width, [(0, a), (1, b), (2, c), (3, d), (4, e), (5, f), (6, 1.0)])
-    pack_ref[...] = jnp.concatenate([grad_out, stats.astype(BF16), tap_grad], axis=0)
-
-
-def backward(all_ref, packs_ref, own_ref, pair_ref, pack_own_ref, pack_pair_ref, bias_ref, pair_bias_ref, mine_ref, other_ref):
+    pack_ref[...] = jnp.concatenate([grad_out, stats.astype(BF16), tap_grad, swish], axis=0)
+
+
+def backward(place_ref, all_ref, packs_ref, own_ref, pair_ref, pack_own_ref, pack_pair_ref, mine_ref, other_ref):
     blocks = all_ref.shape[0]
+    base = place_ref[4] * blocks
+    pair_base = blocks - base
+    pair_bias = jnp.concatenate([bias_of(place_ref, place_ref[0], base), bias_of(place_ref, place_ref[0], pair_base)], axis=1)
     head = 64
     width = 128
     scale = head ** -0.5
@@ -173,7 +213,7 @@
     query = (both[0:head].astype(F32) * scale).astype(BF16)
     query = jnp.concatenate([query, packs[head : head + 16]], axis=0)
     ones = [(0, 1.0), (1, 1.0), (2, 1.0)]
-    key_rows = rows_of(16, 2 * width, ones + [(6, pair_bias_ref[0:1])]).astype(BF16)
+    key_rows = rows_of(16, 2 * width, ones + [(6, pair_bias)]).astype(BF16)
     key = jnp.concatenate([both[head : 2 * head], key_rows], axis=0)
     value_rows = rows_of(16, 2 * width, [(3, 1.0), (4, 1.0), (5, 1.0)]).astype(BF16)
     value = jnp.concatenate([both[2 * head : 3 * head], value_rows], axis=0)
@@ -183,7 +223,7 @@
     tap_sum = jnp.zeros((16, width), F32)
     for b in range(blocks):
         key_b = all_ref[b, head : 2 * head]
-        key_aug = jnp.concatenate([key_b, rows_of(16, width, ones + [(6, bias_ref[b : b + 1])]).astype(BF16)], axis=0)
+        key_aug = jnp.concatenate([key_b, rows_of(16, width, ones + [(6, bias_of(place_ref, b, base))]).astype(BF16)], axis=0)
         value_aug = jnp.concatenate([all_ref[b, 2 * head : 3 * head], value_rows[:, :width]], axis=0)
         weight = jnp.exp(dot00(key_aug, query))
         d_score = (weight * dot00(value_aug, packs)).astype(BF16)
@@ -214,16 +254,30 @@
     taps_ref[16:32] = tap[:, 64:128]
 
 
-def mix_sum(parts_ref, out_ref):
+def mix_slab(packs_ref, slab_ref, out_ref):
+    total = jnp.zeros(out_ref.shape, F32)
+    for b in range(packs_ref.shape[0]):
+        total = total + dot11(packs_ref[b, 96:160], slab_ref[b])
+    out_ref[...] = total
+
+
+def mix_spread(mine_ref, got_ref, out_ref):
+    total = (mine_ref[...] + got_ref[...]).astype(BF16)
+    for j in range(out_ref.shape[0]):
+        out_ref[j] = total
+
+
+def mix_place(norm, parts_ref, out_ref):
+    step = parts_ref.shape[2]
+    for piece in range(parts_ref.shape[0]):
+        out_ref[:, piece * step : (piece + 1) * step] = parts_ref[piece].astype(F32) * norm
+
+
+def sum_blocks(parts_ref, out_ref):
     total = jnp.zeros(out_ref.shape, F32)
     for j in range(parts_ref.shape[0]):
         total = total + parts_ref[j].astype(F32)
     out_ref[...] = total.astype(BF16)
-
-
-def mix_place(norm, parts_ref, out_ref):
-    for piece in range(parts_ref.shape[0]):
-        out_ref[:, piece * 128 : (piece + 1) * 128] = parts_ref[piece].astype(F32) * norm
 
 
 def body(query_rows, key_rows, value_rows, valid_frames, depth_kernel, mix_weight, out_grad):
@@ -238,17 +292,9 @@
     valid = valid_frames[0]
     half = lax.axis_index("yh")
     spot = lax.axis_index("z")
-    frame = jnp.arange(width, dtype=jnp.int32)
-    half_ids = (half * depth + jnp.arange(depth, dtype=jnp.int32)[:, None]) * width + frame[None, :]
-    key_bias = jnp.where(half_ids < valid, 0.0, LOW).astype(F32)
-    own_ids = (half * depth + spot) * width + frame
-    pair_ids = ((1 - half) * depth + spot) * width + frame
-    pair_bias = jnp.where(jnp.concatenate([own_ids, pair_ids]) < valid, 0.0, LOW).astype(F32)[None, :]
-    place = jnp.stack([spot, (half * depth + spot) * width, valid, jnp.int32(width * devices)]).astype(jnp.int32)
+    place = jnp.stack([spot, (half * depth + spot) * width, valid, jnp.int32(width * devices), half]).astype(jnp.int32)
     swap = [(0, 1), (1, 0)]
     taps = depth_kernel.T
-    over_up = [(h * depth + z, (1 - h) * depth + (z + 1) % depth) for h in range(2) for z in range(depth)]
-    over_down = [(h * depth + z, (1 - h) * depth + (z - 1) % depth) for h in range(2) for z in range(depth)]
     rim_pairs = []
     sides = RIM // rows8
     for i in range(devices - 1):
@@ -257,51 +303,62 @@
             rim_pairs.append(((i + 1) * lanes + k, i * lanes + lanes - sides + k))
 
     rim_rows = lax.ppermute(out_grad, ("yh", "z", "tp"), rim_pairs)
-    shared = lax.all_gather(jnp.concatenate([out_grad, rim_rows, mix_weight], axis=0), "tp", axis=0)
-    query_turned = query_rows.T
-    low = lax.ppermute(query_turned, ctx, over_up)
-    high = lax.ppermute(query_turned, ctx, over_down)
-    own = jnp.concatenate([query_turned, key_rows.T, value_rows.T], axis=0)
-    pair = lax.ppermute(own, "yh", swap)
-    everyone = lax.all_gather(own, "z", axis=0)
+    own = jnp.concatenate([query_rows.T, key_rows.T, value_rows.T], axis=0)
+    both = lax.all_gather(own, "yh", axis=0)
+    rim_rows, both = lax.optimization_barrier((rim_rows, both))
+    front, pair = call(
+        first_pack,
+        (jax.ShapeDtypeStruct((3 * head + 32, width), BF16), jax.ShapeDtypeStruct((3 * head, width), BF16)),
+        2 ** 20,
+        scalars=1,
+    )(place, both)
+    with_rim = jnp.concatenate([out_grad, rim_rows], axis=0)
+    shared = lax.all_to_all(jnp.broadcast_to(with_rim[None], (lanes,) + with_rim.shape), "tp", 0, 0, tiled=True)
+    everyone = lax.all_gather(front, "z", axis=0)
+    shared, everyone = lax.optimization_barrier((shared, everyone))
 
     part = jax.ShapeDtypeStruct((head + 8, 2 * width), F32)
     block = jax.ShapeDtypeStruct((head, width), BF16)
     mine, other = call(
         attend, (part, part), 2 ** 28, [pltpu.VMEM((depth, width, 3 * width), F32)], scalars=1
-    )(place, everyone, own, pair, low, high, key_bias)
+    )(place, everyone, own, pair)
+    shared, other = lax.optimization_barrier((shared, other))
     got = lax.ppermute(other, "yh", swap)
-    grad_block = shared[:, :rows8].reshape(lanes * rows8, model)
-    grad_low = shared[:sides, rows8 : 2 * rows8].reshape(RIM, model)
-    grad_high = shared[lanes - sides :, rows8 : 2 * rows8].reshape(RIM, model)
-    partial, mix_parts, pack = call(
+    rim_shape = jax.ShapeDtypeStruct((RIM, model), BF16)
+    grad_block, grad_low, grad_high, turned = call(
+        lay_grads,
+        (jax.ShapeDtypeStruct((width, model), BF16), rim_shape, rim_shape, jax.ShapeDtypeStruct((model, width), BF16)),
+        2 ** 33,
+    )(shared)
+    slab = lax.all_to_all(turned.reshape(depth, model // depth, width), "z", 0, 0, tiled=True)
+    partial, pack = call(
         middle_part,
-        (
-            jax.ShapeDtypeStruct((width, model), F32),
-            jax.ShapeDtypeStruct((model // 128, head, 128), BF16),
-            jax.ShapeDtypeStruct((96, width), BF16),
-        ),
+        (jax.ShapeDtypeStruct((width, model), BF16), jax.ShapeDtypeStruct((96 + head, width), BF16)),
         2 ** 27,
         scalars=1,
     )(place, mine, got, taps, mix_weight, grad_block, grad_low, grad_high)
-    block_out = lax.psum_scatter(partial, "tp", scatter_dimension=0, tiled=True).astype(BF16)
-    chunk = head * model // 128 // devices
-    mix_mine = lax.all_to_all(mix_parts.reshape(devices, chunk, 128), ctx, 0, 0, tiled=True)
     pack_pair = lax.ppermute(pack, "yh", swap)
     packs = lax.all_gather(pack, "z", axis=0)
-    mix_mine, packs = lax.optimization_barrier((mix_mine, packs))
+    packs, slab, partial = lax.optimization_barrier((packs, slab, partial))
+
+    slab_shape = jax.ShapeDtypeStruct((head, model // depth), F32)
+    mix_mine = call(mix_slab, slab_shape, 2 ** 27)(packs, slab)
+    mix_got = lax.ppermute(mix_mine, "yh", swap)
+    block_parts = lax.all_to_all(partial.reshape(lanes, rows8, model), "tp", 0, 0, tiled=True)
+    packs, mix_mine = lax.optimization_barrier((packs, mix_mine))
     result = jax.ShapeDtypeStruct((3 * head + 16, width), F32)
-    mine, other = call(backward, (result, result), 2 ** 29)(
-        everyone, packs, own, pair, pack, pack_pair, key_bias, pair_bias
+    mine, other = call(backward, (result, result), 2 ** 29, scalars=1)(
+        place, everyone, packs, own, pair, pack, pack_pair
     )
     got = lax.ppermute(other, "yh", swap)
     d_query, d_key, d_value, tap_total = call(
         functools.partial(finish, norm), (block, block, block, jax.ShapeDtypeStruct((KSIZE, head), F32)), 2 ** 20
     )(mine, got)
 
-    mix_total = call(mix_sum, jax.ShapeDtypeStruct((chunk, 128), BF16), 2 ** 20)(mix_mine)
-    spread = jnp.broadcast_to(mix_total[None], (devices, chunk, 128))
-    pieces = lax.all_to_all(spread, ctx, 0, 0, tiled=True).reshape(model // 128, head, 128)
+    mix_got, block_parts = lax.optimization_barrier((mix_got, block_parts))
+    spread = call(mix_spread, jax.ShapeDtypeStruct((depth, head, model // depth), BF16), 2 ** 20)(mix_mine, mix_got)
+    pieces = lax.all_to_all(spread, "z", 0, 0, tiled=True)
+    block_out = call(sum_blocks, jax.ShapeDtypeStruct((rows8, model), BF16), 2 ** 20)(block_parts)
     mix_grad = call(functools.partial(mix_place, norm), jax.ShapeDtypeStruct((head, model), F32), 2 ** 20)(pieces)
     return block_out, d_query.T, d_key.T, d_value.T, mix_grad, tap_total
 

time: 176 us -> 164 us (0.932)
  the two profiles are of different devices: /device:TPU:30 before, /device:TPU:32 now
where the time goes in v3:
time: 164 us; the launch traced here: 163 us
  blocking collectives  78.2 us (48%)
  starting transfers between devices  51.6 us (31%)
  Pallas kernels  16.1 us (10%)
  waiting for transfers between devices  14.1 us (9%)
    all_gather x1, blocking collectives, body(): everyone = lax.all_gather(front, 'z', axis=0)  39.9 us
    all_gather x1, blocking collectives, body(): packs = lax.all_gather(pack, 'z', axis=0)  31.9 us
    all_to_all x1, starting transfers between devices, body(): pieces = lax.all_to_all(spread, 'z', 0, 0, tiled=True)  10.2 us
    ppermute x2, starting transfers between devices, body(): got = lax.ppermute(other, 'yh', swap)  9.13 us
    all_to_all x1, starting transfers between devices, body(): lax.all_to_all(turned.reshape(depth, model // depth, width), 'z', 0, 0, t...  8.59 us
    ppermute x2, waiting for transfers between devices, body(): got = lax.ppermute(other, 'yh', swap)  6.6 us
    all_gather x1, blocking collectives, body(): both = lax.all_gather(own, 'yh', axis=0)  6.39 us
    all_to_all x1, starting transfers between devices, body(): lax.all_to_all(partial.reshape(lanes, rows8, model), 'tp', 0, 0, tiled=True)  5.71 us
  transfers between devices with their start and end apart: 9, of which 4 were waited for; matrix products, arithmetic and copies ran while one was open for 1% of the time, Pallas kernels for 7%

profile of v3, /device:TPU:32, one launch (start us, length us, event | category | flops | bytes accessed | tf_op | source)
XLA Modules:
  0.0 163.3 jit_solution(14964691187499968138)
XLA Ops:
  0.6 5.2 %collective-permute-start = (bf16[8,1536]{1,0:T(8,128)(2,1)}, bf16[8,1536]{1,0:T(8,128)(2,1)S(1)}, u32[]{:S(2)}, u32[]{:S(2)}) collective-permute-start(bf16[8,1536]{1,0:T(8,128)(2,1)} %param.13), channel_id=1, source_target_pairs={{14,16},{16,14},{15,17},{17,15},{30,32},{32,30},{31,33},{33,31},{4... | collective-permute-start | bytes 73736 | tf_op jit(solution)/shard_map/ppermute | solution.py:305
  5.9 0.8 pad_maximum_fusion.own_ref
  6.6 6.4 %all-gather = bf16[384,128]{1,0:T(8,128)(2,1)S(1)} all-gather(bf16[192,128]{1,0:T(8,128)(2,1)S(1)} %pad_maximum_fusion.own_ref), channel_id=2, replica_groups=mesh['yh'=2,'z'=16,'tp'=16] {'yh'}, dimensions={0}, use_global_device_ids=true | all-gather | bytes 147456 | tf_op jit(solution)/shard_map/all_gather | solution.py:307
  13.0 0.0 collective-permute-done
  13.0 1.0 broadcast_in_dim.2
  14.0 3.6 %all-to-all-start = ((bf16[16,16,1536]{2,1,0:T(8,128)(2,1)}), bf16[16,16,1536]{2,1,0:T(8,128)(2,1)S(1)}, u32[]{:S(2)}, u32[]{:S(2)}) async-start(bf16[16,16,1536]{2,1,0:T(8,128)(2,1)} %broadcast_in_dim.2), calls=%async_computation | async-start | bytes 1572864 | tf_op jit(solution)/shard_map/all_to_all | solution.py:316
  18.3 0.1 stack.15.place_ref
  18.3 0.7 shard_map.118
  19.0 39.9 %all-gather.1 = bf16[3584,128]{1,0:T(8,128)(2,1)S(1)} all-gather(bf16[224,128]{1,0:T(8,128)(2,1)S(1)} %get-tuple-element.37), channel_id=3, replica_groups=mesh['yh'=2,'z'=16,'tp'=16] {'z'}, dimensions={0}, use_global_device_ids=true | all-gather | bytes 974848 | tf_op jit(solution)/shard_map/all_gather | solution.py:317
  59.0 2.2 %shard_map.119 = (f32[72,256]{1,0:T(8,128)S(1)}, f32[72,256]{1,0:T(8,128)S(1)}) custom-call(s32[5]{0:T(128)S(1)} %stack.15.place_ref, bf16[16,224,128]{2,1,0:T(8,128)(2,1)S(1)} %bitcast.15, bf16[192,128]{1,0:T(8,128)(2,1)S(1)} %pad_maximum_fusion.own_ref, bf16[192,128]{1,0:T(8,128)(2,1)S(1)} %get-tuple-element.39.pair_ref), custom_call_target="tpu_custom_call" | custom-call | flops 268435456 | bytes 1048576 | tf_op jit(solution)/shard_map/pallas_call | solution.py:322
  61.1 0.9 shard_map.120
  62.1 8.6 %all-to-all-start.1 = ((bf16[16,96,128]{2,1,0:T(8,128)(2,1)}), bf16[16,96,128]{2,1,0:T(8,128)(2,1)S(1)}, u32[]{:S(2)}, u32[]{:S(2)}) async-start(bf16[16,96,128]{2,1,0:T(8,128)(2,1)} %bitcast.10), calls=%async_computation.1 | async-start | bytes 786432 | tf_op jit(solution)/shard_map/all_to_all | solution.py:333
  70.7 4.8 %collective-permute-start.1 = (f32[72,256]{1,0:T(8,128)S(1)}, f32[72,256]{1,0:T(8,128)S(1)}, u32[]{:S(2)}, u32[]{:S(2)}) collective-permute-start(f32[72,256]{1,0:T(8,128)S(1)} %get-tuple-element.43), channel_id=1, source_target_pairs={{0,256},{256,0},{1,257},{257,1},{2,258},{258,2},{3,259},{259,3},{4... | collective-permute-start | bytes 221192 | tf_op jit(solution)/shard_map/ppermute | solution.py:326
  75.5 0.1 copy.13
  75.6 2.8 %collective-permute-done.1.got_ref = f32[72,256]{1,0:T(8,128)S(1)} collective-permute-done((f32[72,256]{1,0:T(8,128)S(1)}, f32[72,256]{1,0:T(8,128)S(1)}, u32[]{:S(2)}, u32[]{:S(2)}) %collective-permute-start.1) | collective-permute-done | bytes 73760 | tf_op jit(solution)/shard_map/ppermute | solution.py:326
  78.4 3.3 %shard_map.121 = (bf16[128,1536]{1,0:T(8,128)(2,1)}, bf16[160,128]{1,0:T(8,128)(2,1)S(1)}) custom-call(s32[5]{0:T(128)S(1)} %stack.15.place_ref, f32[72,256]{1,0:T(8,128)S(1)} %get-tuple-element.40.mine_ref, f32[72,256]{1,0:T(8,128)S(1)} %collective-permute-done.1.got_ref, f32[64,32]{1,0:T(8,128)S(1)} %bitcast.20, bf16[64,1536]{1,0:T(8,128)(2,1)S(1)} %copy-done, ...), custom_call_target="tpu_custom_call" | custom-call | flops 134217728 | bytes 1048576 | tf_op jit(solution)/shard_map/pallas_call | solution.py:334
  81.7 31.9 %all-gather.2 = bf16[2560,128]{1,0:T(8,128)(2,1)S(1)} all-gather(bf16[160,128]{1,0:T(8,128)(2,1)S(1)} %get-tuple-element.48.pack_own_ref), channel_id=4, replica_groups=mesh['yh'=2,'z'=16,'tp'=16] {'z'}, dimensions={0}, use_global_device_ids=true | all-gather | bytes 696320 | tf_op jit(solution)/shard_map/all_gather | solution.py:341
  113.6 5.7 %all-to-all-start.2 = ((bf16[16,8,1536]{2,1,0:T(8,128)(2,1)}), bf16[16,8,1536]{2,1,0:T(8,128)(2,1)S(1)}, u32[]{:S(2)}, u32[]{:S(2)}) async-start(bf16[16,8,1536]{2,1,0:T(8,128)(2,1)} %bitcast.11), calls=%async_computation.2 | async-start | bytes 786432 | tf_op jit(solution)/shard_map/all_to_all | solution.py:347
  119.3 0.3 shard_map.122.mine_ref
  119.7 4.8 %collective-permute-start.2 = (f32[64,96]{1,0:T(8,128)S(1)}, f32[64,96]{1,0:T(8,128)S(1)}, u32[]{:S(2)}, u32[]{:S(2)}) collective-permute-start(f32[64,96]{1,0:T(8,128)S(1)} %shard_map.122.mine_ref), channel_id=1, source_target_pairs={{0,256},{256,0},{1,257},{257,1},{2,258},{258,2},{3,259},{259,3},{4... | collective-permute-start | bytes 73736 | tf_op jit(solution)/shard_map/ppermute | solution.py:346
  124.5 4.4 %collective-permute-done.2.got_ref = f32[64,96]{1,0:T(8,128)S(1)} collective-permute-done((f32[64,96]{1,0:T(8,128)S(1)}, f32[64,96]{1,0:T(8,128)S(1)}, u32[]{:S(2)}, u32[]{:S(2)}) %collective-permute-start.2) | collective-permute-done | bytes 24608 | tf_op jit(solution)/shard_map/ppermute | solution.py:346
  129.0 0.8 shard_map.126
  129.7 10.2 %all-to-all-start.3 = ((bf16[16,64,96]{2,1,0:T(8,128)(2,1)}), bf16[16,64,96]{2,1,0:T(8,128)(2,1)S(1)}, u32[]{:S(2)}, u32[]{:S(2)}) async-start(bf16[16,64,96]{2,1,0:T(8,128)(2,1)} %shard_map.126), calls=%async_computation.3 | async-start | bytes 524288 | tf_op jit(solution)/shard_map/all_to_all | solution.py:360
  139.9 4.3 %collective-permute-start.3 = (bf16[160,128]{1,0:T(8,128)(2,1)S(1)}, bf16[160,128]{1,0:T(8,128)(2,1)S(1)}, u32[]{:S(2)}, u32[]{:S(2)}) collective-permute-start(bf16[160,128]{1,0:T(8,128)(2,1)S(1)} %get-tuple-element.48.pack_own_ref), channel_id=1, source_target_pairs={{0,256},{256,0},{1,257},{257,1},{2,258},{258,2},{3,259},{259,3},{4... | collective-permute-start | bytes 122888 | tf_op jit(solution)/shard_map/ppermute | solution.py:340
  144.2 3.1 %collective-permute-done.3.pack_pair_ref = bf16[160,128]{1,0:T(8,128)(2,1)S(1)} collective-permute-done((bf16[160,128]{1,0:T(8,128)(2,1)S(1)}, bf16[160,128]{1,0:T(8,128)(2,1)S(1)}, u32[]{:S(2)}, u32[]{:S(2)}) %collective-permute-start.3) | collective-permute-done | bytes 40992 | tf_op jit(solution)/shard_map/ppermute | solution.py:340
  147.3 5.6 %shard_map.124 = (f32[208,128]{1,0:T(8,128)S(1)}, f32[208,128]{1,0:T(8,128)S(1)}) custom-call(s32[5]{0:T(128)S(1)} %stack.15.place_ref, bf16[16,224,128]{2,1,0:T(8,128)(2,1)S(1)} %bitcast.16, bf16[16,160,128]{2,1,0:T(8,128)(2,1)S(1)} %bitcast.18, bf16[192,128]{1,0:T(8,128)(2,1)S(1)} %pad_maximum_fusion.own_ref, ...), custom_call_target="tpu_custom_call" | custom-call | flops 536870912 | bytes 1048576 | tf_op jit(solution)/shard_map/pallas_call | solution.py:350
  152.9 4.3 %collective-permute-start.4 = (f32[208,128]{1,0:T(8,128)S(1)}, f32[208,128]{1,0:T(8,128)S(1)}, u32[]{:S(2)}, u32[]{:S(2)}) collective-permute-start(f32[208,128]{1,0:T(8,128)S(1)} %get-tuple-element.57), channel_id=1, source_target_pairs={{0,256},{256,0},{1,257},{257,1},{2,258},{258,2},{3,259},{259,3},{4... | collective-permute-start | bytes 319496 | tf_op jit(solution)/shard_map/ppermute | solution.py:353
  157.3 3.8 %collective-permute-done.4.got_ref = f32[208,128]{1,0:T(8,128)S(1)} collective-permute-done((f32[208,128]{1,0:T(8,128)S(1)}, f32[208,128]{1,0:T(8,128)S(1)}, u32[]{:S(2)}, u32[]{:S(2)}) %collective-permute-start.4) | collective-permute-done | bytes 106528 | tf_op jit(solution)/shard_map/ppermute | solution.py:353
  161.0 0.7 shard_map.125
  161.7 0.7 shard_map.123
  162.4 0.0 all-to-all-done.3.parts_ref
  162.4 0.9 shard_map.127
  (10 shorter events, 0.0 us)
Async XLA Ops:
  0.6 12.4 %collective-permute-start = (bf16[8,1536]{1,0:T(8,128)(2,1)}, bf16[8,1536]{1,0:T(8,128)(2,1)S(1)}, u32[]{:S(2)}, u32[]{:S(2)}) collective-permute-start(bf16[8,1536]{1,0:T(8,128)(2,1)} %param.13), channel_id=1, source_target_pairs={{14,16},{16,14},{15,17},{17,15},{30,32},{32,30},{31,33},{33,31},{4... | collective-permute-start | bytes 73736 | tf_op jit(solution)/shard_map/ppermute | solution.py:305
  6.6 6.4 %copy-start.1 = (bf16[8,1536]{1,0:T(8,128)(2,1)S(1)}, bf16[8,1536]{1,0:T(8,128)(2,1)}, u32[]{:S(2)}) copy-start(bf16[8,1536]{1,0:T(8,128)(2,1)} %param.13) | copy-start | bytes 73732
  14.0 45.0 %all-to-all-start = ((bf16[16,16,1536]{2,1,0:T(8,128)(2,1)}), bf16[16,16,1536]{2,1,0:T(8,128)(2,1)S(1)}, u32[]{:S(2)}, u32[]{:S(2)}) async-start(bf16[16,16,1536]{2,1,0:T(8,128)(2,1)} %broadcast_in_dim.2), calls=%async_computation | async-start | bytes 1572864 | tf_op jit(solution)/shard_map/all_to_all | solution.py:316
  62.1 13.4 %copy-start.2 = (f32[32,64]{1,0:T(8,128)S(1)}, f32[32,64]{1,0:T(8,128)}, u32[]{:S(2)}) copy-start(f32[32,64]{1,0:T(8,128)} %param.11) | copy-start | bytes 24580
  62.1 16.3 %copy-start = (bf16[64,1536]{1,0:T(8,128)(2,1)S(1)}, bf16[64,1536]{1,0:T(8,128)(2,1)}, u32[]{:S(2)}) copy-start(bf16[64,1536]{1,0:T(8,128)(2,1)} %weight_ref.1) | copy-start | bytes 589828
  62.1 51.5 %all-to-all-start.1 = ((bf16[16,96,128]{2,1,0:T(8,128)(2,1)}), bf16[16,96,128]{2,1,0:T(8,128)(2,1)S(1)}, u32[]{:S(2)}, u32[]{:S(2)}) async-start(bf16[16,96,128]{2,1,0:T(8,128)(2,1)} %bitcast.10), calls=%async_computation.1 | async-start | bytes 786432 | tf_op jit(solution)/shard_map/all_to_all | solution.py:333
  70.7 7.7 %collective-permute-start.1 = (f32[72,256]{1,0:T(8,128)S(1)}, f32[72,256]{1,0:T(8,128)S(1)}, u32[]{:S(2)}, u32[]{:S(2)}) collective-permute-start(f32[72,256]{1,0:T(8,128)S(1)} %get-tuple-element.43), channel_id=1, source_target_pairs={{0,256},{256,0},{1,257},{257,1},{2,258},{258,2},{3,259},{259,3},{4... | collective-permute-start | bytes 221192 | tf_op jit(solution)/shard_map/ppermute | solution.py:326
  113.6 15.4 %all-to-all-start.2 = ((bf16[16,8,1536]{2,1,0:T(8,128)(2,1)}), bf16[16,8,1536]{2,1,0:T(8,128)(2,1)S(1)}, u32[]{:S(2)}, u32[]{:S(2)}) async-start(bf16[16,8,1536]{2,1,0:T(8,128)(2,1)} %bitcast.11), calls=%async_computation.2 | async-start | bytes 786432 | tf_op jit(solution)/shard_map/all_to_all | solution.py:347
  119.7 9.3 %collective-permute-start.2 = (f32[64,96]{1,0:T(8,128)S(1)}, f32[64,96]{1,0:T(8,128)S(1)}, u32[]{:S(2)}, u32[]{:S(2)}) collective-permute-start(f32[64,96]{1,0:T(8,128)S(1)} %shard_map.122.mine_ref), channel_id=1, source_target_pairs={{0,256},{256,0},{1,257},{257,1},{2,258},{258,2},{3,259},{259,3},{4... | collective-permute-start | bytes 73736 | tf_op jit(solution)/shard_map/ppermute | solution.py:346
  129.7 32.7 %all-to-all-start.3 = ((bf16[16,64,96]{2,1,0:T(8,128)(2,1)}), bf16[16,64,96]{2,1,0:T(8,128)(2,1)S(1)}, u32[]{:S(2)}, u32[]{:S(2)}) async-start(bf16[16,64,96]{2,1,0:T(8,128)(2,1)} %shard_map.126), calls=%async_computation.3 | async-start | bytes 524288 | tf_op jit(solution)/shard_map/all_to_all | solution.py:360
  139.9 7.4 %collective-permute-start.3 = (bf16[160,128]{1,0:T(8,128)(2,1)S(1)}, bf16[160,128]{1,0:T(8,128)(2,1)S(1)}, u32[]{:S(2)}, u32[]{:S(2)}) collective-permute-start(bf16[160,128]{1,0:T(8,128)(2,1)S(1)} %get-tuple-element.48.pack_own_ref), channel_id=1, source_target_pairs={{0,256},{256,0},{1,257},{257,1},{2,258},{258,2},{3,259},{259,3},{4... | collective-permute-start | bytes 122888 | tf_op jit(solution)/shard_map/ppermute | solution.py:340
  152.9 8.1 %collective-permute-start.4 = (f32[208,128]{1,0:T(8,128)S(1)}, f32[208,128]{1,0:T(8,128)S(1)}, u32[]{:S(2)}, u32[]{:S(2)}) collective-permute-start(f32[208,128]{1,0:T(8,128)S(1)} %get-tuple-element.57), channel_id=1, source_target_pairs={{0,256},{256,0},{1,257},{257,1},{2,258},{258,2},{3,259},{259,3},{4... | collective-permute-start | bytes 319496 | tf_op jit(solution)/shard_map/ppermute | solution.py:353

commit v4 on v3

--- a/solution.py
+++ b/solution.py
@@ -132,10 +132,14 @@
         peak = jnp.maximum(peak, jnp.max(score, axis=0, keepdims=True))
     total = jnp.zeros((1, lanes), F32)
     out = jnp.zeros((head, lanes), F32)
-    for b in range(blocks):
-        weight = jnp.exp(score_ref[b] - peak)
-        total = total + jnp.sum(weight, axis=0, keepdims=True)
-        out = out + dot10(all_ref[b, 2 * head : 3 * head], weight.astype(BF16))
+    for b in range(0, blocks, 2):
+        pair_weight = []
+        for k in (b, b + 1):
+            weight = jnp.exp(score_ref[k] - peak)
+            total = total + jnp.sum(weight, axis=0, keepdims=True)
+            pair_weight.append(weight.astype(BF16))
+        values = jnp.concatenate([all_ref[b, 2 * head : 3 * head], all_ref[b + 1, 2 * head : 3 * head]], axis=1)
+        out = out + dot10(values, jnp.concatenate(pair_weight, axis=0))
     out = out / total
     lse = peak + jnp.log(total)
     both = jnp.concatenate([out, jnp.broadcast_to(lse, (8, lanes))], axis=0)
@@ -159,10 +163,11 @@
     valid = place_ref[2]
     frames = place_ref[3]
     mine = mine_ref[64:65]
-    got = got_ref[64:65]
+    side_at = 1 - place_ref[4]
+    got = got_ref[side_at, 64:65]
     top = jnp.maximum(mine, got)
     lse = top + jnp.log(jnp.exp(mine - top) + jnp.exp(got - top))
-    attn = mine_ref[0:64] * jnp.exp(mine - lse) + got_ref[0:64] * jnp.exp(got - lse)
+    attn = mine_ref[0:64] * jnp.exp(mine - lse) + got_ref[side_at, 0:64] * jnp.exp(got - lse)
     attn = attn.astype(BF16).astype(F32)
     lane = lax.broadcasted_iota(jnp.int32, (1, ring), 1)
     frame = start + jnp.where(lane < ring - width // 2, lane, lane - ring)
@@ -197,7 +202,8 @@
     a, b, c = split3(-lse[:, :width])
     d, e, f = split3(-delta)
     stats = rows_of(16, width, [(0, a), (1, b), (2, c), (3, d), (4, e), (5, f), (6, 1.0)])
-    pack_ref[...] = jnp.concatenate([grad_out, stats.astype(BF16), tap_grad, swish], axis=0)
+    pack = jnp.concatenate([grad_out, stats.astype(BF16), tap_grad, swish], axis=0)
+    pack_ref[...] = pack
 
 
 def backward(place_ref, all_ref, packs_ref, own_ref, pair_ref, pack_own_ref, pack_pair_ref, mine_ref, other_ref):
@@ -221,31 +227,37 @@
     d_key = jnp.zeros((head, 2 * width), F32)
     d_value = jnp.zeros((head, 2 * width), F32)
     tap_sum = jnp.zeros((16, width), F32)
-    for b in range(blocks):
-        key_b = all_ref[b, head : 2 * head]
-        key_aug = jnp.concatenate([key_b, rows_of(16, width, ones + [(6, bias_of(place_ref, b, base))]).astype(BF16)], axis=0)
-        value_aug = jnp.concatenate([all_ref[b, 2 * head : 3 * head], value_rows[:, :width]], axis=0)
-        weight = jnp.exp(dot00(key_aug, query))
-        d_score = (weight * dot00(value_aug, packs)).astype(BF16)
-        d_query = d_query + dot10(key_b, d_score)
-
-        query_b = (all_ref[b, 0:head].astype(F32) * scale).astype(BF16)
-        query_aug = jnp.concatenate([query_b, packs_ref[b, head : head + 16]], axis=0)
-        weight = jnp.exp(dot00(query_aug, key))
-        d_score = (weight * dot00(packs_ref[b, 0:80], value)).astype(BF16)
-        d_key = d_key + dot10(query_b, d_score)
-        d_value = d_value + dot10(packs_ref[b, 0:head], weight.astype(BF16))
-        tap_sum = tap_sum + packs_ref[b, 80:96].astype(F32)
+    for first in range(0, blocks, 2):
+        keys, queries, grads, query_scores, key_scores, weights = [], [], [], [], [], []
+        for b in (first, first + 1):
+            key_b = all_ref[b, head : 2 * head]
+            key_aug = jnp.concatenate([key_b, rows_of(16, width, ones + [(6, bias_of(place_ref, b, base))]).astype(BF16)], axis=0)
+            value_aug = jnp.concatenate([all_ref[b, 2 * head : 3 * head], value_rows[:, :width]], axis=0)
+            weight = jnp.exp(dot00(key_aug, query))
+            query_scores.append((weight * dot00(value_aug, packs)).astype(BF16))
+            keys.append(key_b)
+            query_b = (all_ref[b, 0:head].astype(F32) * scale).astype(BF16)
+            query_aug = jnp.concatenate([query_b, packs_ref[b, head : head + 16]], axis=0)
+            weight = jnp.exp(dot00(query_aug, key))
+            key_scores.append((weight * dot00(packs_ref[b, 0:80], value)).astype(BF16))
+            weights.append(weight.astype(BF16))
+            queries.append(query_b)
+            grads.append(packs_ref[b, 0:head])
+            tap_sum = tap_sum + packs_ref[b, 80:96].astype(F32)
+        d_query = d_query + dot10(jnp.concatenate(keys, axis=1), jnp.concatenate(query_scores, axis=0))
+        d_key = d_key + dot10(jnp.concatenate(queries, axis=1), jnp.concatenate(key_scores, axis=0))
+        d_value = d_value + dot10(jnp.concatenate(grads, axis=1), jnp.concatenate(weights, axis=0))
     d_query = d_query * scale
     for ref, at in ((mine_ref, 0), (other_ref, width)):
-        ref[0:head] = d_query[:, at : at + width]
-        ref[head : 2 * head] = d_key[:, at : at + width]
-        ref[2 * head : 3 * head] = d_value[:, at : at + width]
-        ref[3 * head : 3 * head + 16] = tap_sum
+        kind = ref.dtype
+        ref[0:head] = d_query[:, at : at + width].astype(kind)
+        ref[head : 2 * head] = d_key[:, at : at + width].astype(kind)
+        ref[2 * head : 3 * head] = d_value[:, at : at + width].astype(kind)
+        ref[3 * head : 3 * head + 16] = tap_sum.astype(kind)
 
 
 def finish(norm, mine_ref, got_ref, query_ref, key_ref, value_ref, taps_ref):
-    total = mine_ref[...] + got_ref[...]
+    total = mine_ref[...] + got_ref[...].astype(F32)
     query_ref[...] = total[0:64].astype(BF16)
     key_ref[...] = total[64:128].astype(BF16)
     value_ref[...] = total[128:192].astype(BF16)
@@ -255,22 +267,28 @@
 
 
 def mix_slab(packs_ref, slab_ref, out_ref):
-    total = jnp.zeros(out_ref.shape, F32)
+    rows = out_ref.shape[0]
+    total = jnp.zeros((2 * rows, 64), F32)
     for b in range(packs_ref.shape[0]):
-        total = total + dot11(packs_ref[b, 96:160], slab_ref[b])
-    out_ref[...] = total
-
-
-def mix_spread(mine_ref, got_ref, out_ref):
-    total = (mine_ref[...] + got_ref[...]).astype(BF16)
+        total = total + dot11(slab_ref[b], packs_ref[b, 96:160])
+    out_ref[...] = jnp.concatenate([total[0:rows], total[rows:]], axis=1)
+
+
+def mix_spread(both_ref, out_ref):
+    total = (both_ref[0] + both_ref[1]).astype(BF16)
     for j in range(out_ref.shape[0]):
         out_ref[j] = total
 
 
 def mix_place(norm, parts_ref, out_ref):
-    step = parts_ref.shape[2]
-    for piece in range(parts_ref.shape[0]):
-        out_ref[:, piece * step : (piece + 1) * step] = parts_ref[piece].astype(F32) * norm
+    rows = []
+    for z in range(parts_ref.shape[0]):
+        both = parts_ref[z].astype(F32)
+        rows += [both[:, 0:64], both[:, 64:128]]
+    full = jnp.concatenate(rows, axis=0) * norm
+    for piece in range(out_ref.shape[1] // 128):
+        columns = slice(128 * piece, 128 * piece + 128)
+        out_ref[:, columns] = full[columns].T
 
 
 def sum_blocks(parts_ref, out_ref):
@@ -323,7 +341,7 @@
         attend, (part, part), 2 ** 28, [pltpu.VMEM((depth, width, 3 * width), F32)], scalars=1
     )(place, everyone, own, pair)
     shared, other = lax.optimization_barrier((shared, other))
-    got = lax.ppermute(other, "yh", swap)
+    got = lax.all_gather(other, "yh", axis=0)
     rim_shape = jax.ShapeDtypeStruct((RIM, model), BF16)
     grad_block, grad_low, grad_high, turned = call(
         lay_grads,
@@ -331,23 +349,30 @@
         2 ** 33,
     )(shared)
     slab = lax.all_to_all(turned.reshape(depth, model // depth, width), "z", 0, 0, tiled=True)
+    pack_rows = 96 + head
     partial, pack = call(
         middle_part,
-        (jax.ShapeDtypeStruct((width, model), BF16), jax.ShapeDtypeStruct((96 + head, width), BF16)),
+        (
+            jax.ShapeDtypeStruct((width, model), BF16),
+            jax.ShapeDtypeStruct((pack_rows, width), BF16),
+        ),
         2 ** 27,
         scalars=1,
     )(place, mine, got, taps, mix_weight, grad_block, grad_low, grad_high)
     pack_pair = lax.ppermute(pack, "yh", swap)
     packs = lax.all_gather(pack, "z", axis=0)
-    packs, slab, partial = lax.optimization_barrier((packs, slab, partial))
-
-    slab_shape = jax.ShapeDtypeStruct((head, model // depth), F32)
-    mix_mine = call(mix_slab, slab_shape, 2 ** 27)(packs, slab)
-    mix_got = lax.ppermute(mix_mine, "yh", swap)
+    packs, pack_pair, slab, partial = lax.optimization_barrier((packs, pack_pair, slab, partial))
+
+    slab_rows = model // depth // 2
+    mix_mine = call(mix_slab, jax.ShapeDtypeStruct((slab_rows, width), F32), 2 ** 27)(packs, slab)
+    mix_both = lax.all_gather(mix_mine, "yh", axis=0)
+    spread = call(mix_spread, jax.ShapeDtypeStruct((depth, slab_rows, width), BF16), 2 ** 20)(mix_both)
     block_parts = lax.all_to_all(partial.reshape(lanes, rows8, model), "tp", 0, 0, tiled=True)
-    packs, mix_mine = lax.optimization_barrier((packs, mix_mine))
+    spread, block_parts = lax.optimization_barrier((spread, block_parts))
+    pieces = lax.all_to_all(spread, "z", 0, 0, tiled=True)
     result = jax.ShapeDtypeStruct((3 * head + 16, width), F32)
-    mine, other = call(backward, (result, result), 2 ** 29, scalars=1)(
+    sent = jax.ShapeDtypeStruct(result.shape, BF16)
+    mine, other = call(backward, (result, sent), 2 ** 29, scalars=1)(
         place, everyone, packs, own, pair, pack, pack_pair
     )
     got = lax.ppermute(other, "yh", swap)
@@ -355,9 +380,6 @@
         functools.partial(finish, norm), (block, block, block, jax.ShapeDtypeStruct((KSIZE, head), F32)), 2 ** 20
     )(mine, got)
 
-    mix_got, block_parts = lax.optimization_barrier((mix_got, block_parts))
-    spread = call(mix_spread, jax.ShapeDtypeStruct((depth, head, model // depth), BF16), 2 ** 20)(mix_mine, mix_got)
-    pieces = lax.all_to_all(spread, "z", 0, 0, tiled=True)
     block_out = call(sum_blocks, jax.ShapeDtypeStruct((rows8, model), BF16), 2 ** 20)(block_parts)
     mix_grad = call(functools.partial(mix_place, norm), jax.ShapeDtypeStruct((head, model), F32), 2 ** 20)(pieces)
     return block_out, d_query.T, d_key.T, d_value.T, mix_grad, tap_total

time: 164 us -> 159 us (0.970)
  the two profiles are of different devices: /device:TPU:32 before, /device:TPU:8 now
where the time goes in v4:
time: 159 us
  blocking collectives  87 us (55%)
  starting transfers between devices  45.7 us (29%)
  Pallas kernels  13.6 us (9%)
  waiting for transfers between devices  9.08 us (6%)
    all_gather x1, blocking collectives, body(): everyone = lax.all_gather(front, 'z', axis=0)  33.6 us
    all_gather x1, blocking collectives, body(): packs = lax.all_gather(pack, 'z', axis=0)  33.5 us
    all_to_all x1, starting transfers between devices, body(): lax.all_to_all(jnp.broadcast_to(with_rim[None], (lanes,) + with_rim.shape...  16.4 us
    all_to_all x1, starting transfers between devices, body(): pieces = lax.all_to_all(spread, 'z', 0, 0, tiled=True)  8.86 us
    all_gather x1, blocking collectives, body(): mix_both = lax.all_gather(mix_mine, 'yh', axis=0)  7.03 us
    all_to_all x1, starting transfers between devices, body(): lax.all_to_all(turned.reshape(depth, model // depth, width), 'z', 0, 0, t...  6.87 us
    all_gather x1, blocking collectives, body(): got = lax.all_gather(other, 'yh', axis=0)  6.53 us
    all_gather x1, blocking collectives, body(): both = lax.all_gather(own, 'yh', axis=0)  6.39 us
  transfers between devices with their start and end apart: 7, of which 2 were waited for; matrix products, arithmetic and copies ran while one was open for 1% of the time, Pallas kernels for 6%

profile of v4, /device:TPU:8, one launch (start us, length us, event | category | flops | bytes accessed | tf_op | source)
XLA Modules:
  0.0 158.7 jit_solution(4523635267238325272)
XLA Ops:
  0.6 0.7 collective-permute-start
  1.3 0.8 pad_maximum_fusion.own_ref
  2.1 6.4 %all-gather = bf16[384,128]{1,0:T(8,128)(2,1)S(1)} all-gather(bf16[192,128]{1,0:T(8,128)(2,1)S(1)} %pad_maximum_fusion.own_ref), channel_id=2, replica_groups=mesh['yh'=2,'z'=16,'tp'=16] {'yh'}, dimensions={0}, use_global_device_ids=true | all-gather | bytes 147456 | tf_op jit(solution)/shard_map/all_gather | solution.py:325
  8.5 0.0 collective-permute-done
  8.5 1.0 broadcast_in_dim.2
  9.4 16.4 %all-to-all-start = ((bf16[16,16,1536]{2,1,0:T(8,128)(2,1)}), bf16[16,16,1536]{2,1,0:T(8,128)(2,1)S(1)}, u32[]{:S(2)}, u32[]{:S(2)}) async-start(bf16[16,16,1536]{2,1,0:T(8,128)(2,1)} %broadcast_in_dim.2), calls=%async_computation | async-start | bytes 1572864 | tf_op jit(solution)/shard_map/all_to_all | solution.py:334
  26.4 0.1 stack.15.place_ref
  26.5 0.7 shard_map.118
  27.2 33.6 %all-gather.1 = bf16[3584,128]{1,0:T(8,128)(2,1)S(1)} all-gather(bf16[224,128]{1,0:T(8,128)(2,1)S(1)} %get-tuple-element.36), channel_id=3, replica_groups=mesh['yh'=2,'z'=16,'tp'=16] {'z'}, dimensions={0}, use_global_device_ids=true | all-gather | bytes 974848 | tf_op jit(solution)/shard_map/all_gather | solution.py:335
  60.9 0.0 all-to-all-done.shared_ref
  60.9 2.2 %shard_map.119 = (f32[72,256]{1,0:T(8,128)S(1)}, f32[72,256]{1,0:T(8,128)S(1)}) custom-call(s32[5]{0:T(128)S(1)} %stack.15.place_ref, bf16[16,224,128]{2,1,0:T(8,128)(2,1)S(1)} %bitcast.17, bf16[192,128]{1,0:T(8,128)(2,1)S(1)} %pad_maximum_fusion.own_ref, bf16[192,128]{1,0:T(8,128)(2,1)S(1)} %get-tuple-element.38.pair_ref), custom_call_target="tpu_custom_call" | custom-call | flops 268435456 | bytes 1048576 | tf_op jit(solution)/shard_map/pallas_call | solution.py:340
  63.1 0.9 shard_map.120
  64.0 6.9 %all-to-all-start.1 = ((bf16[16,96,128]{2,1,0:T(8,128)(2,1)}), bf16[16,96,128]{2,1,0:T(8,128)(2,1)S(1)}, u32[]{:S(2)}, u32[]{:S(2)}) async-start(bf16[16,96,128]{2,1,0:T(8,128)(2,1)} %bitcast.11), calls=%async_computation.1 | async-start | bytes 786432 | tf_op jit(solution)/shard_map/all_to_all | solution.py:351
  70.9 0.0 copy-start
  70.9 0.1 copy.13
  71.0 6.5 %all-gather.2 = f32[144,256]{1,0:T(8,128)S(1)} all-gather(f32[72,256]{1,0:T(8,128)S(1)} %get-tuple-element.42), channel_id=4, replica_groups=mesh['yh'=2,'z'=16,'tp'=16] {'yh'}, dimensions={0}, use_global_device_ids=true | all-gather | bytes 221184 | tf_op jit(solution)/shard_map/all_gather | solution.py:344
  77.5 3.3 %shard_map.121 = (bf16[128,1536]{1,0:T(8,128)(2,1)}, bf16[160,128]{1,0:T(8,128)(2,1)S(1)}) custom-call(s32[5]{0:T(128)S(1)} %stack.15.place_ref, f32[72,256]{1,0:T(8,128)S(1)} %get-tuple-element.39.mine_ref, f32[2,72,256]{2,1,0:T(8,128)S(1)} %bitcast.21, f32[64,32]{1,0:T(8,128)S(1)} %bitcast.24, bf16[64,1536]{1,0:T(8,128)(2,1)S(1)} %copy-done, ...), custom_call_target="tpu_custom_call" | custom-call | flops 134217728 | bytes 1048576 | tf_op jit(solution)/shard_map/pallas_call | solution.py:353
  80.8 4.2 %collective-permute-start.1 = (bf16[160,128]{1,0:T(8,128)(2,1)S(1)}, bf16[160,128]{1,0:T(8,128)(2,1)S(1)}, u32[]{:S(2)}, u32[]{:S(2)}) collective-permute-start(bf16[160,128]{1,0:T(8,128)(2,1)S(1)} %get-tuple-element.47.pack_own_ref), channel_id=1, source_target_pairs={{0,256},{256,0},{1,257},{257,1},{2,258},{258,2},{3,259},{259,3},{4... | collective-permute-start | bytes 122888 | tf_op jit(solution)/shard_map/ppermute | solution.py:362
  85.0 33.5 %all-gather.3 = bf16[2560,128]{1,0:T(8,128)(2,1)S(1)} all-gather(bf16[160,128]{1,0:T(8,128)(2,1)S(1)} %get-tuple-element.47.pack_own_ref), channel_id=5, replica_groups=mesh['yh'=2,'z'=16,'tp'=16] {'z'}, dimensions={0}, use_global_device_ids=true | all-gather | bytes 696320 | tf_op jit(solution)/shard_map/all_gather | solution.py:363
  118.5 0.0 all-to-all-done.1.slab_ref
  118.5 5.8 %all-to-all-start.2 = ((bf16[16,8,1536]{2,1,0:T(8,128)(2,1)}), bf16[16,8,1536]{2,1,0:T(8,128)(2,1)S(1)}, u32[]{:S(2)}, u32[]{:S(2)}) async-start(bf16[16,8,1536]{2,1,0:T(8,128)(2,1)} %bitcast.13), calls=%async_computation.2 | async-start | bytes 786432 | tf_op jit(solution)/shard_map/all_to_all | solution.py:370
  124.3 0.3 shard_map.122
  124.6 7.0 %all-gather.4 = f32[96,128]{1,0:T(8,128)S(1)} all-gather(f32[48,128]{1,0:T(8,128)S(1)} %shard_map.122), channel_id=6, replica_groups=mesh['yh'=2,'z'=16,'tp'=16] {'yh'}, dimensions={0}, use_global_device_ids=true | all-gather | bytes 73728 | tf_op jit(solution)/shard_map/all_gather | solution.py:368
  131.6 0.7 shard_map.123
  132.3 8.9 %all-to-all-start.3 = ((bf16[16,48,128]{2,1,0:T(8,128)(2,1)}), bf16[16,48,128]{2,1,0:T(8,128)(2,1)S(1)}, u32[]{:S(2)}, u32[]{:S(2)}) async-start(bf16[16,48,128]{2,1,0:T(8,128)(2,1)} %shard_map.123), calls=%async_computation.3 | async-start | bytes 393216 | tf_op jit(solution)/shard_map/all_to_all | solution.py:372
  141.2 3.1 %shard_map.125 = (f32[208,128]{1,0:T(8,128)S(1)}, bf16[208,128]{1,0:T(8,128)(2,1)S(1)}) custom-call(s32[5]{0:T(128)S(1)} %stack.15.place_ref, bf16[16,224,128]{2,1,0:T(8,128)(2,1)S(1)} %bitcast.18, bf16[16,160,128]{2,1,0:T(8,128)(2,1)S(1)} %bitcast.20, bf16[192,128]{1,0:T(8,128)(2,1)S(1)} %pad_maximum_fusion.own_ref, ...), custom_call_target="tpu_custom_call" | custom-call | flops 536870912 | bytes 1048576 | tf_op jit(solution)/shard_map/pallas_call | solution.py:375
  144.2 3.0 %collective-permute-start.2 = (bf16[208,128]{1,0:T(8,128)(2,1)S(1)}, bf16[208,128]{1,0:T(8,128)(2,1)S(1)}, u32[]{:S(2)}, u32[]{:S(2)}) collective-permute-start(bf16[208,128]{1,0:T(8,128)(2,1)S(1)} %get-tuple-element.56), channel_id=1, source_target_pairs={{0,256},{256,0},{1,257},{257,1},{2,258},{258,2},{3,259},{259,3},{4... | collective-permute-start | bytes 159752 | tf_op jit(solution)/shard_map/ppermute | solution.py:378
  147.2 4.5 %collective-permute-done.2.got_ref = bf16[208,128]{1,0:T(8,128)(2,1)S(1)} collective-permute-done((bf16[208,128]{1,0:T(8,128)(2,1)S(1)}, bf16[208,128]{1,0:T(8,128)(2,1)S(1)}, u32[]{:S(2)}, u32[]{:S(2)}) %collective-permute-start.2) | collective-permute-done | bytes 53280 | tf_op jit(solution)/shard_map/ppermute | solution.py:378
  151.8 0.7 shard_map.126
  152.5 0.7 shard_map.124
  153.1 4.5 %all-to-all-done.3.parts_ref = bf16[16,48,128]{2,1,0:T(8,128)(2,1)S(1)} async-done(((bf16[16,48,128]{2,1,0:T(8,128)(2,1)}), bf16[16,48,128]{2,1,0:T(8,128)(2,1)S(1)}, u32[]{:S(2)}, u32[]{:S(2)}) %all-to-all-start.3) | async-done | bytes 196640 | tf_op jit(solution)/shard_map/all_to_all | solution.py:372
  157.7 1.1 shard_map.127
  (8 shorter events, 0.0 us)
Async XLA Ops:
  0.6 7.8 %collective-permute-start = (bf16[8,1536]{1,0:T(8,128)(2,1)}, bf16[8,1536]{1,0:T(8,128)(2,1)S(1)}, u32[]{:S(2)}, u32[]{:S(2)}) collective-permute-start(bf16[8,1536]{1,0:T(8,128)(2,1)} %param.13), channel_id=1, source_target_pairs={{14,16},{16,14},{15,17},{17,15},{30,32},{32,30},{31,33},{33,31},{4... | collective-permute-start | bytes 73736 | tf_op jit(solution)/shard_map/ppermute | solution.py:323
  2.1 6.4 %copy-start.1 = (bf16[8,1536]{1,0:T(8,128)(2,1)S(1)}, bf16[8,1536]{1,0:T(8,128)(2,1)}, u32[]{:S(2)}) copy-start(bf16[8,1536]{1,0:T(8,128)(2,1)} %param.13) | copy-start | bytes 73732
  9.4 51.4 %all-to-all-start = ((bf16[16,16,1536]{2,1,0:T(8,128)(2,1)}), bf16[16,16,1536]{2,1,0:T(8,128)(2,1)S(1)}, u32[]{:S(2)}, u32[]{:S(2)}) async-start(bf16[16,16,1536]{2,1,0:T(8,128)(2,1)} %broadcast_in_dim.2), calls=%async_computation | async-start | bytes 1572864 | tf_op jit(solution)/shard_map/all_to_all | solution.py:334
  64.0 6.9 %copy-start.2 = (f32[32,64]{1,0:T(8,128)S(1)}, f32[32,64]{1,0:T(8,128)}, u32[]{:S(2)}) copy-start(f32[32,64]{1,0:T(8,128)} %param.11) | copy-start | bytes 24580
  64.0 54.5 %all-to-all-start.1 = ((bf16[16,96,128]{2,1,0:T(8,128)(2,1)}), bf16[16,96,128]{2,1,0:T(8,128)(2,1)S(1)}, u32[]{:S(2)}, u32[]{:S(2)}) async-start(bf16[16,96,128]{2,1,0:T(8,128)(2,1)} %bitcast.11), calls=%async_computation.1 | async-start | bytes 786432 | tf_op jit(solution)/shard_map/all_to_all | solution.py:351
  70.9 6.6 %copy-start = (bf16[64,1536]{1,0:T(8,128)(2,1)S(1)}, bf16[64,1536]{1,0:T(8,128)(2,1)}, u32[]{:S(2)}) copy-start(bf16[64,1536]{1,0:T(8,128)(2,1)} %weight_ref.1) | copy-start | bytes 589828
  80.8 37.7 %collective-permute-start.1 = (bf16[160,128]{1,0:T(8,128)(2,1)S(1)}, bf16[160,128]{1,0:T(8,128)(2,1)S(1)}, u32[]{:S(2)}, u32[]{:S(2)}) collective-permute-start(bf16[160,128]{1,0:T(8,128)(2,1)S(1)} %get-tuple-element.47.pack_own_ref), channel_id=1, source_target_pairs={{0,256},{256,0},{1,257},{257,1},{2,258},{258,2},{3,259},{259,3},{4... | collective-permute-start | bytes 122888 | tf_op jit(solution)/shard_map/ppermute | solution.py:362
  118.5 13.8 %all-to-all-start.2 = ((bf16[16,8,1536]{2,1,0:T(8,128)(2,1)}), bf16[16,8,1536]{2,1,0:T(8,128)(2,1)S(1)}, u32[]{:S(2)}, u32[]{:S(2)}) async-start(bf16[16,8,1536]{2,1,0:T(8,128)(2,1)} %bitcast.13), calls=%async_computation.2 | async-start | bytes 786432 | tf_op jit(solution)/shard_map/all_to_all | solution.py:370
  132.3 25.3 %all-to-all-start.3 = ((bf16[16,48,128]{2,1,0:T(8,128)(2,1)}), bf16[16,48,128]{2,1,0:T(8,128)(2,1)S(1)}, u32[]{:S(2)}, u32[]{:S(2)}) async-start(bf16[16,48,128]{2,1,0:T(8,128)(2,1)} %shard_map.123), calls=%async_computation.3 | async-start | bytes 393216 | tf_op jit(solution)/shard_map/all_to_all | solution.py:372
  144.2 7.5 %collective-permute-start.2 = (bf16[208,128]{1,0:T(8,128)(2,1)S(1)}, bf16[208,128]{1,0:T(8,128)(2,1)S(1)}, u32[]{:S(2)}, u32[]{:S(2)}) collective-permute-start(bf16[208,128]{1,0:T(8,128)(2,1)S(1)} %get-tuple-element.56), channel_id=1, source_target_pairs={{0,256},{256,0},{1,257},{257,1},{2,258},{258,2},{3,259},{259,3},{4... | collective-permute-start | bytes 159752 | tf_op jit(solution)/shard_map/ppermute | solution.py:378

commit v5 on v4

--- a/solution.py
+++ b/solution.py
@@ -84,7 +84,7 @@
     pack_ref[192:224] = edge.astype(BF16)
 
 
-def lay_grads(shared_ref, grad_ref, low_ref, high_ref, turned_ref):
+def lay_grads(shared_ref, grad_ref, low_ref, high_ref):
     lanes = shared_ref.shape[0]
     for i in range(lanes // 2):
         even = shared_ref[2 * i].astype(F32)
@@ -94,9 +94,6 @@
             low_ref[...] = jnp.concatenate([even[8:16], odd[8:16]], axis=0).astype(BF16)
         if i == lanes // 2 - 1:
             high_ref[...] = jnp.concatenate([even[8:16], odd[8:16]], axis=0).astype(BF16)
-    for piece in range(grad_ref.shape[1] // 128):
-        columns = slice(128 * piece, 128 * piece + 128)
-        turned_ref[columns] = grad_ref[:, columns].astype(F32).T.astype(BF16)
 
 
 def attend(place_ref, all_ref, own_ref, pair_ref, mine_ref, other_ref, score_ref):
@@ -156,7 +153,7 @@
     return pltpu.roll(ring, (-offset) % ring.shape[1], 1)
 
 
-def middle_part(place_ref, mine_ref, got_ref, taps_ref, weight_ref, grad_ref, low_ref, high_ref, partial_ref, pack_ref):
+def middle_part(place_ref, mine_ref, got_ref, taps_ref, weight_ref, grad_ref, low_ref, high_ref, partial_ref, pack_ref, copies_ref):
     width = 128
     ring = 2 * width
     start = place_ref[1]
@@ -181,6 +178,8 @@
     gate = jax.nn.sigmoid(depth)
     swish = (depth[:, :width] * gate[:, :width]).astype(BF16)
     grad = grad_ref[...]
+    mix = dot10(swish, grad)
+    mix = jnp.concatenate([mix[:, at : at + width] for at in range(0, mix.shape[1], width)], axis=0).astype(BF16)
     weight = weight_ref[...]
     partial_ref[...] = dot00(swish, weight).astype(BF16)
     gap = jnp.zeros((width - 2 * RIM, grad.shape[1]), BF16)
@@ -202,8 +201,12 @@
     a, b, c = split3(-lse[:, :width])
     d, e, f = split3(-delta)
     stats = rows_of(16, width, [(0, a), (1, b), (2, c), (3, d), (4, e), (5, f), (6, 1.0)])
-    pack = jnp.concatenate([grad_out, stats.astype(BF16), tap_grad, swish], axis=0)
+    pack = jnp.concatenate([grad_out, stats.astype(BF16), tap_grad], axis=0)
     pack_ref[...] = pack
+    share = copies_ref.shape[1] - 96
+    for j in range(copies_ref.shape[0]):
+        copies_ref[j, 0:96] = pack
+        copies_ref[j, 96:] = mix[j * share : (j + 1) * share]
 
 
 def backward(place_ref, all_ref, packs_ref, own_ref, pair_ref, pack_own_ref, pack_pair_ref, mine_ref, other_ref):
@@ -266,12 +269,11 @@
     taps_ref[16:32] = tap[:, 64:128]
 
 
-def mix_slab(packs_ref, slab_ref, out_ref):
-    rows = out_ref.shape[0]
-    total = jnp.zeros((2 * rows, 64), F32)
-    for b in range(packs_ref.shape[0]):
-        total = total + dot11(slab_ref[b], packs_ref[b, 96:160])
-    out_ref[...] = jnp.concatenate([total[0:rows], total[rows:]], axis=1)
+def mix_sum(packs_ref, out_ref):
+    total = jnp.zeros(out_ref.shape, F32)
+    for j in range(packs_ref.shape[0]):
+        total = total + packs_ref[j, 96:].astype(F32)
+    out_ref[...] = total
 
 
 def mix_spread(both_ref, out_ref):
@@ -281,14 +283,8 @@
 
 
 def mix_place(norm, parts_ref, out_ref):
-    rows = []
-    for z in range(parts_ref.shape[0]):
-        both = parts_ref[z].astype(F32)
-        rows += [both[:, 0:64], both[:, 64:128]]
-    full = jnp.concatenate(rows, axis=0) * norm
-    for piece in range(out_ref.shape[1] // 128):
-        columns = slice(128 * piece, 128 * piece + 128)
-        out_ref[:, columns] = full[columns].T
+    for piece in range(parts_ref.shape[0]):
+        out_ref[:, piece * 128 : (piece + 1) * 128] = parts_ref[piece].astype(F32) * norm
 
 
 def sum_blocks(parts_ref, out_ref):
@@ -343,33 +339,30 @@
     shared, other = lax.optimization_barrier((shared, other))
     got = lax.all_gather(other, "yh", axis=0)
     rim_shape = jax.ShapeDtypeStruct((RIM, model), BF16)
-    grad_block, grad_low, grad_high, turned = call(
-        lay_grads,
-        (jax.ShapeDtypeStruct((width, model), BF16), rim_shape, rim_shape, jax.ShapeDtypeStruct((model, width), BF16)),
-        2 ** 33,
+    grad_block, grad_low, grad_high = call(
+        lay_grads, (jax.ShapeDtypeStruct((width, model), BF16), rim_shape, rim_shape), 2 ** 22
     )(shared)
-    slab = lax.all_to_all(turned.reshape(depth, model // depth, width), "z", 0, 0, tiled=True)
-    pack_rows = 96 + head
-    partial, pack = call(
+    share = head * model // width // depth
+    partial, pack, copies = call(
         middle_part,
         (
             jax.ShapeDtypeStruct((width, model), BF16),
-            jax.ShapeDtypeStruct((pack_rows, width), BF16),
+            jax.ShapeDtypeStruct((96, width), BF16),
+            jax.ShapeDtypeStruct((depth, 96 + share, width), BF16),
         ),
         2 ** 27,
         scalars=1,
     )(place, mine, got, taps, mix_weight, grad_block, grad_low, grad_high)
+    packs = lax.all_to_all(copies, "z", 0, 0, tiled=True)
     pack_pair = lax.ppermute(pack, "yh", swap)
-    packs = lax.all_gather(pack, "z", axis=0)
-    packs, pack_pair, slab, partial = lax.optimization_barrier((packs, pack_pair, slab, partial))
-
-    slab_rows = model // depth // 2
-    mix_mine = call(mix_slab, jax.ShapeDtypeStruct((slab_rows, width), F32), 2 ** 27)(packs, slab)
+    packs, pack_pair, partial = lax.optimization_barrier((packs, pack_pair, partial))
+
+    mix_mine = call(mix_sum, jax.ShapeDtypeStruct((share, width), F32), 2 ** 22)(packs)
     mix_both = lax.all_gather(mix_mine, "yh", axis=0)
-    spread = call(mix_spread, jax.ShapeDtypeStruct((depth, slab_rows, width), BF16), 2 ** 20)(mix_both)
+    spread = call(mix_spread, jax.ShapeDtypeStruct((depth, share, width), BF16), 2 ** 20)(mix_both)
     block_parts = lax.all_to_all(partial.reshape(lanes, rows8, model), "tp", 0, 0, tiled=True)
     spread, block_parts = lax.optimization_barrier((spread, block_parts))
-    pieces = lax.all_to_all(spread, "z", 0, 0, tiled=True)
+    pieces = lax.all_to_all(spread, "z", 0, 0, tiled=True).reshape(model // width, head, width)
     result = jax.ShapeDtypeStruct((3 * head + 16, width), F32)
     sent = jax.ShapeDtypeStruct(result.shape, BF16)
     mine, other = call(backward, (result, sent), 2 ** 29, scalars=1)(

time: 159 us -> 146 us (0.918)
  the two profiles are of different devices: /device:TPU:8 before, /device:TPU:4 now
where the time goes in v5:
time: 146 us; the launch traced here: 145 us
  blocking collectives  55.4 us (38%)
  starting transfers between devices  45.2 us (31%)
  waiting for transfers between devices  27.1 us (19%)
  Pallas kernels  13 us (9%)
  local copies, waits for them, and re-layouts  2.03 us (1%)
    all_gather x1, blocking collectives, body(): everyone = lax.all_gather(front, 'z', axis=0)  33.6 us
    all_to_all x1, starting transfers between devices, body(): lax.all_to_all(jnp.broadcast_to(with_rim[None], (lanes,) + with_rim.shape...  16.5 us
    all_to_all x1, waiting for transfers between devices, body(): packs = lax.all_to_all(copies, 'z', 0, 0, tiled=True)  15.6 us
    all_gather x1, blocking collectives, body(): mix_both = lax.all_gather(mix_mine, 'yh', axis=0)  8.81 us
    all_to_all x1, starting transfers between devices, body(): lax.all_to_all(spread, 'z', 0, 0, tiled=True)  7.81 us
    all_to_all x1, starting transfers between devices, body(): packs = lax.all_to_all(copies, 'z', 0, 0, tiled=True)  6.73 us
    all_gather x1, blocking collectives, body(): got = lax.all_gather(other, 'yh', axis=0)  6.53 us
    all_gather x1, blocking collectives, body(): both = lax.all_gather(own, 'yh', axis=0)  6.39 us
  transfers between devices with their start and end apart: 7, of which 4 were waited for; matrix products, arithmetic and copies ran while one was open for 1% of the time, Pallas kernels for 4%

profile of v5, /device:TPU:4, one launch (start us, length us, event | category | flops | bytes accessed | tf_op | source)
XLA Modules:
  0.0 144.8 jit_solution(11224878123701412373)
XLA Ops:
  0.6 0.7 collective-permute-start
  1.3 0.8 pad_maximum_fusion.own_ref
  2.1 6.4 %all-gather = bf16[384,128]{1,0:T(8,128)(2,1)S(1)} all-gather(bf16[192,128]{1,0:T(8,128)(2,1)S(1)} %pad_maximum_fusion.own_ref), channel_id=2, replica_groups=mesh['yh'=2,'z'=16,'tp'=16] {'yh'}, dimensions={0}, use_global_device_ids=true | all-gather | bytes 147456 | tf_op jit(solution)/shard_map/all_gather | solution.py:321
  8.5 0.0 collective-permute-done
  8.5 0.0 copy-done.1
  8.5 1.0 broadcast_in_dim.2
  9.4 16.5 %all-to-all-start = ((bf16[16,16,1536]{2,1,0:T(8,128)(2,1)}), bf16[16,16,1536]{2,1,0:T(8,128)(2,1)S(1)}, u32[]{:S(2)}, u32[]{:S(2)}) async-start(bf16[16,16,1536]{2,1,0:T(8,128)(2,1)} %broadcast_in_dim.2), calls=%async_computation | async-start | bytes 1572864 | tf_op jit(solution)/shard_map/all_to_all | solution.py:330
  26.6 0.1 copy.13
  26.7 0.1 stack.15.place_ref
  26.8 0.7 shard_map.118
  27.5 33.6 %all-gather.1 = bf16[3584,128]{1,0:T(8,128)(2,1)S(1)} all-gather(bf16[224,128]{1,0:T(8,128)(2,1)S(1)} %get-tuple-element.35), channel_id=3, replica_groups=mesh['yh'=2,'z'=16,'tp'=16] {'z'}, dimensions={0}, use_global_device_ids=true | all-gather | bytes 974848 | tf_op jit(solution)/shard_map/all_gather | solution.py:331
  61.1 0.0 all-to-all-done.shared_ref
  61.1 2.2 %shard_map.119 = (f32[72,256]{1,0:T(8,128)S(1)}, f32[72,256]{1,0:T(8,128)S(1)}) custom-call(s32[5]{0:T(128)S(1)} %stack.15.place_ref, bf16[16,224,128]{2,1,0:T(8,128)(2,1)S(1)} %bitcast.16, bf16[192,128]{1,0:T(8,128)(2,1)S(1)} %pad_maximum_fusion.own_ref, bf16[192,128]{1,0:T(8,128)(2,1)S(1)} %get-tuple-element.37.pair_ref), custom_call_target="tpu_custom_call" | custom-call | flops 268435456 | bytes 1048576 | tf_op jit(solution)/shard_map/pallas_call | solution.py:336
  63.4 6.5 %all-gather.2 = f32[144,256]{1,0:T(8,128)S(1)} all-gather(f32[72,256]{1,0:T(8,128)S(1)} %get-tuple-element.41), channel_id=4, replica_groups=mesh['yh'=2,'z'=16,'tp'=16] {'yh'}, dimensions={0}, use_global_device_ids=true | all-gather | bytes 221184 | tf_op jit(solution)/shard_map/all_gather | solution.py:340
  69.9 0.9 copy-done
  70.8 4.1 %shard_map.121 = (bf16[128,1536]{1,0:T(8,128)(2,1)}, bf16[96,128]{1,0:T(8,128)(2,1)S(1)}, bf16[16,144,128]{2,1,0:T(8,128)(2,1)}) custom-call(s32[5]{0:T(128)S(1)} %stack.15.place_ref, f32[72,256]{1,0:T(8,128)S(1)} %get-tuple-element.38.mine_ref, f32[2,72,256]{2,1,0:T(8,128)S(1)} %bitcast.19, f32[64,32]{1,0:T(8,128)S(1)} %bitcast.22, ...), custom_call_target="tpu_custom_call" | custom-call | flops 134217728 | bytes 1048576 | tf_op jit(solution)/shard_map/pallas_call | solution.py:346
  74.9 6.7 %all-to-all-start.1 = ((bf16[16,144,128]{2,1,0:T(8,128)(2,1)}), bf16[16,144,128]{2,1,0:T(8,128)(2,1)S(1)}, u32[]{:S(2)}, u32[]{:S(2)}) async-start(bf16[16,144,128]{2,1,0:T(8,128)(2,1)} %get-tuple-element.46), calls=%async_computation.1 | async-start | bytes 1179648 | tf_op jit(solution)/shard_map/all_to_all | solution.py:356
  81.7 4.8 %collective-permute-start.1 = (bf16[96,128]{1,0:T(8,128)(2,1)S(1)}, bf16[96,128]{1,0:T(8,128)(2,1)S(1)}, u32[]{:S(2)}, u32[]{:S(2)}) collective-permute-start(bf16[96,128]{1,0:T(8,128)(2,1)S(1)} %get-tuple-element.47.pack_own_ref), channel_id=1, source_target_pairs={{0,256},{256,0},{1,257},{257,1},{2,258},{258,2},{3,259},{259,3},{4... | collective-permute-start | bytes 73736 | tf_op jit(solution)/shard_map/ppermute | solution.py:357
  86.5 2.4 %collective-permute-done.1.pack_pair_ref = bf16[96,128]{1,0:T(8,128)(2,1)S(1)} collective-permute-done((bf16[96,128]{1,0:T(8,128)(2,1)S(1)}, bf16[96,128]{1,0:T(8,128)(2,1)S(1)}, u32[]{:S(2)}, u32[]{:S(2)}) %collective-permute-start.1) | collective-permute-done | bytes 24608 | tf_op jit(solution)/shard_map/ppermute | solution.py:357
  88.9 15.6 %all-to-all-done.1.packs_ref = bf16[16,144,128]{2,1,0:T(8,128)(2,1)S(1)} async-done(((bf16[16,144,128]{2,1,0:T(8,128)(2,1)}), bf16[16,144,128]{2,1,0:T(8,128)(2,1)S(1)}, u32[]{:S(2)}, u32[]{:S(2)}) %all-to-all-start.1) | async-done | bytes 589856 | tf_op jit(solution)/shard_map/all_to_all | solution.py:356
  104.4 6.1 %all-to-all-start.2 = ((bf16[16,8,1536]{2,1,0:T(8,128)(2,1)}), bf16[16,8,1536]{2,1,0:T(8,128)(2,1)S(1)}, u32[]{:S(2)}, u32[]{:S(2)}) async-start(bf16[16,8,1536]{2,1,0:T(8,128)(2,1)} %bitcast.11), calls=%async_computation.2 | async-start | bytes 786432 | tf_op jit(solution)/shard_map/all_to_all | solution.py:363
  110.6 8.8 %all-gather.3 = f32[96,128]{1,0:T(8,128)S(1)} all-gather(f32[48,128]{1,0:T(8,128)S(1)} %shard_map.122), channel_id=5, replica_groups=mesh['yh'=2,'z'=16,'tp'=16] {'yh'}, dimensions={0}, use_global_device_ids=true | all-gather | bytes 73728 | tf_op jit(solution)/shard_map/all_gather | solution.py:361
  119.4 0.7 shard_map.123
  120.1 0.0 all-to-all-done.2.parts_ref
  120.1 7.8 %all-to-all-start.3 = ((bf16[16,48,128]{2,1,0:T(8,128)(2,1)}), bf16[16,48,128]{2,1,0:T(8,128)(2,1)S(1)}, u32[]{:S(2)}, u32[]{:S(2)}) async-start(bf16[16,48,128]{2,1,0:T(8,128)(2,1)} %shard_map.123), calls=%async_computation.3 | async-start | bytes 393216 | tf_op jit(solution)/shard_map/all_to_all | solution.py:365
  127.9 3.1 %shard_map.125 = (f32[208,128]{1,0:T(8,128)S(1)}, bf16[208,128]{1,0:T(8,128)(2,1)S(1)}) custom-call(s32[5]{0:T(128)S(1)} %stack.15.place_ref, bf16[16,224,128]{2,1,0:T(8,128)(2,1)S(1)} %bitcast.17, bf16[16,144,128]{2,1,0:T(8,128)(2,1)S(1)} %all-to-all-done.1.packs_ref, bf16[192,128]{1,0:T(8,128)(2,1)S(1)} %pad_maximum_fusion.own_ref, ...), custom_call_target="tpu_custom_call" | custom-call | flops 536870912 | bytes 1048576 | tf_op jit(solution)/shard_map/pallas_call | solution.py:368
  131.0 2.5 %collective-permute-start.2 = (bf16[208,128]{1,0:T(8,128)(2,1)S(1)}, bf16[208,128]{1,0:T(8,128)(2,1)S(1)}, u32[]{:S(2)}, u32[]{:S(2)}) collective-permute-start(bf16[208,128]{1,0:T(8,128)(2,1)S(1)} %get-tuple-element.54), channel_id=1, source_target_pairs={{0,256},{256,0},{1,257},{257,1},{2,258},{258,2},{3,259},{259,3},{4... | collective-permute-start | bytes 159752 | tf_op jit(solution)/shard_map/ppermute | solution.py:371
  133.6 5.0 %collective-permute-done.2.got_ref = bf16[208,128]{1,0:T(8,128)(2,1)S(1)} collective-permute-done((bf16[208,128]{1,0:T(8,128)(2,1)S(1)}, bf16[208,128]{1,0:T(8,128)(2,1)S(1)}, u32[]{:S(2)}, u32[]{:S(2)}) %collective-permute-start.2) | collective-permute-done | bytes 53280 | tf_op jit(solution)/shard_map/ppermute | solution.py:371
  138.5 0.7 shard_map.126
  139.2 0.7 shard_map.124
  139.9 4.2 %all-to-all-done.3 = bf16[16,48,128]{2,1,0:T(8,128)(2,1)S(1)} async-done(((bf16[16,48,128]{2,1,0:T(8,128)(2,1)}), bf16[16,48,128]{2,1,0:T(8,128)(2,1)S(1)}, u32[]{:S(2)}, u32[]{:S(2)}) %all-to-all-start.3) | async-done | bytes 196640 | tf_op jit(solution)/shard_map/all_to_all | solution.py:365
  144.1 0.8 shard_map.127
  (7 shorter events, 0.1 us)
Async XLA Ops:
  0.6 7.8 %collective-permute-start = (bf16[8,1536]{1,0:T(8,128)(2,1)}, bf16[8,1536]{1,0:T(8,128)(2,1)S(1)}, u32[]{:S(2)}, u32[]{:S(2)}) collective-permute-start(bf16[8,1536]{1,0:T(8,128)(2,1)} %param.13), channel_id=1, source_target_pairs={{14,16},{16,14},{15,17},{17,15},{30,32},{32,30},{31,33},{33,31},{4... | collective-permute-start | bytes 73736 | tf_op jit(solution)/shard_map/ppermute | solution.py:319
  2.1 6.4 %copy-start.1 = (bf16[8,1536]{1,0:T(8,128)(2,1)S(1)}, bf16[8,1536]{1,0:T(8,128)(2,1)}, u32[]{:S(2)}) copy-start(bf16[8,1536]{1,0:T(8,128)(2,1)} %param.13) | copy-start | bytes 73732
  9.4 17.2 %copy-start.2 = (f32[32,64]{1,0:T(8,128)S(1)}, f32[32,64]{1,0:T(8,128)}, u32[]{:S(2)}) copy-start(f32[32,64]{1,0:T(8,128)} %param.11) | copy-start | bytes 24580
  9.4 51.7 %all-to-all-start = ((bf16[16,16,1536]{2,1,0:T(8,128)(2,1)}), bf16[16,16,1536]{2,1,0:T(8,128)(2,1)S(1)}, u32[]{:S(2)}, u32[]{:S(2)}) async-start(bf16[16,16,1536]{2,1,0:T(8,128)(2,1)} %broadcast_in_dim.2), calls=%async_computation | async-start | bytes 1572864 | tf_op jit(solution)/shard_map/all_to_all | solution.py:330
  69.9 0.9 copy-start
  74.9 29.5 %all-to-all-start.1 = ((bf16[16,144,128]{2,1,0:T(8,128)(2,1)}), bf16[16,144,128]{2,1,0:T(8,128)(2,1)S(1)}, u32[]{:S(2)}, u32[]{:S(2)}) async-start(bf16[16,144,128]{2,1,0:T(8,128)(2,1)} %get-tuple-element.46), calls=%async_computation.1 | async-start | bytes 1179648 | tf_op jit(solution)/shard_map/all_to_all | solution.py:356
  81.7 7.2 %collective-permute-start.1 = (bf16[96,128]{1,0:T(8,128)(2,1)S(1)}, bf16[96,128]{1,0:T(8,128)(2,1)S(1)}, u32[]{:S(2)}, u32[]{:S(2)}) collective-permute-start(bf16[96,128]{1,0:T(8,128)(2,1)S(1)} %get-tuple-element.47.pack_own_ref), channel_id=1, source_target_pairs={{0,256},{256,0},{1,257},{257,1},{2,258},{258,2},{3,259},{259,3},{4... | collective-permute-start | bytes 73736 | tf_op jit(solution)/shard_map/ppermute | solution.py:357
  104.4 15.7 %all-to-all-start.2 = ((bf16[16,8,1536]{2,1,0:T(8,128)(2,1)}), bf16[16,8,1536]{2,1,0:T(8,128)(2,1)S(1)}, u32[]{:S(2)}, u32[]{:S(2)}) async-start(bf16[16,8,1536]{2,1,0:T(8,128)(2,1)} %bitcast.11), calls=%async_computation.2 | async-start | bytes 786432 | tf_op jit(solution)/shard_map/all_to_all | solution.py:363
  120.1 23.9 %all-to-all-start.3 = ((bf16[16,48,128]{2,1,0:T(8,128)(2,1)}), bf16[16,48,128]{2,1,0:T(8,128)(2,1)S(1)}, u32[]{:S(2)}, u32[]{:S(2)}) async-start(bf16[16,48,128]{2,1,0:T(8,128)(2,1)} %shard_map.123), calls=%async_computation.3 | async-start | bytes 393216 | tf_op jit(solution)/shard_map/all_to_all | solution.py:365
  131.0 7.5 %collective-permute-start.2 = (bf16[208,128]{1,0:T(8,128)(2,1)S(1)}, bf16[208,128]{1,0:T(8,128)(2,1)S(1)}, u32[]{:S(2)}, u32[]{:S(2)}) collective-permute-start(bf16[208,128]{1,0:T(8,128)(2,1)S(1)} %get-tuple-element.54), channel_id=1, source_target_pairs={{0,256},{256,0},{1,257},{257,1},{2,258},{258,2},{3,259},{259,3},{4... | collective-permute-start | bytes 159752 | tf_op jit(solution)/shard_map/ppermute | solution.py:371

commit v6 on v5

--- a/solution.py
+++ b/solution.py
@@ -42,11 +42,12 @@
     return high, mid, rest - mid
 
 
-def call(kernel, out_shapes, flops, scratch=(), scalars=0):
+def call(kernel, out_shapes, flops, scratch=(), scalars=0, remote=0):
     specs = {}
     if scalars:
         count = kernel.__code__.co_argcount - len(scratch) - len(jax.tree.leaves(out_shapes))
-        specs["in_specs"] = [pl.BlockSpec(memory_space=pltpu.SMEM)] + [pl.BlockSpec(memory_space=pltpu.VMEM)] * (count - 1)
+        spaces = [pltpu.SMEM] + [pl.ANY] * remote + [pltpu.VMEM] * (count - 1 - remote)
+        specs["in_specs"] = [pl.BlockSpec(memory_space=space) for space in spaces]
     return pl.pallas_call(
         kernel,
         out_shape=out_shapes,
@@ -84,16 +85,17 @@
     pack_ref[192:224] = edge.astype(BF16)
 
 
-def lay_grads(shared_ref, grad_ref, low_ref, high_ref):
-    lanes = shared_ref.shape[0]
-    for i in range(lanes // 2):
+def lay_grads(shared_ref):
+    rows = []
+    for i in range(shared_ref.shape[0] // 2):
         even = shared_ref[2 * i].astype(F32)
         odd = shared_ref[2 * i + 1].astype(F32)
-        grad_ref[16 * i : 16 * i + 16] = jnp.concatenate([even[0:8], odd[0:8]], axis=0).astype(BF16)
+        rows.append(jnp.concatenate([even[0:8], odd[0:8]], axis=0).astype(BF16))
+        rim = jnp.concatenate([even[8:16], odd[8:16]], axis=0).astype(BF16)
         if i == 0:
-            low_ref[...] = jnp.concatenate([even[8:16], odd[8:16]], axis=0).astype(BF16)
-        if i == lanes // 2 - 1:
-            high_ref[...] = jnp.concatenate([even[8:16], odd[8:16]], axis=0).astype(BF16)
+            low = rim
+    gap = jnp.zeros((128 - 2 * RIM, shared_ref.shape[2]), BF16)
+    return jnp.concatenate(rows, axis=0), jnp.concatenate([rim, gap, low], axis=0)
 
 
 def attend(place_ref, all_ref, own_ref, pair_ref, mine_ref, other_ref, score_ref):
@@ -153,7 +155,9 @@
     return pltpu.roll(ring, (-offset) % ring.shape[1], 1)
 
 
-def middle_part(place_ref, mine_ref, got_ref, taps_ref, weight_ref, grad_ref, low_ref, high_ref, partial_ref, pack_ref, copies_ref):
+def middle_part(place_ref, weight_hbm, mine_ref, got_ref, taps_ref, shared_ref, keep_ref, send_ref, pack_ref, copies_ref, weight_ref, sem):
+    fetch = pltpu.make_async_copy(weight_hbm, weight_ref, sem)
+    fetch.start()
     width = 128
     ring = 2 * width
     start = place_ref[1]
@@ -177,13 +181,17 @@
         depth = depth + taps[:, t : t + 1] * shifted(masked, t - RIM)
     gate = jax.nn.sigmoid(depth)
     swish = (depth[:, :width] * gate[:, :width]).astype(BF16)
-    grad = grad_ref[...]
+    grad, side = lay_grads(shared_ref)
     mix = dot10(swish, grad)
     mix = jnp.concatenate([mix[:, at : at + width] for at in range(0, mix.shape[1], width)], axis=0).astype(BF16)
+    fetch.wait()
     weight = weight_ref[...]
-    partial_ref[...] = dot00(swish, weight).astype(BF16)
-    gap = jnp.zeros((width - 2 * RIM, grad.shape[1]), BF16)
-    side = jnp.concatenate([high_ref[...], gap, low_ref[...]], axis=0)
+    partial = dot00(swish, weight)
+    core = place_ref[5] == 0
+    even = jnp.concatenate([partial[at : at + 8] for at in range(0, width, 16)], axis=0)
+    odd = jnp.concatenate([partial[at + 8 : at + 16] for at in range(0, width, 16)], axis=0)
+    keep_ref[...] = jnp.where(core, even, odd).astype(BF16)
+    send_ref[...] = jnp.where(core, odd, even).astype(BF16)
     back = jnp.concatenate([dot11(weight, grad), dot11(weight, side)], axis=1)
     dgrad = back * gate * (1.0 + depth * (1.0 - gate))
     dgrad = jnp.where(inside, dgrad, 0.0).astype(BF16).astype(F32)
@@ -195,18 +203,19 @@
         sums = jnp.where(row == t, column, sums)
         total = total + taps[:, t : t + 1] * shifted(dgrad, RIM - t)[:, :width]
     turned = sums.T
-    tap_grad = jnp.concatenate([turned[0:16, 0:64], turned[16:32, 0:64]], axis=1).astype(BF16)
+    tap_grad = jnp.concatenate([turned[0:16, 0:64], turned[16:32, 0:64]], axis=1)
     grad_out = jnp.where(live[:, :width], total, 0.0).astype(BF16)
     delta = jnp.sum(grad_out.astype(F32) * attn[:, :width], axis=0, keepdims=True)
     a, b, c = split3(-lse[:, :width])
     d, e, f = split3(-delta)
     stats = rows_of(16, width, [(0, a), (1, b), (2, c), (3, d), (4, e), (5, f), (6, 1.0)])
-    pack = jnp.concatenate([grad_out, stats.astype(BF16), tap_grad], axis=0)
-    pack_ref[...] = pack
-    share = copies_ref.shape[1] - 96
+    pack_ref[...] = jnp.concatenate([grad_out, stats.astype(BF16)], axis=0)
+    row = lax.broadcasted_iota(jnp.int32, stats.shape, 0)
+    share = copies_ref.shape[1] - 80
     for j in range(copies_ref.shape[0]):
-        copies_ref[j, 0:96] = pack
-        copies_ref[j, 96:] = mix[j * share : (j + 1) * share]
+        copies_ref[j, 0:64] = grad_out
+        copies_ref[j, 64:80] = jnp.where(row == 7, tap_grad[j : j + 1], stats).astype(BF16)
+        copies_ref[j, 80:] = mix[j * share : (j + 1) * share]
 
 
 def backward(place_ref, all_ref, packs_ref, own_ref, pair_ref, pack_own_ref, pack_pair_ref, mine_ref, other_ref):
@@ -229,7 +238,6 @@
     d_query = jnp.zeros((head, 2 * width), F32)
     d_key = jnp.zeros((head, 2 * width), F32)
     d_value = jnp.zeros((head, 2 * width), F32)
-    tap_sum = jnp.zeros((16, width), F32)
     for first in range(0, blocks, 2):
         keys, queries, grads, query_scores, key_scores, weights = [], [], [], [], [], []
         for b in (first, first + 1):
@@ -246,7 +254,6 @@
             weights.append(weight.astype(BF16))
             queries.append(query_b)
             grads.append(packs_ref[b, 0:head])
-            tap_sum = tap_sum + packs_ref[b, 80:96].astype(F32)
         d_query = d_query + dot10(jnp.concatenate(keys, axis=1), jnp.concatenate(query_scores, axis=0))
         d_key = d_key + dot10(jnp.concatenate(queries, axis=1), jnp.concatenate(key_scores, axis=0))
         d_value = d_value + dot10(jnp.concatenate(grads, axis=1), jnp.concatenate(weights, axis=0))
@@ -256,24 +263,28 @@
         ref[0:head] = d_query[:, at : at + width].astype(kind)
         ref[head : 2 * head] = d_key[:, at : at + width].astype(kind)
         ref[2 * head : 3 * head] = d_value[:, at : at + width].astype(kind)
-        ref[3 * head : 3 * head + 16] = tap_sum.astype(kind)
-
-
-def finish(norm, mine_ref, got_ref, query_ref, key_ref, value_ref, taps_ref):
+
+
+def finish(mine_ref, got_ref, query_ref, key_ref, value_ref):
     total = mine_ref[...] + got_ref[...].astype(F32)
     query_ref[...] = total[0:64].astype(BF16)
     key_ref[...] = total[64:128].astype(BF16)
     value_ref[...] = total[128:192].astype(BF16)
-    tap = total[192:208] * norm
-    taps_ref[0:16] = tap[:, 0:64]
-    taps_ref[16:32] = tap[:, 64:128]
+
+
+def add_pair(mine_ref, got_ref, out_ref):
+    out_ref[...] = (mine_ref[...].astype(F32) + got_ref[...].astype(F32)).astype(BF16)
 
 
 def mix_sum(packs_ref, out_ref):
-    total = jnp.zeros(out_ref.shape, F32)
+    share = packs_ref.shape[1] - 80
+    total = jnp.zeros((share, 128), F32)
+    stats = jnp.zeros((16, 128), F32)
     for j in range(packs_ref.shape[0]):
-        total = total + packs_ref[j, 96:].astype(F32)
-    out_ref[...] = total
+        total = total + packs_ref[j, 80:].astype(F32)
+        stats = stats + packs_ref[j, 64:80].astype(F32)
+    out_ref[0:share] = total
+    out_ref[share:] = rows_of(out_ref.shape[0] - share, 128, [(0, stats[7:8])])
 
 
 def mix_spread(both_ref, out_ref):
@@ -282,9 +293,14 @@
         out_ref[j] = total
 
 
-def mix_place(norm, parts_ref, out_ref):
-    for piece in range(parts_ref.shape[0]):
-        out_ref[:, piece * 128 : (piece + 1) * 128] = parts_ref[piece].astype(F32) * norm
+def mix_place(norm, share, parts_ref, out_ref, taps_ref):
+    pieces = [parts_ref[z].astype(F32) * norm for z in range(parts_ref.shape[0])]
+    full = jnp.concatenate([piece[0:share] for piece in pieces], axis=0)
+    for at in range(out_ref.shape[1] // 128):
+        out_ref[:, at * 128 : (at + 1) * 128] = full[at * 64 : (at + 1) * 64]
+    tap = rows_of(len(pieces), 128, [(z, piece[share : share + 1]) for z, piece in enumerate(pieces)])
+    taps_ref[0:16] = tap[:, 0:64]
+    taps_ref[16:32] = tap[:, 64:128]
 
 
 def sum_blocks(parts_ref, out_ref):
@@ -298,15 +314,16 @@
     width, head = query_rows.shape
     depth = lax.axis_size("z")
     ctx = ("yh", "z")
+    tp = ("chip", "core")
     devices = 2 * depth
-    lanes = lax.axis_size("tp")
+    lanes = lax.axis_size(tp)
     model = mix_weight.shape[1]
     rows8 = out_grad.shape[0]
     norm = (width * devices) ** -0.5
     valid = valid_frames[0]
     half = lax.axis_index("yh")
     spot = lax.axis_index("z")
-    place = jnp.stack([spot, (half * depth + spot) * width, valid, jnp.int32(width * devices), half]).astype(jnp.int32)
+    place = jnp.stack([spot, (half * depth + spot) * width, valid, jnp.int32(width * devices), half, lax.axis_index("core")]).astype(jnp.int32)
     swap = [(0, 1), (1, 0)]
     taps = depth_kernel.T
     rim_pairs = []
@@ -316,7 +333,7 @@
             rim_pairs.append((i * lanes + lanes - sides + k, (i + 1) * lanes + k))
             rim_pairs.append(((i + 1) * lanes + k, i * lanes + lanes - sides + k))
 
-    rim_rows = lax.ppermute(out_grad, ("yh", "z", "tp"), rim_pairs)
+    rim_rows = lax.ppermute(out_grad, ctx + tp, rim_pairs)
     own = jnp.concatenate([query_rows.T, key_rows.T, value_rows.T], axis=0)
     both = lax.all_gather(own, "yh", axis=0)
     rim_rows, both = lax.optimization_barrier((rim_rows, both))
@@ -327,7 +344,7 @@
         scalars=1,
     )(place, both)
     with_rim = jnp.concatenate([out_grad, rim_rows], axis=0)
-    shared = lax.all_to_all(jnp.broadcast_to(with_rim[None], (lanes,) + with_rim.shape), "tp", 0, 0, tiled=True)
+    shared = lax.all_to_all(jnp.broadcast_to(with_rim[None], (lanes,) + with_rim.shape), tp, 0, 0, tiled=True)
     everyone = lax.all_gather(front, "z", axis=0)
     shared, everyone = lax.optimization_barrier((shared, everyone))
 
@@ -338,70 +355,75 @@
     )(place, everyone, own, pair)
     shared, other = lax.optimization_barrier((shared, other))
     got = lax.all_gather(other, "yh", axis=0)
-    rim_shape = jax.ShapeDtypeStruct((RIM, model), BF16)
-    grad_block, grad_low, grad_high = call(
-        lay_grads, (jax.ShapeDtypeStruct((width, model), BF16), rim_shape, rim_shape), 2 ** 22
-    )(shared)
     share = head * model // width // depth
-    partial, pack, copies = call(
+    half_rows = jax.ShapeDtypeStruct((width // 2, model), BF16)
+    keep, send, pack, copies = call(
         middle_part,
         (
-            jax.ShapeDtypeStruct((width, model), BF16),
-            jax.ShapeDtypeStruct((96, width), BF16),
-            jax.ShapeDtypeStruct((depth, 96 + share, width), BF16),
+            half_rows,
+            half_rows,
+            jax.ShapeDtypeStruct((80, width), BF16),
+            jax.ShapeDtypeStruct((depth, 80 + share, width), BF16),
         ),
         2 ** 27,
+        [pltpu.VMEM(mix_weight.shape, BF16), pltpu.SemaphoreType.DMA],
         scalars=1,
-    )(place, mine, got, taps, mix_weight, grad_block, grad_low, grad_high)
+        remote=1,
+    )(place, mix_weight, mine, got, taps, shared)
     packs = lax.all_to_all(copies, "z", 0, 0, tiled=True)
+    keep_got = lax.ppermute(send, "core", swap)
+    partial = call(add_pair, half_rows, 2 ** 20)(keep, keep_got)
     pack_pair = lax.ppermute(pack, "yh", swap)
     packs, pack_pair, partial = lax.optimization_barrier((packs, pack_pair, partial))
 
-    mix_mine = call(mix_sum, jax.ShapeDtypeStruct((share, width), F32), 2 ** 22)(packs)
+    mix_mine = call(mix_sum, jax.ShapeDtypeStruct((share + 16, width), F32), 2 ** 22)(packs)
     mix_both = lax.all_gather(mix_mine, "yh", axis=0)
-    spread = call(mix_spread, jax.ShapeDtypeStruct((depth, share, width), BF16), 2 ** 20)(mix_both)
-    block_parts = lax.all_to_all(partial.reshape(lanes, rows8, model), "tp", 0, 0, tiled=True)
+    spread = call(mix_spread, jax.ShapeDtypeStruct((depth, share + 16, width), BF16), 2 ** 20)(mix_both)
+    block_parts = lax.all_to_all(partial.reshape(lanes // 2, rows8, model), "chip", 0, 0, tiled=True)
     spread, block_parts = lax.optimization_barrier((spread, block_parts))
-    pieces = lax.all_to_all(spread, "z", 0, 0, tiled=True).reshape(model // width, head, width)
-    result = jax.ShapeDtypeStruct((3 * head + 16, width), F32)
+    pieces = lax.all_to_all(spread, "z", 0, 0, tiled=True)
+    result = jax.ShapeDtypeStruct((3 * head, width), F32)
     sent = jax.ShapeDtypeStruct(result.shape, BF16)
     mine, other = call(backward, (result, sent), 2 ** 29, scalars=1)(
         place, everyone, packs, own, pair, pack, pack_pair
     )
     got = lax.ppermute(other, "yh", swap)
-    d_query, d_key, d_value, tap_total = call(
-        functools.partial(finish, norm), (block, block, block, jax.ShapeDtypeStruct((KSIZE, head), F32)), 2 ** 20
-    )(mine, got)
+    d_query, d_key, d_value = call(finish, (block, block, block), 2 ** 20)(mine, got)
 
     block_out = call(sum_blocks, jax.ShapeDtypeStruct((rows8, model), BF16), 2 ** 20)(block_parts)
-    mix_grad = call(functools.partial(mix_place, norm), jax.ShapeDtypeStruct((head, model), F32), 2 ** 20)(pieces)
+    mix_grad, tap_total = call(
+        functools.partial(mix_place, norm, share),
+        (jax.ShapeDtypeStruct((head, model), F32), jax.ShapeDtypeStruct((KSIZE, head), F32)),
+        2 ** 20,
+    )(pieces)
     return block_out, d_query.T, d_key.T, d_value.T, mix_grad, tap_total
 
 
 def solution(mesh):
     count = mesh.shape["ctx"]
-    fine = Mesh(mesh.devices.reshape(2, count // 2, mesh.shape["tp"]), ("yh", "z", "tp"))
+    fine = Mesh(mesh.devices.reshape(2, count // 2, mesh.shape["tp"] // 2, 2), ("yh", "z", "chip", "core"))
     ctx = ("yh", "z")
-    every = ("yh", "z", "tp")
+    tp = ("chip", "core")
+    every = ctx + tp
     return jax.shard_map(
         body,
         mesh=fine,
         in_specs=(
-            P(ctx, "tp"),
-            P(ctx, "tp"),
-            P(ctx, "tp"),
+            P(ctx, tp),
+            P(ctx, tp),
+            P(ctx, tp),
             P(),
-            P(None, "tp"),
-            P("tp", None),
+            P(None, tp),
+            P(tp, None),
             P(every, None),
         ),
         out_specs=(
             P(every, None),
-            P(ctx, "tp"),
-            P(ctx, "tp"),
-            P(ctx, "tp"),
-            P("tp", None),
-            P(None, "tp"),
+            P(ctx, tp),
+            P(ctx, tp),
+            P(ctx, tp),
+            P(tp, None),
+            P(None, tp),
         ),
         check_vma=False,
     )

time: 146 us -> 138 us (0.945)
  the two profiles are of different devices: /device:TPU:4 before, /device:TPU:34 now
where the time goes in v6:
time: 138 us
  blocking collectives  59.1 us (43%)
  starting transfers between devices  42.2 us (31%)
  waiting for transfers between devices  19.2 us (14%)
  Pallas kernels  13.9 us (10%)
  between operations  1.39 us (1%)
    all_gather x1, blocking collectives, body(): everyone = lax.all_gather(front, 'z', axis=0)  39.6 us
    all_to_all x1, waiting for transfers between devices, body(): packs = lax.all_to_all(copies, 'z', 0, 0, tiled=True)  11.8 us
    all_to_all x1, starting transfers between devices, body(): packs = lax.all_to_all(copies, 'z', 0, 0, tiled=True)  8.61 us
    all_to_all x1, starting transfers between devices, body(): lax.all_to_all(jnp.broadcast_to(with_rim[None], (lanes,) + with_rim.shape...  8.56 us
    all_to_all x1, starting transfers between devices, body(): pieces = lax.all_to_all(spread, 'z', 0, 0, tiled=True)  6.94 us
    all_gather x1, blocking collectives, body(): got = lax.all_gather(other, 'yh', axis=0)  6.67 us
    all_gather x1, blocking collectives, body(): both = lax.all_gather(own, 'yh', axis=0)  6.39 us
    all_gather x1, blocking collectives, body(): mix_both = lax.all_gather(mix_mine, 'yh', axis=0)  6.36 us
  transfers between devices with their start and end apart: 8, of which 4 were waited for; matrix products, arithmetic and copies ran while one was open for 1% of the time, Pallas kernels for 5%

profile of v6, /device:TPU:34, one launch (start us, length us, event | category | flops | bytes accessed | tf_op | source)
XLA Modules:
  0.0 137.6 jit_solution(14349462057681566170)
XLA Ops:
  0.6 0.7 collective-permute-start
  1.3 0.8 pad_maximum_fusion.own_ref
  2.1 6.4 %all-gather = bf16[384,128]{1,0:T(8,128)(2,1)S(1)} all-gather(bf16[192,128]{1,0:T(8,128)(2,1)S(1)} %pad_maximum_fusion.own_ref), channel_id=2, replica_groups=mesh['yh'=2,'z'=16,'chip'=8,'core'=2] {'yh'}, dimensions={0}, use_global_device_ids=true | all-gather | bytes 147456 | tf_op jit(solution)/shard_map/all_gather | solution.py:338
  8.5 1.0 broadcast_in_dim.2
  9.4 8.6 %all-to-all-start = ((bf16[16,16,1536]{2,1,0:T(8,128)(2,1)}), bf16[16,16,1536]{2,1,0:T(8,128)(2,1)S(1)}, u32[]{:S(2)}, u32[]{:S(2)}) async-start(bf16[16,16,1536]{2,1,0:T(8,128)(2,1)} %broadcast_in_dim.2), calls=%async_computation | async-start | bytes 1572864 | tf_op jit(solution)/shard_map/all_to_all | solution.py:347
  18.7 0.0 copy-done.2
  18.7 0.1 copy.13
  18.8 0.1 stack.19.place_ref
  18.9 0.7 shard_map.118
  19.6 39.6 %all-gather.1 = bf16[3584,128]{1,0:T(8,128)(2,1)S(1)} all-gather(bf16[224,128]{1,0:T(8,128)(2,1)S(1)} %get-tuple-element.34), channel_id=3, replica_groups=mesh['yh'=2,'z'=16,'chip'=8,'core'=2] {'z'}, dimensions={0}, use_global_device_ids=true | all-gather | bytes 974848 | tf_op jit(solution)/shard_map/all_gather | solution.py:348
  59.2 0.0 all-to-all-done.shared_ref
  59.2 2.2 %shard_map.119 = (f32[72,256]{1,0:T(8,128)S(1)}, f32[72,256]{1,0:T(8,128)S(1)}) custom-call(s32[6]{0:T(128)S(1)} %stack.19.place_ref, bf16[16,224,128]{2,1,0:T(8,128)(2,1)S(1)} %bitcast.16, bf16[192,128]{1,0:T(8,128)(2,1)S(1)} %pad_maximum_fusion.own_ref, bf16[192,128]{1,0:T(8,128)(2,1)S(1)} %get-tuple-element.36.pair_ref), custom_call_target="tpu_custom_call" | custom-call | flops 268435456 | bytes 1048576 | tf_op jit(solution)/shard_map/pallas_call | solution.py:353
  61.4 0.0 copy-start
  61.5 6.7 %all-gather.2 = f32[144,256]{1,0:T(8,128)S(1)} all-gather(f32[72,256]{1,0:T(8,128)S(1)} %get-tuple-element.40), channel_id=4, replica_groups=mesh['yh'=2,'z'=16,'chip'=8,'core'=2] {'yh'}, dimensions={0}, use_global_device_ids=true | all-gather | bytes 221184 | tf_op jit(solution)/shard_map/all_gather | solution.py:357
  68.1 4.4 %shard_map.120 = (bf16[64,1536]{1,0:T(8,128)(2,1)S(1)}, bf16[64,1536]{1,0:T(8,128)(2,1)S(1)}, bf16[80,128]{1,0:T(8,128)(2,1)S(1)}, bf16[16,128,128]{2,1,0:T(8,128)(2,1)}) custom-call(s32[6]{0:T(128)S(1)} %stack.19.place_ref, bf16[64,1536]{1,0:T(8,128)(2,1)S(1)} %copy-done, f32[72,256]{1,0:T(8,128)S(1)} %get-tuple-element.37.mine_ref, ...), custom_call_target="tpu_custom_call" | custom-call | flops 134217728 | bytes 1048576 | tf_op jit(solution)/shard_map/pallas_call | solution.py:360
  72.5 8.6 %all-to-all-start.1 = ((bf16[16,128,128]{2,1,0:T(8,128)(2,1)}), bf16[16,128,128]{2,1,0:T(8,128)(2,1)S(1)}, u32[]{:S(2)}, u32[]{:S(2)}) async-start(bf16[16,128,128]{2,1,0:T(8,128)(2,1)} %get-tuple-element.42), calls=%async_computation.1 | async-start | bytes 1048576 | tf_op jit(solution)/shard_map/all_to_all | solution.py:373
  81.1 1.9 %collective-permute-start.2 = (bf16[64,1536]{1,0:T(8,128)(2,1)S(1)}, bf16[64,1536]{1,0:T(8,128)(2,1)S(1)}, u32[]{:S(2)}, u32[]{:S(2)}) collective-permute-start(bf16[64,1536]{1,0:T(8,128)(2,1)S(1)} %get-tuple-element.45), channel_id=1, source_target_pairs={{0,1},{1,0},{2,3},{3,2},{4,5},{5,4},{6,7},{7,6},{8,9},{9,8},{10,11... | collective-permute-start | bytes 589832 | tf_op jit(solution)/shard_map/ppermute | solution.py:374
  83.0 4.8 %collective-permute-start.1 = (bf16[80,128]{1,0:T(8,128)(2,1)S(1)}, bf16[80,128]{1,0:T(8,128)(2,1)S(1)}, u32[]{:S(2)}, u32[]{:S(2)}) collective-permute-start(bf16[80,128]{1,0:T(8,128)(2,1)S(1)} %get-tuple-element.43.pack_own_ref), channel_id=1, source_target_pairs={{0,256},{256,0},{1,257},{257,1},{2,258},{258,2},{3,259},{259,3},{4... | collective-permute-start | bytes 61448 | tf_op jit(solution)/shard_map/ppermute | solution.py:376
  87.8 0.7 shard_map.121
  88.6 1.6 %collective-permute-done.1.pack_pair_ref = bf16[80,128]{1,0:T(8,128)(2,1)S(1)} collective-permute-done((bf16[80,128]{1,0:T(8,128)(2,1)S(1)}, bf16[80,128]{1,0:T(8,128)(2,1)S(1)}, u32[]{:S(2)}, u32[]{:S(2)}) %collective-permute-start.1) | collective-permute-done | bytes 20512 | tf_op jit(solution)/shard_map/ppermute | solution.py:376
  90.2 11.8 %all-to-all-done.1.packs_ref = bf16[16,128,128]{2,1,0:T(8,128)(2,1)S(1)} async-done(((bf16[16,128,128]{2,1,0:T(8,128)(2,1)}), bf16[16,128,128]{2,1,0:T(8,128)(2,1)S(1)}, u32[]{:S(2)}, u32[]{:S(2)}) %all-to-all-start.1) | async-done | bytes 524320 | tf_op jit(solution)/shard_map/all_to_all | solution.py:373
  102.0 6.1 %all-to-all-start.2 = ((bf16[8,8,1536]{2,1,0:T(8,128)(2,1)}), bf16[8,8,1536]{2,1,0:T(8,128)(2,1)S(1)}, u32[]{:S(2)}, u32[]{:S(2)}) async-start(bf16[8,8,1536]{2,1,0:T(8,128)(2,1)} %bitcast.12), calls=%async_computation.2 | async-start | bytes 393216 | tf_op jit(solution)/shard_map/all_to_all | solution.py:382
  108.1 6.4 %all-gather.3 = f32[128,128]{1,0:T(8,128)S(1)} all-gather(f32[64,128]{1,0:T(8,128)S(1)} %shard_map.122), channel_id=5, replica_groups=mesh['yh'=2,'z'=16,'chip'=8,'core'=2] {'yh'}, dimensions={0}, use_global_device_ids=true | all-gather | bytes 98304 | tf_op jit(solution)/shard_map/all_gather | solution.py:380
  114.5 0.7 shard_map.123
  115.2 6.9 %all-to-all-start.3 = ((bf16[16,64,128]{2,1,0:T(8,128)(2,1)}), bf16[16,64,128]{2,1,0:T(8,128)(2,1)S(1)}, u32[]{:S(2)}, u32[]{:S(2)}) async-start(bf16[16,64,128]{2,1,0:T(8,128)(2,1)} %shard_map.123), calls=%async_computation.3 | async-start | bytes 524288 | tf_op jit(solution)/shard_map/all_to_all | solution.py:384
  122.1 3.0 %shard_map.125 = (f32[192,128]{1,0:T(8,128)S(1)}, bf16[192,128]{1,0:T(8,128)(2,1)S(1)}) custom-call(s32[6]{0:T(128)S(1)} %stack.19.place_ref, bf16[16,224,128]{2,1,0:T(8,128)(2,1)S(1)} %bitcast.17, bf16[16,128,128]{2,1,0:T(8,128)(2,1)S(1)} %all-to-all-done.1.packs_ref, bf16[192,128]{1,0:T(8,128)(2,1)S(1)} %pad_maximum_fusion.own_ref, ...), custom_call_target="tpu_custom_call" | custom-call | flops 536870912 | bytes 1048576 | tf_op jit(solution)/shard_map/pallas_call | solution.py:387
  125.2 4.6 %collective-permute-start.3 = (bf16[192,128]{1,0:T(8,128)(2,1)S(1)}, bf16[192,128]{1,0:T(8,128)(2,1)S(1)}, u32[]{:S(2)}, u32[]{:S(2)}) collective-permute-start(bf16[192,128]{1,0:T(8,128)(2,1)S(1)} %get-tuple-element.51), channel_id=1, source_target_pairs={{0,256},{256,0},{1,257},{257,1},{2,258},{258,2},{3,259},{259,3},{4... | collective-permute-start | bytes 147464 | tf_op jit(solution)/shard_map/ppermute | solution.py:390
  129.8 2.9 %collective-permute-done.3.got_ref = bf16[192,128]{1,0:T(8,128)(2,1)S(1)} collective-permute-done((bf16[192,128]{1,0:T(8,128)(2,1)S(1)}, bf16[192,128]{1,0:T(8,128)(2,1)S(1)}, u32[]{:S(2)}, u32[]{:S(2)}) %collective-permute-start.3) | collective-permute-done | bytes 49184 | tf_op jit(solution)/shard_map/ppermute | solution.py:390
  132.7 0.6 shard_map.126
  133.3 0.6 shard_map.124
  134.0 2.9 %all-to-all-done.3.parts_ref = bf16[16,64,128]{2,1,0:T(8,128)(2,1)S(1)} async-done(((bf16[16,64,128]{2,1,0:T(8,128)(2,1)}), bf16[16,64,128]{2,1,0:T(8,128)(2,1)S(1)}, u32[]{:S(2)}, u32[]{:S(2)}) %all-to-all-start.3) | async-done | bytes 262176 | tf_op jit(solution)/shard_map/all_to_all | solution.py:384
  136.8 0.8 shard_map.127
  (9 shorter events, 0.1 us)
Async XLA Ops:
  0.6 7.8 %collective-permute-start = (bf16[8,1536]{1,0:T(8,128)(2,1)}, bf16[8,1536]{1,0:T(8,128)(2,1)S(1)}, u32[]{:S(2)}, u32[]{:S(2)}) collective-permute-start(bf16[8,1536]{1,0:T(8,128)(2,1)} %param.13), channel_id=1, source_target_pairs={{14,16},{16,14},{15,17},{17,15},{30,32},{32,30},{31,33},{33,31},{4... | collective-permute-start | bytes 73736 | tf_op jit(solution)/shard_map/ppermute | solution.py:336
  2.1 6.4 %copy-start.1 = (bf16[8,1536]{1,0:T(8,128)(2,1)S(1)}, bf16[8,1536]{1,0:T(8,128)(2,1)}, u32[]{:S(2)}) copy-start(bf16[8,1536]{1,0:T(8,128)(2,1)} %param.13) | copy-start | bytes 73732
  9.4 49.8 %all-to-all-start = ((bf16[16,16,1536]{2,1,0:T(8,128)(2,1)}), bf16[16,16,1536]{2,1,0:T(8,128)(2,1)S(1)}, u32[]{:S(2)}, u32[]{:S(2)}) async-start(bf16[16,16,1536]{2,1,0:T(8,128)(2,1)} %broadcast_in_dim.2), calls=%async_computation | async-start | bytes 1572864 | tf_op jit(solution)/shard_map/all_to_all | solution.py:347
  18.0 0.7 copy-start.2
  61.4 6.7 %copy-start = (bf16[64,1536]{1,0:T(8,128)(2,1)S(1)}, bf16[64,1536]{1,0:T(8,128)(2,1)}, u32[]{:S(2)}) copy-start(bf16[64,1536]{1,0:T(8,128)(2,1)} %weight_hbm.1) | copy-start | bytes 589828
  72.5 29.5 %all-to-all-start.1 = ((bf16[16,128,128]{2,1,0:T(8,128)(2,1)}), bf16[16,128,128]{2,1,0:T(8,128)(2,1)S(1)}, u32[]{:S(2)}, u32[]{:S(2)}) async-start(bf16[16,128,128]{2,1,0:T(8,128)(2,1)} %get-tuple-element.42), calls=%async_computation.1 | async-start | bytes 1048576 | tf_op jit(solution)/shard_map/all_to_all | solution.py:373
  81.1 6.7 %collective-permute-start.2 = (bf16[64,1536]{1,0:T(8,128)(2,1)S(1)}, bf16[64,1536]{1,0:T(8,128)(2,1)S(1)}, u32[]{:S(2)}, u32[]{:S(2)}) collective-permute-start(bf16[64,1536]{1,0:T(8,128)(2,1)S(1)} %get-tuple-element.45), channel_id=1, source_target_pairs={{0,1},{1,0},{2,3},{3,2},{4,5},{5,4},{6,7},{7,6},{8,9},{9,8},{10,11... | collective-permute-start | bytes 589832 | tf_op jit(solution)/shard_map/ppermute | solution.py:374
  83.0 7.2 %collective-permute-start.1 = (bf16[80,128]{1,0:T(8,128)(2,1)S(1)}, bf16[80,128]{1,0:T(8,128)(2,1)S(1)}, u32[]{:S(2)}, u32[]{:S(2)}) collective-permute-start(bf16[80,128]{1,0:T(8,128)(2,1)S(1)} %get-tuple-element.43.pack_own_ref), channel_id=1, source_target_pairs={{0,256},{256,0},{1,257},{257,1},{2,258},{258,2},{3,259},{259,3},{4... | collective-permute-start | bytes 61448 | tf_op jit(solution)/shard_map/ppermute | solution.py:376
  102.0 13.3 %all-to-all-start.2 = ((bf16[8,8,1536]{2,1,0:T(8,128)(2,1)}), bf16[8,8,1536]{2,1,0:T(8,128)(2,1)S(1)}, u32[]{:S(2)}, u32[]{:S(2)}) async-start(bf16[8,8,1536]{2,1,0:T(8,128)(2,1)} %bitcast.12), calls=%async_computation.2 | async-start | bytes 393216 | tf_op jit(solution)/shard_map/all_to_all | solution.py:382
  115.2 21.6 %all-to-all-start.3 = ((bf16[16,64,128]{2,1,0:T(8,128)(2,1)}), bf16[16,64,128]{2,1,0:T(8,128)(2,1)S(1)}, u32[]{:S(2)}, u32[]{:S(2)}) async-start(bf16[16,64,128]{2,1,0:T(8,128)(2,1)} %shard_map.123), calls=%async_computation.3 | async-start | bytes 524288 | tf_op jit(solution)/shard_map/all_to_all | solution.py:384
  125.2 7.5 %collective-permute-start.3 = (bf16[192,128]{1,0:T(8,128)(2,1)S(1)}, bf16[192,128]{1,0:T(8,128)(2,1)S(1)}, u32[]{:S(2)}, u32[]{:S(2)}) collective-permute-start(bf16[192,128]{1,0:T(8,128)(2,1)S(1)} %get-tuple-element.51), channel_id=1, source_target_pairs={{0,256},{256,0},{1,257},{257,1},{2,258},{258,2},{3,259},{259,3},{4... | collective-permute-start | bytes 147464 | tf_op jit(solution)/shard_map/ppermute | solution.py:390

commit v7 on v6

--- a/solution.py
+++ b/solution.py
@@ -211,14 +211,44 @@
     stats = rows_of(16, width, [(0, a), (1, b), (2, c), (3, d), (4, e), (5, f), (6, 1.0)])
     pack_ref[...] = jnp.concatenate([grad_out, stats.astype(BF16)], axis=0)
     row = lax.broadcasted_iota(jnp.int32, stats.shape, 0)
-    share = copies_ref.shape[1] - 80
+    share = copies_ref.shape[1] - 72
     for j in range(copies_ref.shape[0]):
         copies_ref[j, 0:64] = grad_out
-        copies_ref[j, 64:80] = jnp.where(row == 7, tap_grad[j : j + 1], stats).astype(BF16)
-        copies_ref[j, 80:] = mix[j * share : (j + 1) * share]
-
-
-def backward(place_ref, all_ref, packs_ref, own_ref, pair_ref, pack_own_ref, pack_pair_ref, mine_ref, other_ref):
+        rest = jnp.where(row == 7, tap_grad[j : j + 1], stats)[0:8]
+        rest = jnp.concatenate([rest, mix[j * share : (j + 1) * share].astype(F32)], axis=0)
+        copies_ref[j, 64:] = rest.astype(BF16)
+
+
+ONES = [(0, 1.0), (1, 1.0), (2, 1.0)]
+DELTAS = [(3, 1.0), (4, 1.0), (5, 1.0)]
+
+
+def query_back(place_ref, all_ref, own_ref, pair_ref, pack_own_ref, pack_pair_ref, out_ref):
+    blocks = all_ref.shape[0]
+    base = place_ref[4] * blocks
+    head = 64
+    width = 128
+    scale = head ** -0.5
+    query = jnp.concatenate([own_ref[0:head], pair_ref[0:head]], axis=1)
+    packs = jnp.concatenate([pack_own_ref[...], pack_pair_ref[...]], axis=1)
+    query = (query.astype(F32) * scale).astype(BF16)
+    query = jnp.concatenate([query, packs[head : head + 16]], axis=0)
+    value_rows = rows_of(16, width, DELTAS).astype(BF16)
+    total = jnp.zeros((head, 2 * width), F32)
+    for first in range(0, blocks, 2):
+        keys, scores = [], []
+        for b in (first, first + 1):
+            key_b = all_ref[b, head : 2 * head]
+            key_rows = rows_of(16, width, ONES + [(6, bias_of(place_ref, b, base))]).astype(BF16)
+            value_aug = jnp.concatenate([all_ref[b, 2 * head : 3 * head], value_rows], axis=0)
+            weight = jnp.exp(dot00(jnp.concatenate([key_b, key_rows], axis=0), query))
+            scores.append((weight * dot00(value_aug, packs)).astype(BF16))
+            keys.append(key_b)
+        total = total + dot10(jnp.concatenate(keys, axis=1), jnp.concatenate(scores, axis=0))
+    out_ref[...] = total * scale
+
+
+def backward(place_ref, all_ref, packs_ref, own_ref, pair_ref, d_query_ref, mine_ref, other_ref):
     blocks = all_ref.shape[0]
     base = place_ref[4] * blocks
     pair_base = blocks - base
@@ -226,47 +256,34 @@
     head = 64
     width = 128
     scale = head ** -0.5
-    both = jnp.concatenate([own_ref[...], pair_ref[...]], axis=1)
-    packs = jnp.concatenate([pack_own_ref[0:80], pack_pair_ref[0:80]], axis=1)
-    query = (both[0:head].astype(F32) * scale).astype(BF16)
-    query = jnp.concatenate([query, packs[head : head + 16]], axis=0)
-    ones = [(0, 1.0), (1, 1.0), (2, 1.0)]
-    key_rows = rows_of(16, 2 * width, ones + [(6, pair_bias)]).astype(BF16)
-    key = jnp.concatenate([both[head : 2 * head], key_rows], axis=0)
-    value_rows = rows_of(16, 2 * width, [(3, 1.0), (4, 1.0), (5, 1.0)]).astype(BF16)
-    value = jnp.concatenate([both[2 * head : 3 * head], value_rows], axis=0)
-    d_query = jnp.zeros((head, 2 * width), F32)
+    both = jnp.concatenate([own_ref[head:], pair_ref[head:]], axis=1)
+    more = packs_ref.shape[1] - head
+    key_rows = rows_of(more, 2 * width, ONES + [(6, pair_bias)]).astype(BF16)
+    key = jnp.concatenate([both[0:head], key_rows], axis=0)
+    value = jnp.concatenate([both[head:], rows_of(more, 2 * width, DELTAS).astype(BF16)], axis=0)
     d_key = jnp.zeros((head, 2 * width), F32)
     d_value = jnp.zeros((head, 2 * width), F32)
     for first in range(0, blocks, 2):
-        keys, queries, grads, query_scores, key_scores, weights = [], [], [], [], [], []
+        queries, grads, scores, weights = [], [], [], []
         for b in (first, first + 1):
-            key_b = all_ref[b, head : 2 * head]
-            key_aug = jnp.concatenate([key_b, rows_of(16, width, ones + [(6, bias_of(place_ref, b, base))]).astype(BF16)], axis=0)
-            value_aug = jnp.concatenate([all_ref[b, 2 * head : 3 * head], value_rows[:, :width]], axis=0)
-            weight = jnp.exp(dot00(key_aug, query))
-            query_scores.append((weight * dot00(value_aug, packs)).astype(BF16))
-            keys.append(key_b)
             query_b = (all_ref[b, 0:head].astype(F32) * scale).astype(BF16)
-            query_aug = jnp.concatenate([query_b, packs_ref[b, head : head + 16]], axis=0)
+            query_aug = jnp.concatenate([query_b, packs_ref[b, head:]], axis=0)
             weight = jnp.exp(dot00(query_aug, key))
-            key_scores.append((weight * dot00(packs_ref[b, 0:80], value)).astype(BF16))
+            scores.append((weight * dot00(packs_ref[b], value)).astype(BF16))
             weights.append(weight.astype(BF16))
             queries.append(query_b)
             grads.append(packs_ref[b, 0:head])
-        d_query = d_query + dot10(jnp.concatenate(keys, axis=1), jnp.concatenate(query_scores, axis=0))
-        d_key = d_key + dot10(jnp.concatenate(queries, axis=1), jnp.concatenate(key_scores, axis=0))
+        d_key = d_key + dot10(jnp.concatenate(queries, axis=1), jnp.concatenate(scores, axis=0))
         d_value = d_value + dot10(jnp.concatenate(grads, axis=1), jnp.concatenate(weights, axis=0))
-    d_query = d_query * scale
     for ref, at in ((mine_ref, 0), (other_ref, width)):
         kind = ref.dtype
-        ref[0:head] = d_query[:, at : at + width].astype(kind)
+        ref[0:head] = d_query_ref[:, at : at + width].astype(kind)
         ref[head : 2 * head] = d_key[:, at : at + width].astype(kind)
         ref[2 * head : 3 * head] = d_value[:, at : at + width].astype(kind)
 
 
-def finish(mine_ref, got_ref, query_ref, key_ref, value_ref):
-    total = mine_ref[...] + got_ref[...].astype(F32)
+def finish(place_ref, mine_ref, got_ref, query_ref, key_ref, value_ref):
+    total = mine_ref[...] + got_ref[1 - place_ref[4]].astype(F32)
     query_ref[...] = total[0:64].astype(BF16)
     key_ref[...] = total[64:128].astype(BF16)
     value_ref[...] = total[128:192].astype(BF16)
@@ -277,14 +294,12 @@
 
 
 def mix_sum(packs_ref, out_ref):
-    share = packs_ref.shape[1] - 80
-    total = jnp.zeros((share, 128), F32)
-    stats = jnp.zeros((16, 128), F32)
+    share = packs_ref.shape[1] - 72
+    total = jnp.zeros((share + 8, 128), F32)
     for j in range(packs_ref.shape[0]):
-        total = total + packs_ref[j, 80:].astype(F32)
-        stats = stats + packs_ref[j, 64:80].astype(F32)
-    out_ref[0:share] = total
-    out_ref[share:] = rows_of(out_ref.shape[0] - share, 128, [(0, stats[7:8])])
+        total = total + packs_ref[j, 64:].astype(F32)
+    out_ref[0:share] = total[8:]
+    out_ref[share:] = rows_of(out_ref.shape[0] - share, 128, [(0, total[7:8])])
 
 
 def mix_spread(both_ref, out_ref):
@@ -363,7 +378,7 @@
             half_rows,
             half_rows,
             jax.ShapeDtypeStruct((80, width), BF16),
-            jax.ShapeDtypeStruct((depth, 80 + share, width), BF16),
+            jax.ShapeDtypeStruct((depth, 72 + share, width), BF16),
         ),
         2 ** 27,
         [pltpu.VMEM(mix_weight.shape, BF16), pltpu.SemaphoreType.DMA],
@@ -374,21 +389,24 @@
     keep_got = lax.ppermute(send, "core", swap)
     partial = call(add_pair, half_rows, 2 ** 20)(keep, keep_got)
     pack_pair = lax.ppermute(pack, "yh", swap)
-    packs, pack_pair, partial = lax.optimization_barrier((packs, pack_pair, partial))
-
-    mix_mine = call(mix_sum, jax.ShapeDtypeStruct((share + 16, width), F32), 2 ** 22)(packs)
+    d_query = call(query_back, jax.ShapeDtypeStruct((head, 2 * width), F32), 2 ** 28, scalars=1)(
+        place, everyone, own, pair, pack, pack_pair
+    )
+    packs, d_query, partial = lax.optimization_barrier((packs, d_query, partial))
+
+    mix_mine = call(mix_sum, jax.ShapeDtypeStruct((share + 8, width), F32), 2 ** 22)(packs)
     mix_both = lax.all_gather(mix_mine, "yh", axis=0)
-    spread = call(mix_spread, jax.ShapeDtypeStruct((depth, share + 16, width), BF16), 2 ** 20)(mix_both)
+    spread = call(mix_spread, jax.ShapeDtypeStruct((depth, share + 8, width), BF16), 2 ** 20)(mix_both)
     block_parts = lax.all_to_all(partial.reshape(lanes // 2, rows8, model), "chip", 0, 0, tiled=True)
     spread, block_parts = lax.optimization_barrier((spread, block_parts))
     pieces = lax.all_to_all(spread, "z", 0, 0, tiled=True)
     result = jax.ShapeDtypeStruct((3 * head, width), F32)
     sent = jax.ShapeDtypeStruct(result.shape, BF16)
     mine, other = call(backward, (result, sent), 2 ** 29, scalars=1)(
-        place, everyone, packs, own, pair, pack, pack_pair
+        place, everyone, packs, own, pair, d_query
     )
-    got = lax.ppermute(other, "yh", swap)
-    d_query, d_key, d_value = call(finish, (block, block, block), 2 ** 20)(mine, got)
+    got = lax.all_gather(other, "yh", axis=0)
+    d_query, d_key, d_value = call(finish, (block, block, block), 2 ** 20, scalars=1)(place, mine, got)
 
     block_out = call(sum_blocks, jax.ShapeDtypeStruct((rows8, model), BF16), 2 ** 20)(block_parts)
     mix_grad, tap_total = call(

time: 138 us -> 136 us (0.986)
  the two profiles are of different devices: /device:TPU:34 before, /device:TPU:56 now
where the time goes in v7:
time: 136 us
  blocking collectives  65.4 us (48%)
  starting transfers between devices  35.4 us (26%)
  Pallas kernels  15.9 us (12%)
  waiting for transfers between devices  15.6 us (11%)
  between operations  1.38 us (1%)
    all_gather x1, blocking collectives, body(): everyone = lax.all_gather(front, 'z', axis=0)  39.5 us
    all_gather x2, blocking collectives, body(): got = lax.all_gather(other, 'yh', axis=0)  12.9 us
    all_to_all x1, starting transfers between devices, body(): lax.all_to_all(jnp.broadcast_to(with_rim[None], (lanes,) + with_rim.shape...  8.6 us
    all_to_all x1, starting transfers between devices, body(): packs = lax.all_to_all(copies, 'z', 0, 0, tiled=True)  8.47 us
    all_to_all x1, waiting for transfers between devices, body(): packs = lax.all_to_all(copies, 'z', 0, 0, tiled=True)  7.87 us
    all_to_all x1, starting transfers between devices, body(): pieces = lax.all_to_all(spread, 'z', 0, 0, tiled=True)  6.84 us
    all_gather x1, blocking collectives, body(): both = lax.all_gather(own, 'yh', axis=0)  6.56 us
    all_gather x1, blocking collectives, body(): mix_both = lax.all_gather(mix_mine, 'yh', axis=0)  6.4 us
  transfers between devices with their start and end apart: 7, of which 3 were waited for; matrix products, arithmetic and copies ran while one was open for 1% of the time, Pallas kernels for 6%

profile of v7, /device:TPU:56, one launch (start us, length us, event | category | flops | bytes accessed | tf_op | source)
XLA Modules:
  0.0 135.7 jit_solution(3623851433940109674)
XLA Ops:
  0.6 0.7 collective-permute-start
  1.3 0.8 pad_maximum_fusion.own_ref
  2.1 6.6 %all-gather = bf16[384,128]{1,0:T(8,128)(2,1)S(1)} all-gather(bf16[192,128]{1,0:T(8,128)(2,1)S(1)} %pad_maximum_fusion.own_ref), channel_id=2, replica_groups=mesh['yh'=2,'z'=16,'chip'=8,'core'=2] {'yh'}, dimensions={0}, use_global_device_ids=true | all-gather | bytes 147456 | tf_op jit(solution)/shard_map/all_gather | solution.py:353
  8.6 1.0 broadcast_in_dim.2
  9.6 8.6 %all-to-all-start = ((bf16[16,16,1536]{2,1,0:T(8,128)(2,1)}), bf16[16,16,1536]{2,1,0:T(8,128)(2,1)S(1)}, u32[]{:S(2)}, u32[]{:S(2)}) async-start(bf16[16,16,1536]{2,1,0:T(8,128)(2,1)} %broadcast_in_dim.2), calls=%async_computation | async-start | bytes 1572864 | tf_op jit(solution)/shard_map/all_to_all | solution.py:362
  18.9 0.0 copy-done.2
  18.9 0.1 copy.13
  19.0 0.1 stack.19.place_ref
  19.1 0.7 shard_map.118
  19.8 39.5 %all-gather.1 = bf16[3584,128]{1,0:T(8,128)(2,1)S(1)} all-gather(bf16[224,128]{1,0:T(8,128)(2,1)S(1)} %get-tuple-element.34), channel_id=3, replica_groups=mesh['yh'=2,'z'=16,'chip'=8,'core'=2] {'z'}, dimensions={0}, use_global_device_ids=true | all-gather | bytes 974848 | tf_op jit(solution)/shard_map/all_gather | solution.py:363
  59.3 2.2 %shard_map.119 = (f32[72,256]{1,0:T(8,128)S(1)}, f32[72,256]{1,0:T(8,128)S(1)}) custom-call(s32[6]{0:T(128)S(1)} %stack.19.place_ref, bf16[16,224,128]{2,1,0:T(8,128)(2,1)S(1)} %bitcast.17, bf16[192,128]{1,0:T(8,128)(2,1)S(1)} %pad_maximum_fusion.own_ref, bf16[192,128]{1,0:T(8,128)(2,1)S(1)} %get-tuple-element.36.pair_ref), custom_call_target="tpu_custom_call" | custom-call | flops 268435456 | bytes 1048576 | tf_op jit(solution)/shard_map/pallas_call | solution.py:368
  61.5 0.0 copy-start
  61.5 6.7 %all-gather.2 = f32[144,256]{1,0:T(8,128)S(1)} all-gather(f32[72,256]{1,0:T(8,128)S(1)} %get-tuple-element.40), channel_id=4, replica_groups=mesh['yh'=2,'z'=16,'chip'=8,'core'=2] {'yh'}, dimensions={0}, use_global_device_ids=true | all-gather | bytes 221184 | tf_op jit(solution)/shard_map/all_gather | solution.py:372
  68.2 4.3 %shard_map.120 = (bf16[64,1536]{1,0:T(8,128)(2,1)S(1)}, bf16[64,1536]{1,0:T(8,128)(2,1)S(1)}, bf16[80,128]{1,0:T(8,128)(2,1)S(1)}, bf16[16,120,128]{2,1,0:T(8,128)(2,1)}) custom-call(s32[6]{0:T(128)S(1)} %stack.19.place_ref, bf16[64,1536]{1,0:T(8,128)(2,1)S(1)} %copy-done, f32[72,256]{1,0:T(8,128)S(1)} %get-tuple-element.37.mine_ref, ...), custom_call_target="tpu_custom_call" | custom-call | flops 134217728 | bytes 1048576 | tf_op jit(solution)/shard_map/pallas_call | solution.py:375
  72.6 8.5 %all-to-all-start.1 = ((bf16[16,120,128]{2,1,0:T(8,128)(2,1)}), bf16[16,120,128]{2,1,0:T(8,128)(2,1)S(1)}, u32[]{:S(2)}, u32[]{:S(2)}) async-start(bf16[16,120,128]{2,1,0:T(8,128)(2,1)} %get-tuple-element.42), calls=%async_computation.1 | async-start | bytes 983040 | tf_op jit(solution)/shard_map/all_to_all | solution.py:388
  81.0 1.9 %collective-permute-start.2 = (bf16[64,1536]{1,0:T(8,128)(2,1)S(1)}, bf16[64,1536]{1,0:T(8,128)(2,1)S(1)}, u32[]{:S(2)}, u32[]{:S(2)}) collective-permute-start(bf16[64,1536]{1,0:T(8,128)(2,1)S(1)} %get-tuple-element.45), channel_id=1, source_target_pairs={{0,1},{1,0},{2,3},{3,2},{4,5},{5,4},{6,7},{7,6},{8,9},{9,8},{10,11... | collective-permute-start | bytes 589832 | tf_op jit(solution)/shard_map/ppermute | solution.py:389
  82.9 3.2 %collective-permute-start.1 = (bf16[80,128]{1,0:T(8,128)(2,1)S(1)}, bf16[80,128]{1,0:T(8,128)(2,1)S(1)}, u32[]{:S(2)}, u32[]{:S(2)}) collective-permute-start(bf16[80,128]{1,0:T(8,128)(2,1)S(1)} %get-tuple-element.43.pack_own_ref), channel_id=1, source_target_pairs={{0,256},{256,0},{1,257},{257,1},{2,258},{258,2},{3,259},{259,3},{4... | collective-permute-start | bytes 61448 | tf_op jit(solution)/shard_map/ppermute | solution.py:391
  86.1 4.0 %collective-permute-done.1.pack_pair_ref = bf16[80,128]{1,0:T(8,128)(2,1)S(1)} collective-permute-done((bf16[80,128]{1,0:T(8,128)(2,1)S(1)}, bf16[80,128]{1,0:T(8,128)(2,1)S(1)}, u32[]{:S(2)}, u32[]{:S(2)}) %collective-permute-start.1) | collective-permute-done | bytes 20512 | tf_op jit(solution)/shard_map/ppermute | solution.py:391
  90.1 2.2 %shard_map.121.d_query_ref = f32[64,256]{1,0:T(8,128)S(1)} custom-call(s32[6]{0:T(128)S(1)} %stack.19.place_ref, bf16[16,224,128]{2,1,0:T(8,128)(2,1)S(1)} %bitcast.18, bf16[192,128]{1,0:T(8,128)(2,1)S(1)} %pad_maximum_fusion.own_ref, bf16[192,128]{1,0:T(8,128)(2,1)S(1)} %get-tuple-element.36.pair_ref, bf16[80,128]{1,0:T(8,128)(2,1)S(1)} %get-tuple-element.43.pack_own_ref, ...), custom_call_target="tpu_custom_call" | custom-call | flops 268435456 | bytes 1048576 | tf_op jit(solution)/shard_map/pallas_call | solution.py:392
  92.4 0.0 collective-permute-done.2.got_ref
  92.4 0.7 shard_map.122
  93.1 7.9 %all-to-all-done.1.packs_ref = bf16[16,120,128]{2,1,0:T(8,128)(2,1)S(1)} async-done(((bf16[16,120,128]{2,1,0:T(8,128)(2,1)}), bf16[16,120,128]{2,1,0:T(8,128)(2,1)S(1)}, u32[]{:S(2)}, u32[]{:S(2)}) %all-to-all-start.1) | async-done | bytes 491552 | tf_op jit(solution)/shard_map/all_to_all | solution.py:388
  101.0 5.7 %all-to-all-start.2 = ((bf16[8,8,1536]{2,1,0:T(8,128)(2,1)}), bf16[8,8,1536]{2,1,0:T(8,128)(2,1)S(1)}, u32[]{:S(2)}, u32[]{:S(2)}) async-start(bf16[8,8,1536]{2,1,0:T(8,128)(2,1)} %bitcast.12), calls=%async_computation.2 | async-start | bytes 393216 | tf_op jit(solution)/shard_map/all_to_all | solution.py:400
  106.7 6.4 %all-gather.3 = f32[112,128]{1,0:T(8,128)S(1)} all-gather(f32[56,128]{1,0:T(8,128)S(1)} %shard_map.123), channel_id=5, replica_groups=mesh['yh'=2,'z'=16,'chip'=8,'core'=2] {'yh'}, dimensions={0}, use_global_device_ids=true | all-gather | bytes 86016 | tf_op jit(solution)/shard_map/all_gather | solution.py:398
  113.1 0.7 shard_map.124
  113.8 6.8 %all-to-all-start.3 = ((bf16[16,56,128]{2,1,0:T(8,128)(2,1)}), bf16[16,56,128]{2,1,0:T(8,128)(2,1)S(1)}, u32[]{:S(2)}, u32[]{:S(2)}) async-start(bf16[16,56,128]{2,1,0:T(8,128)(2,1)} %shard_map.124), calls=%async_computation.3 | async-start | bytes 458752 | tf_op jit(solution)/shard_map/all_to_all | solution.py:402
  120.7 2.4 %shard_map.126 = (f32[192,128]{1,0:T(8,128)S(1)}, bf16[192,128]{1,0:T(8,128)(2,1)S(1)}) custom-call(s32[6]{0:T(128)S(1)} %stack.19.place_ref, bf16[16,224,128]{2,1,0:T(8,128)(2,1)S(1)} %bitcast.19, bf16[16,120,128]{2,1,0:T(8,128)(2,1)S(1)} %all-to-all-done.1.packs_ref, bf16[192,128]{1,0:T(8,128)(2,1)S(1)} %pad_maximum_fusion.own_ref, ...), custom_call_target="tpu_custom_call" | custom-call | flops 536870912 | bytes 1048576 | tf_op jit(solution)/shard_map/pallas_call | solution.py:405
  123.1 6.3 %all-gather.4 = bf16[384,128]{1,0:T(8,128)(2,1)S(1)} all-gather(bf16[192,128]{1,0:T(8,128)(2,1)S(1)} %get-tuple-element.51), channel_id=6, replica_groups=mesh['yh'=2,'z'=16,'chip'=8,'core'=2] {'yh'}, dimensions={0}, use_global_device_ids=true | all-gather | bytes 147456 | tf_op jit(solution)/shard_map/all_gather | solution.py:408
  129.4 1.2 shard_map.127
  130.5 0.6 shard_map.125
  131.2 3.8 %all-to-all-done.3.parts_ref = bf16[16,56,128]{2,1,0:T(8,128)(2,1)S(1)} async-done(((bf16[16,56,128]{2,1,0:T(8,128)(2,1)}), bf16[16,56,128]{2,1,0:T(8,128)(2,1)S(1)}, u32[]{:S(2)}, u32[]{:S(2)}) %all-to-all-start.3) | async-done | bytes 229408 | tf_op jit(solution)/shard_map/all_to_all | solution.py:402
  134.9 0.8 shard_map.128
  (9 shorter events, 0.1 us)
Async XLA Ops:
  0.6 8.0 %collective-permute-start = (bf16[8,1536]{1,0:T(8,128)(2,1)}, bf16[8,1536]{1,0:T(8,128)(2,1)S(1)}, u32[]{:S(2)}, u32[]{:S(2)}) collective-permute-start(bf16[8,1536]{1,0:T(8,128)(2,1)} %param.13), channel_id=1, source_target_pairs={{14,16},{16,14},{15,17},{17,15},{30,32},{32,30},{31,33},{33,31},{4... | collective-permute-start | bytes 73736 | tf_op jit(solution)/shard_map/ppermute | solution.py:351
  2.1 6.6 %copy-start.1 = (bf16[8,1536]{1,0:T(8,128)(2,1)S(1)}, bf16[8,1536]{1,0:T(8,128)(2,1)}, u32[]{:S(2)}) copy-start(bf16[8,1536]{1,0:T(8,128)(2,1)} %param.13) | copy-start | bytes 73732
  9.6 49.7 %all-to-all-start = ((bf16[16,16,1536]{2,1,0:T(8,128)(2,1)}), bf16[16,16,1536]{2,1,0:T(8,128)(2,1)S(1)}, u32[]{:S(2)}, u32[]{:S(2)}) async-start(bf16[16,16,1536]{2,1,0:T(8,128)(2,1)} %broadcast_in_dim.2), calls=%async_computation | async-start | bytes 1572864 | tf_op jit(solution)/shard_map/all_to_all | solution.py:362
  18.2 0.7 copy-start.2
  61.5 6.7 %copy-start = (bf16[64,1536]{1,0:T(8,128)(2,1)S(1)}, bf16[64,1536]{1,0:T(8,128)(2,1)}, u32[]{:S(2)}) copy-start(bf16[64,1536]{1,0:T(8,128)(2,1)} %weight_hbm.1) | copy-start | bytes 589828
  72.6 28.4 %all-to-all-start.1 = ((bf16[16,120,128]{2,1,0:T(8,128)(2,1)}), bf16[16,120,128]{2,1,0:T(8,128)(2,1)S(1)}, u32[]{:S(2)}, u32[]{:S(2)}) async-start(bf16[16,120,128]{2,1,0:T(8,128)(2,1)} %get-tuple-element.42), calls=%async_computation.1 | async-start | bytes 983040 | tf_op jit(solution)/shard_map/all_to_all | solution.py:388
  81.0 11.3 %collective-permute-start.2 = (bf16[64,1536]{1,0:T(8,128)(2,1)S(1)}, bf16[64,1536]{1,0:T(8,128)(2,1)S(1)}, u32[]{:S(2)}, u32[]{:S(2)}) collective-permute-start(bf16[64,1536]{1,0:T(8,128)(2,1)S(1)} %get-tuple-element.45), channel_id=1, source_target_pairs={{0,1},{1,0},{2,3},{3,2},{4,5},{5,4},{6,7},{7,6},{8,9},{9,8},{10,11... | collective-permute-start | bytes 589832 | tf_op jit(solution)/shard_map/ppermute | solution.py:389
  82.9 7.2 %collective-permute-start.1 = (bf16[80,128]{1,0:T(8,128)(2,1)S(1)}, bf16[80,128]{1,0:T(8,128)(2,1)S(1)}, u32[]{:S(2)}, u32[]{:S(2)}) collective-permute-start(bf16[80,128]{1,0:T(8,128)(2,1)S(1)} %get-tuple-element.43.pack_own_ref), channel_id=1, source_target_pairs={{0,256},{256,0},{1,257},{257,1},{2,258},{258,2},{3,259},{259,3},{4... | collective-permute-start | bytes 61448 | tf_op jit(solution)/shard_map/ppermute | solution.py:391
  101.0 12.9 %all-to-all-start.2 = ((bf16[8,8,1536]{2,1,0:T(8,128)(2,1)}), bf16[8,8,1536]{2,1,0:T(8,128)(2,1)S(1)}, u32[]{:S(2)}, u32[]{:S(2)}) async-start(bf16[8,8,1536]{2,1,0:T(8,128)(2,1)} %bitcast.12), calls=%async_computation.2 | async-start | bytes 393216 | tf_op jit(solution)/shard_map/all_to_all | solution.py:400
  113.8 21.1 %all-to-all-start.3 = ((bf16[16,56,128]{2,1,0:T(8,128)(2,1)}), bf16[16,56,128]{2,1,0:T(8,128)(2,1)S(1)}, u32[]{:S(2)}, u32[]{:S(2)}) async-start(bf16[16,56,128]{2,1,0:T(8,128)(2,1)} %shard_map.124), calls=%async_computation.3 | async-start | bytes 458752 | tf_op jit(solution)/shard_map/all_to_all | solution.py:402

commit v8 on v7

--- a/solution.py
+++ b/solution.py
@@ -94,8 +94,7 @@
         rim = jnp.concatenate([even[8:16], odd[8:16]], axis=0).astype(BF16)
         if i == 0:
             low = rim
-    gap = jnp.zeros((128 - 2 * RIM, shared_ref.shape[2]), BF16)
-    return jnp.concatenate(rows, axis=0), jnp.concatenate([rim, gap, low], axis=0)
+    return jnp.concatenate([low] + rows + [rim], axis=0)
 
 
 def attend(place_ref, all_ref, own_ref, pair_ref, mine_ref, other_ref, score_ref):
@@ -149,17 +148,14 @@
     other_ref[:, width:] = pltpu.roll(edges, width // 2, 1)
 
 
-def shifted(ring, offset):
-    if offset == 0:
-        return ring
-    return pltpu.roll(ring, (-offset) % ring.shape[1], 1)
-
-
-def middle_part(place_ref, weight_hbm, mine_ref, got_ref, taps_ref, shared_ref, keep_ref, send_ref, pack_ref, copies_ref, weight_ref, sem):
+def middle_part(place_ref, weight_hbm, mine_ref, got_ref, taps_ref, shared_ref, keep_ref, send_ref, pack_ref, copies_ref, weight_ref, sem, wide_ref, back_ref):
     fetch = pltpu.make_async_copy(weight_hbm, weight_ref, sem)
     fetch.start()
     width = 128
+    head = 64
     ring = 2 * width
+    half = KSIZE // 2
+    reach = width + 2 * RIM
     start = place_ref[1]
     valid = place_ref[2]
     frames = place_ref[3]
@@ -172,50 +168,55 @@
     attn = attn.astype(BF16).astype(F32)
     lane = lax.broadcasted_iota(jnp.int32, (1, ring), 1)
     frame = start + jnp.where(lane < ring - width // 2, lane, lane - ring)
-    inside = (frame >= 0) & (frame < frames) & ((lane < width + 32) | (lane >= ring - 32))
-    live = inside & (frame < valid)
-    masked = jnp.where(live, attn, 0.0)
-    taps = taps_ref[...]
-    depth = jnp.zeros((64, ring), F32)
-    for t in range(KSIZE):
-        depth = depth + taps[:, t : t + 1] * shifted(masked, t - RIM)
+    masked = jnp.where((frame >= 0) & (frame < frames) & (frame < valid), attn, 0.0)
+    own_rows = masked[:, 0:width].T
+    side_rows = masked[:, width:ring].T
+    rows = jnp.concatenate([side_rows[96:128], own_rows, side_rows[0:32]], axis=0)
+    wide_ref[...] = jnp.concatenate([rows[0 : reach + half], rows[half : reach + KSIZE]], axis=1)
+    taps = jnp.concatenate([taps_ref[0:half], taps_ref[half:KSIZE]], axis=1)
+    depth = jnp.zeros((reach, width), F32)
+    for t in range(half):
+        depth = depth + taps[t : t + 1] * wide_ref[t : t + reach]
+    depth = depth[:, 0:head] + depth[:, head:width]
     gate = jax.nn.sigmoid(depth)
-    swish = (depth[:, :width] * gate[:, :width]).astype(BF16)
-    grad, side = lay_grads(shared_ref)
-    mix = dot10(swish, grad)
-    mix = jnp.concatenate([mix[:, at : at + width] for at in range(0, mix.shape[1], width)], axis=0).astype(BF16)
+    swish = (depth * gate)[RIM : RIM + width].astype(BF16)
+    grad = lay_grads(shared_ref)
+    mix = dot00(swish, grad[RIM : RIM + width])
+    mix = jnp.concatenate([mix[:, at : at + width] for at in range(0, mix.shape[1], width)], axis=0)
     fetch.wait()
     weight = weight_ref[...]
-    partial = dot00(swish, weight)
+    partial = dot10(swish, weight)
     core = place_ref[5] == 0
     even = jnp.concatenate([partial[at : at + 8] for at in range(0, width, 16)], axis=0)
     odd = jnp.concatenate([partial[at + 8 : at + 16] for at in range(0, width, 16)], axis=0)
     keep_ref[...] = jnp.where(core, even, odd).astype(BF16)
     send_ref[...] = jnp.where(core, odd, even).astype(BF16)
-    back = jnp.concatenate([dot11(weight, grad), dot11(weight, side)], axis=1)
-    dgrad = back * gate * (1.0 + depth * (1.0 - gate))
-    dgrad = jnp.where(inside, dgrad, 0.0).astype(BF16).astype(F32)
-    row = lax.broadcasted_iota(jnp.int32, (64, width), 1)
-    sums = jnp.zeros((64, width), F32)
-    total = jnp.zeros((64, width), F32)
-    for t in range(KSIZE):
-        column = jnp.sum(shifted(masked, t - RIM)[:, :width] * dgrad[:, :width], axis=1, keepdims=True)
-        sums = jnp.where(row == t, column, sums)
-        total = total + taps[:, t : t + 1] * shifted(dgrad, RIM - t)[:, :width]
-    turned = sums.T
-    tap_grad = jnp.concatenate([turned[0:16, 0:64], turned[16:32, 0:64]], axis=1)
-    grad_out = jnp.where(live[:, :width], total, 0.0).astype(BF16)
+    dgrad = dot11(grad, weight) * gate * (1.0 + depth * (1.0 - gate))
+    row = start - RIM + lax.broadcasted_iota(jnp.int32, (reach, head), 0)
+    dgrad = jnp.where((row >= 0) & (row < frames), dgrad, 0.0).astype(BF16).astype(F32)
+    back_ref[...] = jnp.concatenate([dgrad[half:reach], dgrad[0 : reach - half]], axis=1)
+    inner = dgrad[RIM : RIM + width]
+    inner = jnp.concatenate([inner, inner], axis=1)
+    total = jnp.zeros((width, width), F32)
+    tap_rows = []
+    for t in range(half):
+        total = total + taps[t : t + 1] * back_ref[half - t : half - t + width]
+        tap_rows.append((t, jnp.sum(wide_ref[RIM + t : RIM + t + width] * inner, axis=0, keepdims=True)))
+    tap_grad = rows_of(half, width, tap_rows)
+    total = total[:, 0:head] + total[:, head:width]
+    row = start + lax.broadcasted_iota(jnp.int32, (width, head), 0)
+    grad_out = jnp.where(row < valid, total, 0.0).T.astype(BF16)
     delta = jnp.sum(grad_out.astype(F32) * attn[:, :width], axis=0, keepdims=True)
     a, b, c = split3(-lse[:, :width])
     d, e, f = split3(-delta)
     stats = rows_of(16, width, [(0, a), (1, b), (2, c), (3, d), (4, e), (5, f), (6, 1.0)])
     pack_ref[...] = jnp.concatenate([grad_out, stats.astype(BF16)], axis=0)
-    row = lax.broadcasted_iota(jnp.int32, stats.shape, 0)
+    row = lax.broadcasted_iota(jnp.int32, (8, width), 0)
     share = copies_ref.shape[1] - 72
     for j in range(copies_ref.shape[0]):
         copies_ref[j, 0:64] = grad_out
-        rest = jnp.where(row == 7, tap_grad[j : j + 1], stats)[0:8]
-        rest = jnp.concatenate([rest, mix[j * share : (j + 1) * share].astype(F32)], axis=0)
+        rest = jnp.where(row == 7, tap_grad[j : j + 1], stats[0:8])
+        rest = jnp.concatenate([rest, mix[j * share : (j + 1) * share]], axis=0)
         copies_ref[j, 64:] = rest.astype(BF16)
 
 
@@ -340,7 +341,6 @@
     spot = lax.axis_index("z")
     place = jnp.stack([spot, (half * depth + spot) * width, valid, jnp.int32(width * devices), half, lax.axis_index("core")]).astype(jnp.int32)
     swap = [(0, 1), (1, 0)]
-    taps = depth_kernel.T
     rim_pairs = []
     sides = RIM // rows8
     for i in range(devices - 1):
@@ -381,10 +381,15 @@
             jax.ShapeDtypeStruct((depth, 72 + share, width), BF16),
         ),
         2 ** 27,
-        [pltpu.VMEM(mix_weight.shape, BF16), pltpu.SemaphoreType.DMA],
+        [
+            pltpu.VMEM(mix_weight.shape, BF16),
+            pltpu.SemaphoreType.DMA,
+            pltpu.VMEM((width + 2 * RIM + KSIZE // 2, width), F32),
+            pltpu.VMEM((width + 2 * RIM - KSIZE // 2, width), F32),
+        ],
         scalars=1,
         remote=1,
-    )(place, mix_weight, mine, got, taps, shared)
+    )(place, mix_weight, mine, got, depth_kernel, shared)
     packs = lax.all_to_all(copies, "z", 0, 0, tiled=True)
     keep_got = lax.ppermute(send, "core", swap)
     partial = call(add_pair, half_rows, 2 ** 20)(keep, keep_got)

time: 136 us -> 135 us (level)
  Pallas kernels: 15.9 us -> 14.5 us
    pallas_call x1, Pallas kernels: 4.34 us -> 2.9 us  [body(): call(middle_part, (half_rows, half_rows, jax.ShapeDtypeStruct((80, width)...]
where the time goes in v8:
time: 135 us; the launch traced here: 134 us
  blocking collectives  65.4 us (48%)
  starting transfers between devices  35.3 us (26%)
  waiting for transfers between devices  15.7 us (12%)
  Pallas kernels  14.5 us (11%)
  between operations  1.37 us (1%)
    all_gather x1, blocking collectives, body(): everyone = lax.all_gather(front, 'z', axis=0)  39.5 us
    all_gather x2, blocking collectives, body(): got = lax.all_gather(other, 'yh', axis=0)  12.9 us
    all_to_all x1, starting transfers between devices, body(): lax.all_to_all(jnp.broadcast_to(with_rim[None], (lanes,) + with_rim.shape...  8.6 us
    all_to_all x1, starting transfers between devices, body(): packs = lax.all_to_all(copies, 'z', 0, 0, tiled=True)  8.49 us
    all_to_all x1, waiting for transfers between devices, body(): packs = lax.all_to_all(copies, 'z', 0, 0, tiled=True)  7.86 us
    all_to_all x1, starting transfers between devices, body(): pieces = lax.all_to_all(spread, 'z', 0, 0, tiled=True)  6.84 us
    all_gather x1, blocking collectives, body(): both = lax.all_gather(own, 'yh', axis=0)  6.56 us
    all_gather x1, blocking collectives, body(): mix_both = lax.all_gather(mix_mine, 'yh', axis=0)  6.4 us
  transfers between devices with their start and end apart: 7, of which 3 were waited for; matrix products, arithmetic and copies ran while one was open for 1% of the time, Pallas kernels for 6%

profile of v8, /device:TPU:56, one launch (start us, length us, event | category | flops | bytes accessed | tf_op | source)
XLA Modules:
  0.0 134.1 jit_solution(11753405704266985215)
XLA Ops:
  0.6 0.7 collective-permute-start
  1.3 0.8 pad_maximum_fusion.own_ref
  2.1 6.6 %all-gather = bf16[384,128]{1,0:T(8,128)(2,1)S(1)} all-gather(bf16[192,128]{1,0:T(8,128)(2,1)S(1)} %pad_maximum_fusion.own_ref), channel_id=2, replica_groups=mesh['yh'=2,'z'=16,'chip'=8,'core'=2] {'yh'}, dimensions={0}, use_global_device_ids=true | all-gather | bytes 147456 | tf_op jit(solution)/shard_map/all_gather | solution.py:353
  8.6 0.0 collective-permute-done
  8.6 1.0 broadcast_in_dim.2
  9.6 8.6 %all-to-all-start = ((bf16[16,16,1536]{2,1,0:T(8,128)(2,1)}), bf16[16,16,1536]{2,1,0:T(8,128)(2,1)S(1)}, u32[]{:S(2)}, u32[]{:S(2)}) async-start(bf16[16,16,1536]{2,1,0:T(8,128)(2,1)} %broadcast_in_dim.2), calls=%async_computation | async-start | bytes 1572864 | tf_op jit(solution)/shard_map/all_to_all | solution.py:362
  18.9 0.1 stack.19.place_ref
  18.9 0.7 shard_map.118
  19.6 39.5 %all-gather.1 = bf16[3584,128]{1,0:T(8,128)(2,1)S(1)} all-gather(bf16[224,128]{1,0:T(8,128)(2,1)S(1)} %get-tuple-element.34), channel_id=3, replica_groups=mesh['yh'=2,'z'=16,'chip'=8,'core'=2] {'z'}, dimensions={0}, use_global_device_ids=true | all-gather | bytes 974848 | tf_op jit(solution)/shard_map/all_gather | solution.py:363
  59.2 2.2 %shard_map.119 = (f32[72,256]{1,0:T(8,128)S(1)}, f32[72,256]{1,0:T(8,128)S(1)}) custom-call(s32[6]{0:T(128)S(1)} %stack.19.place_ref, bf16[16,224,128]{2,1,0:T(8,128)(2,1)S(1)} %bitcast.16, bf16[192,128]{1,0:T(8,128)(2,1)S(1)} %pad_maximum_fusion.own_ref, bf16[192,128]{1,0:T(8,128)(2,1)S(1)} %get-tuple-element.36.pair_ref), custom_call_target="tpu_custom_call" | custom-call | flops 268435456 | bytes 1048576 | tf_op jit(solution)/shard_map/pallas_call | solution.py:368
  61.4 0.0 copy-start
  61.4 0.0 copy-start.1
  61.4 6.7 %all-gather.2 = f32[144,256]{1,0:T(8,128)S(1)} all-gather(f32[72,256]{1,0:T(8,128)S(1)} %get-tuple-element.40), channel_id=4, replica_groups=mesh['yh'=2,'z'=16,'chip'=8,'core'=2] {'yh'}, dimensions={0}, use_global_device_ids=true | all-gather | bytes 221184 | tf_op jit(solution)/shard_map/all_gather | solution.py:372
  68.1 2.9 %shard_map.120 = (bf16[64,1536]{1,0:T(8,128)(2,1)S(1)}, bf16[64,1536]{1,0:T(8,128)(2,1)S(1)}, bf16[80,128]{1,0:T(8,128)(2,1)S(1)}, bf16[16,120,128]{2,1,0:T(8,128)(2,1)}) custom-call(s32[6]{0:T(128)S(1)} %stack.19.place_ref, bf16[64,1536]{1,0:T(8,128)(2,1)S(1)} %copy-done, f32[72,256]{1,0:T(8,128)S(1)} %get-tuple-element.37.mine_ref, ...), custom_call_target="tpu_custom_call" | custom-call | flops 134217728 | bytes 1048576 | tf_op jit(solution)/shard_map/pallas_call | solution.py:375
  71.0 8.5 %all-to-all-start.1 = ((bf16[16,120,128]{2,1,0:T(8,128)(2,1)}), bf16[16,120,128]{2,1,0:T(8,128)(2,1)S(1)}, u32[]{:S(2)}, u32[]{:S(2)}) async-start(bf16[16,120,128]{2,1,0:T(8,128)(2,1)} %get-tuple-element.42), calls=%async_computation.1 | async-start | bytes 983040 | tf_op jit(solution)/shard_map/all_to_all | solution.py:393
  79.5 1.9 %collective-permute-start.2 = (bf16[64,1536]{1,0:T(8,128)(2,1)S(1)}, bf16[64,1536]{1,0:T(8,128)(2,1)S(1)}, u32[]{:S(2)}, u32[]{:S(2)}) collective-permute-start(bf16[64,1536]{1,0:T(8,128)(2,1)S(1)} %get-tuple-element.45), channel_id=1, source_target_pairs={{0,1},{1,0},{2,3},{3,2},{4,5},{5,4},{6,7},{7,6},{8,9},{9,8},{10,11... | collective-permute-start | bytes 589832 | tf_op jit(solution)/shard_map/ppermute | solution.py:394
  81.4 3.1 %collective-permute-start.1 = (bf16[80,128]{1,0:T(8,128)(2,1)S(1)}, bf16[80,128]{1,0:T(8,128)(2,1)S(1)}, u32[]{:S(2)}, u32[]{:S(2)}) collective-permute-start(bf16[80,128]{1,0:T(8,128)(2,1)S(1)} %get-tuple-element.43.pack_own_ref), channel_id=1, source_target_pairs={{0,256},{256,0},{1,257},{257,1},{2,258},{258,2},{3,259},{259,3},{4... | collective-permute-start | bytes 61448 | tf_op jit(solution)/shard_map/ppermute | solution.py:396
  84.5 4.0 %collective-permute-done.1.pack_pair_ref = bf16[80,128]{1,0:T(8,128)(2,1)S(1)} collective-permute-done((bf16[80,128]{1,0:T(8,128)(2,1)S(1)}, bf16[80,128]{1,0:T(8,128)(2,1)S(1)}, u32[]{:S(2)}, u32[]{:S(2)}) %collective-permute-start.1) | collective-permute-done | bytes 20512 | tf_op jit(solution)/shard_map/ppermute | solution.py:396
  88.6 2.2 %shard_map.121.d_query_ref = f32[64,256]{1,0:T(8,128)S(1)} custom-call(s32[6]{0:T(128)S(1)} %stack.19.place_ref, bf16[16,224,128]{2,1,0:T(8,128)(2,1)S(1)} %bitcast.17, bf16[192,128]{1,0:T(8,128)(2,1)S(1)} %pad_maximum_fusion.own_ref, bf16[192,128]{1,0:T(8,128)(2,1)S(1)} %get-tuple-element.36.pair_ref, bf16[80,128]{1,0:T(8,128)(2,1)S(1)} %get-tuple-element.43.pack_own_ref, ...), custom_call_target="tpu_custom_call" | custom-call | flops 268435456 | bytes 1048576 | tf_op jit(solution)/shard_map/pallas_call | solution.py:397
  90.8 0.0 collective-permute-done.2.got_ref
  90.8 0.7 shard_map.122
  91.6 7.9 %all-to-all-done.1.packs_ref = bf16[16,120,128]{2,1,0:T(8,128)(2,1)S(1)} async-done(((bf16[16,120,128]{2,1,0:T(8,128)(2,1)}), bf16[16,120,128]{2,1,0:T(8,128)(2,1)S(1)}, u32[]{:S(2)}, u32[]{:S(2)}) %all-to-all-start.1) | async-done | bytes 491552 | tf_op jit(solution)/shard_map/all_to_all | solution.py:393
  99.4 5.7 %all-to-all-start.2 = ((bf16[8,8,1536]{2,1,0:T(8,128)(2,1)}), bf16[8,8,1536]{2,1,0:T(8,128)(2,1)S(1)}, u32[]{:S(2)}, u32[]{:S(2)}) async-start(bf16[8,8,1536]{2,1,0:T(8,128)(2,1)} %bitcast.11), calls=%async_computation.2 | async-start | bytes 393216 | tf_op jit(solution)/shard_map/all_to_all | solution.py:405
  105.2 6.4 %all-gather.3 = f32[112,128]{1,0:T(8,128)S(1)} all-gather(f32[56,128]{1,0:T(8,128)S(1)} %shard_map.123), channel_id=5, replica_groups=mesh['yh'=2,'z'=16,'chip'=8,'core'=2] {'yh'}, dimensions={0}, use_global_device_ids=true | all-gather | bytes 86016 | tf_op jit(solution)/shard_map/all_gather | solution.py:403
  111.6 0.7 shard_map.124
  112.3 6.8 %all-to-all-start.3 = ((bf16[16,56,128]{2,1,0:T(8,128)(2,1)}), bf16[16,56,128]{2,1,0:T(8,128)(2,1)S(1)}, u32[]{:S(2)}, u32[]{:S(2)}) async-start(bf16[16,56,128]{2,1,0:T(8,128)(2,1)} %shard_map.124), calls=%async_computation.3 | async-start | bytes 458752 | tf_op jit(solution)/shard_map/all_to_all | solution.py:407
  119.1 2.4 %shard_map.126 = (f32[192,128]{1,0:T(8,128)S(1)}, bf16[192,128]{1,0:T(8,128)(2,1)S(1)}) custom-call(s32[6]{0:T(128)S(1)} %stack.19.place_ref, bf16[16,224,128]{2,1,0:T(8,128)(2,1)S(1)} %bitcast.18, bf16[16,120,128]{2,1,0:T(8,128)(2,1)S(1)} %all-to-all-done.1.packs_ref, bf16[192,128]{1,0:T(8,128)(2,1)S(1)} %pad_maximum_fusion.own_ref, ...), custom_call_target="tpu_custom_call" | custom-call | flops 536870912 | bytes 1048576 | tf_op jit(solution)/shard_map/pallas_call | solution.py:410
  121.5 6.3 %all-gather.4 = bf16[384,128]{1,0:T(8,128)(2,1)S(1)} all-gather(bf16[192,128]{1,0:T(8,128)(2,1)S(1)} %get-tuple-element.51), channel_id=6, replica_groups=mesh['yh'=2,'z'=16,'chip'=8,'core'=2] {'yh'}, dimensions={0}, use_global_device_ids=true | all-gather | bytes 147456 | tf_op jit(solution)/shard_map/all_gather | solution.py:413
  127.8 1.2 shard_map.127
  129.0 0.6 shard_map.125
  129.6 3.8 %all-to-all-done.3.parts_ref = bf16[16,56,128]{2,1,0:T(8,128)(2,1)S(1)} async-done(((bf16[16,56,128]{2,1,0:T(8,128)(2,1)}), bf16[16,56,128]{2,1,0:T(8,128)(2,1)S(1)}, u32[]{:S(2)}, u32[]{:S(2)}) %all-to-all-start.3) | async-done | bytes 229408 | tf_op jit(solution)/shard_map/all_to_all | solution.py:407
  133.4 0.8 shard_map.128
  (8 shorter events, 0.1 us)
Async XLA Ops:
  0.6 8.0 %collective-permute-start = (bf16[8,1536]{1,0:T(8,128)(2,1)}, bf16[8,1536]{1,0:T(8,128)(2,1)S(1)}, u32[]{:S(2)}, u32[]{:S(2)}) collective-permute-start(bf16[8,1536]{1,0:T(8,128)(2,1)} %param.13), channel_id=1, source_target_pairs={{14,16},{16,14},{15,17},{17,15},{30,32},{32,30},{31,33},{33,31},{4... | collective-permute-start | bytes 73736 | tf_op jit(solution)/shard_map/ppermute | solution.py:351
  2.1 6.6 %copy-start.2 = (bf16[8,1536]{1,0:T(8,128)(2,1)S(1)}, bf16[8,1536]{1,0:T(8,128)(2,1)}, u32[]{:S(2)}) copy-start(bf16[8,1536]{1,0:T(8,128)(2,1)} %param.13) | copy-start | bytes 73732
  9.6 49.6 %all-to-all-start = ((bf16[16,16,1536]{2,1,0:T(8,128)(2,1)}), bf16[16,16,1536]{2,1,0:T(8,128)(2,1)S(1)}, u32[]{:S(2)}, u32[]{:S(2)}) async-start(bf16[16,16,1536]{2,1,0:T(8,128)(2,1)} %broadcast_in_dim.2), calls=%async_computation | async-start | bytes 1572864 | tf_op jit(solution)/shard_map/all_to_all | solution.py:362
  61.4 6.7 %copy-start = (bf16[64,1536]{1,0:T(8,128)(2,1)S(1)}, bf16[64,1536]{1,0:T(8,128)(2,1)}, u32[]{:S(2)}) copy-start(bf16[64,1536]{1,0:T(8,128)(2,1)} %weight_hbm.1) | copy-start | bytes 589828
  61.4 6.7 %copy-start.1 = (f32[32,64]{1,0:T(8,128)S(1)}, f32[32,64]{1,0:T(8,128)}, u32[]{:S(2)}) copy-start(f32[32,64]{1,0:T(8,128)} %taps_ref.1) | copy-start | bytes 24580
  71.0 28.4 %all-to-all-start.1 = ((bf16[16,120,128]{2,1,0:T(8,128)(2,1)}), bf16[16,120,128]{2,1,0:T(8,128)(2,1)S(1)}, u32[]{:S(2)}, u32[]{:S(2)}) async-start(bf16[16,120,128]{2,1,0:T(8,128)(2,1)} %get-tuple-element.42), calls=%async_computation.1 | async-start | bytes 983040 | tf_op jit(solution)/shard_map/all_to_all | solution.py:393
  79.5 11.3 %collective-permute-start.2 = (bf16[64,1536]{1,0:T(8,128)(2,1)S(1)}, bf16[64,1536]{1,0:T(8,128)(2,1)S(1)}, u32[]{:S(2)}, u32[]{:S(2)}) collective-permute-start(bf16[64,1536]{1,0:T(8,128)(2,1)S(1)} %get-tuple-element.45), channel_id=1, source_target_pairs={{0,1},{1,0},{2,3},{3,2},{4,5},{5,4},{6,7},{7,6},{8,9},{9,8},{10,11... | collective-permute-start | bytes 589832 | tf_op jit(solution)/shard_map/ppermute | solution.py:394
  81.4 7.2 %collective-permute-start.1 = (bf16[80,128]{1,0:T(8,128)(2,1)S(1)}, bf16[80,128]{1,0:T(8,128)(2,1)S(1)}, u32[]{:S(2)}, u32[]{:S(2)}) collective-permute-start(bf16[80,128]{1,0:T(8,128)(2,1)S(1)} %get-tuple-element.43.pack_own_ref), channel_id=1, source_target_pairs={{0,256},{256,0},{1,257},{257,1},{2,258},{258,2},{3,259},{259,3},{4... | collective-permute-start | bytes 61448 | tf_op jit(solution)/shard_map/ppermute | solution.py:396
  99.4 12.9 %all-to-all-start.2 = ((bf16[8,8,1536]{2,1,0:T(8,128)(2,1)}), bf16[8,8,1536]{2,1,0:T(8,128)(2,1)S(1)}, u32[]{:S(2)}, u32[]{:S(2)}) async-start(bf16[8,8,1536]{2,1,0:T(8,128)(2,1)} %bitcast.11), calls=%async_computation.2 | async-start | bytes 393216 | tf_op jit(solution)/shard_map/all_to_all | solution.py:405
  112.3 21.1 %all-to-all-start.3 = ((bf16[16,56,128]{2,1,0:T(8,128)(2,1)}), bf16[16,56,128]{2,1,0:T(8,128)(2,1)S(1)}, u32[]{:S(2)}, u32[]{:S(2)}) async-start(bf16[16,56,128]{2,1,0:T(8,128)(2,1)} %shard_map.124), calls=%async_computation.3 | async-start | bytes 458752 | tf_op jit(solution)/shard_map/all_to_all | solution.py:407

commit v9 on v8

--- a/solution.py
+++ b/solution.py
@@ -71,6 +71,12 @@
 def edges_of(packed):
     packed = packed.astype(F32)
     return jnp.concatenate([packed, pltpu.roll(packed, 64, 1)], axis=0)
+
+
+def copy_rows(own_ref, rim_ref, out_ref):
+    both = jnp.concatenate([own_ref[...].astype(F32), rim_ref[...].astype(F32)], axis=0).astype(BF16)
+    for j in range(out_ref.shape[0]):
+        out_ref[j] = both
 
 
 def first_pack(place_ref, both_ref, pack_ref, pair_ref):
@@ -144,8 +150,9 @@
     edges = both[:, 2 * width :]
     mine_ref[:, 0:width] = both[:, 0:width]
     mine_ref[:, width:] = edges
-    other_ref[:, 0:width] = both[:, width : 2 * width]
-    other_ref[:, width:] = pltpu.roll(edges, width // 2, 1)
+    other = jnp.concatenate([both[:, width : 2 * width], pltpu.roll(edges, width // 2, 1)], axis=1)
+    log_rows = rows_of(16, 2 * width, list(enumerate(split3(other[head : head + 1]))))
+    other_ref[...] = jnp.concatenate([other[0:head], log_rows], axis=0).astype(BF16)
 
 
 def middle_part(place_ref, weight_hbm, mine_ref, got_ref, taps_ref, shared_ref, keep_ref, send_ref, pack_ref, copies_ref, weight_ref, sem, wide_ref, back_ref):
@@ -161,10 +168,11 @@
     frames = place_ref[3]
     mine = mine_ref[64:65]
     side_at = 1 - place_ref[4]
-    got = got_ref[side_at, 64:65]
+    sent = got_ref[side_at].astype(F32)
+    got = sent[64:65] + sent[65:66] + sent[66:67]
     top = jnp.maximum(mine, got)
     lse = top + jnp.log(jnp.exp(mine - top) + jnp.exp(got - top))
-    attn = mine_ref[0:64] * jnp.exp(mine - lse) + got_ref[side_at, 0:64] * jnp.exp(got - lse)
+    attn = mine_ref[0:64] * jnp.exp(mine - lse) + sent[0:64] * jnp.exp(got - lse)
     attn = attn.astype(BF16).astype(F32)
     lane = lax.broadcasted_iota(jnp.int32, (1, ring), 1)
     frame = start + jnp.where(lane < ring - width // 2, lane, lane - ring)
@@ -358,15 +366,15 @@
         2 ** 20,
         scalars=1,
     )(place, both)
-    with_rim = jnp.concatenate([out_grad, rim_rows], axis=0)
-    shared = lax.all_to_all(jnp.broadcast_to(with_rim[None], (lanes,) + with_rim.shape), tp, 0, 0, tiled=True)
+    grads = call(copy_rows, jax.ShapeDtypeStruct((lanes, 2 * rows8, model), BF16), 2 ** 20)(out_grad, rim_rows)
+    shared = lax.all_to_all(grads, tp, 0, 0, tiled=True)
     everyone = lax.all_gather(front, "z", axis=0)
     shared, everyone = lax.optimization_barrier((shared, everyone))
 
     part = jax.ShapeDtypeStruct((head + 8, 2 * width), F32)
     block = jax.ShapeDtypeStruct((head, width), BF16)
     mine, other = call(
-        attend, (part, part), 2 ** 28, [pltpu.VMEM((depth, width, 3 * width), F32)], scalars=1
+        attend, (part, jax.ShapeDtypeStruct((head + 16, 2 * width), BF16)), 2 ** 28, [pltpu.VMEM((depth, width, 3 * width), F32)], scalars=1
     )(place, everyone, own, pair)
     shared, other = lax.optimization_barrier((shared, other))
     got = lax.all_gather(other, "yh", axis=0)

time: 135 us -> 134 us (level)
    pallas_call x1 -> x2, Pallas kernels: 2.21 us -> 3.14 us  [the longest x1 2.18 us: body(): call(attend, (part, jax.ShapeDtypeStruct((head + 16, 2 * width), BF16)),...]
where the time goes in v9:
time: 134 us
  blocking collectives  64.9 us (48%)
  starting transfers between devices  35.4 us (26%)
  waiting for transfers between devices  15.6 us (12%)
  Pallas kernels  15.5 us (12%)
  between operations  1.36 us (1%)
    all_gather x1, blocking collectives, body(): everyone = lax.all_gather(front, 'z', axis=0)  39.5 us
    all_gather x2, blocking collectives, body(): got = lax.all_gather(other, 'yh', axis=0)  12.5 us
    all_to_all x1, starting transfers between devices, body(): shared = lax.all_to_all(grads, tp, 0, 0, tiled=True)  8.6 us
    all_to_all x1, starting transfers between devices, body(): packs = lax.all_to_all(copies, 'z', 0, 0, tiled=True)  8.48 us
    all_to_all x1, waiting for transfers between devices, body(): packs = lax.all_to_all(copies, 'z', 0, 0, tiled=True)  7.86 us
    all_to_all x1, starting transfers between devices, body(): pieces = lax.all_to_all(spread, 'z', 0, 0, tiled=True)  6.84 us
    all_gather x1, blocking collectives, body(): both = lax.all_gather(own, 'yh', axis=0)  6.56 us
    all_gather x1, blocking collectives, body(): mix_both = lax.all_gather(mix_mine, 'yh', axis=0)  6.41 us
  transfers between devices with their start and end apart: 7, of which 3 were waited for; matrix products, arithmetic and copies ran while one was open for 1% of the time, Pallas kernels for 6%

profile of v9, /device:TPU:56, one launch (start us, length us, event | category | flops | bytes accessed | tf_op | source)
XLA Modules:
  0.0 133.6 jit_solution(2441368028985101914)
XLA Ops:
  0.6 0.7 collective-permute-start
  1.3 0.8 pad_maximum_fusion.own_ref
  2.1 6.6 %all-gather = bf16[384,128]{1,0:T(8,128)(2,1)S(1)} all-gather(bf16[192,128]{1,0:T(8,128)(2,1)S(1)} %pad_maximum_fusion.own_ref), channel_id=2, replica_groups=mesh['yh'=2,'z'=16,'chip'=8,'core'=2] {'yh'}, dimensions={0}, use_global_device_ids=true | all-gather | bytes 147456 | tf_op jit(solution)/shard_map/all_gather | solution.py:361
  8.6 1.0 shard_map.118
  9.6 8.6 %all-to-all-start = ((bf16[16,16,1536]{2,1,0:T(8,128)(2,1)}), bf16[16,16,1536]{2,1,0:T(8,128)(2,1)S(1)}, u32[]{:S(2)}, u32[]{:S(2)}) async-start(bf16[16,16,1536]{2,1,0:T(8,128)(2,1)} %shard_map.118), calls=%async_computation | async-start | bytes 1572864 | tf_op jit(solution)/shard_map/all_to_all | solution.py:370
  18.8 0.1 stack.19.place_ref
  18.9 0.7 shard_map.119
  19.6 39.5 %all-gather.1 = bf16[3584,128]{1,0:T(8,128)(2,1)S(1)} all-gather(bf16[224,128]{1,0:T(8,128)(2,1)S(1)} %get-tuple-element.34), channel_id=3, replica_groups=mesh['yh'=2,'z'=16,'chip'=8,'core'=2] {'z'}, dimensions={0}, use_global_device_ids=true | all-gather | bytes 974848 | tf_op jit(solution)/shard_map/all_gather | solution.py:371
  59.1 0.0 all-to-all-done.shared_ref
  59.2 2.2 %shard_map.120 = (f32[72,256]{1,0:T(8,128)S(1)}, bf16[80,256]{1,0:T(8,128)(2,1)S(1)}) custom-call(s32[6]{0:T(128)S(1)} %stack.19.place_ref, bf16[16,224,128]{2,1,0:T(8,128)(2,1)S(1)} %bitcast.16, bf16[192,128]{1,0:T(8,128)(2,1)S(1)} %pad_maximum_fusion.own_ref, bf16[192,128]{1,0:T(8,128)(2,1)S(1)} %get-tuple-element.36.pair_ref), custom_call_target="tpu_custom_call" | custom-call | flops 268435456 | bytes 1048576 | tf_op jit(solution)/shard_map/pallas_call | solution.py:376
  61.3 0.0 copy-start.2
  61.3 6.2 %all-gather.2 = bf16[160,256]{1,0:T(8,128)(2,1)S(1)} all-gather(bf16[80,256]{1,0:T(8,128)(2,1)S(1)} %get-tuple-element.40), channel_id=4, replica_groups=mesh['yh'=2,'z'=16,'chip'=8,'core'=2] {'yh'}, dimensions={0}, use_global_device_ids=true | all-gather | bytes 122880 | tf_op jit(solution)/shard_map/all_gather | solution.py:380
  67.5 2.9 %shard_map.121 = (bf16[64,1536]{1,0:T(8,128)(2,1)S(1)}, bf16[64,1536]{1,0:T(8,128)(2,1)S(1)}, bf16[80,128]{1,0:T(8,128)(2,1)S(1)}, bf16[16,120,128]{2,1,0:T(8,128)(2,1)}) custom-call(s32[6]{0:T(128)S(1)} %stack.19.place_ref, bf16[64,1536]{1,0:T(8,128)(2,1)S(1)} %copy-done, f32[72,256]{1,0:T(8,128)S(1)} %get-tuple-element.37.mine_ref, ...), custom_call_target="tpu_custom_call" | custom-call | flops 134217728 | bytes 1048576 | tf_op jit(solution)/shard_map/pallas_call | solution.py:383
  70.5 8.5 %all-to-all-start.1 = ((bf16[16,120,128]{2,1,0:T(8,128)(2,1)}), bf16[16,120,128]{2,1,0:T(8,128)(2,1)S(1)}, u32[]{:S(2)}, u32[]{:S(2)}) async-start(bf16[16,120,128]{2,1,0:T(8,128)(2,1)} %get-tuple-element.42), calls=%async_computation.1 | async-start | bytes 983040 | tf_op jit(solution)/shard_map/all_to_all | solution.py:401
  79.0 1.9 %collective-permute-start.2 = (bf16[64,1536]{1,0:T(8,128)(2,1)S(1)}, bf16[64,1536]{1,0:T(8,128)(2,1)S(1)}, u32[]{:S(2)}, u32[]{:S(2)}) collective-permute-start(bf16[64,1536]{1,0:T(8,128)(2,1)S(1)} %get-tuple-element.45), channel_id=1, source_target_pairs={{0,1},{1,0},{2,3},{3,2},{4,5},{5,4},{6,7},{7,6},{8,9},{9,8},{10,11... | collective-permute-start | bytes 589832 | tf_op jit(solution)/shard_map/ppermute | solution.py:402
  80.9 3.2 %collective-permute-start.1 = (bf16[80,128]{1,0:T(8,128)(2,1)S(1)}, bf16[80,128]{1,0:T(8,128)(2,1)S(1)}, u32[]{:S(2)}, u32[]{:S(2)}) collective-permute-start(bf16[80,128]{1,0:T(8,128)(2,1)S(1)} %get-tuple-element.43.pack_own_ref), channel_id=1, source_target_pairs={{0,256},{256,0},{1,257},{257,1},{2,258},{258,2},{3,259},{259,3},{4... | collective-permute-start | bytes 61448 | tf_op jit(solution)/shard_map/ppermute | solution.py:404
  84.0 4.0 %collective-permute-done.1.pack_pair_ref = bf16[80,128]{1,0:T(8,128)(2,1)S(1)} collective-permute-done((bf16[80,128]{1,0:T(8,128)(2,1)S(1)}, bf16[80,128]{1,0:T(8,128)(2,1)S(1)}, u32[]{:S(2)}, u32[]{:S(2)}) %collective-permute-start.1) | collective-permute-done | bytes 20512 | tf_op jit(solution)/shard_map/ppermute | solution.py:404
  88.0 2.2 %shard_map.122.d_query_ref = f32[64,256]{1,0:T(8,128)S(1)} custom-call(s32[6]{0:T(128)S(1)} %stack.19.place_ref, bf16[16,224,128]{2,1,0:T(8,128)(2,1)S(1)} %bitcast.17, bf16[192,128]{1,0:T(8,128)(2,1)S(1)} %pad_maximum_fusion.own_ref, bf16[192,128]{1,0:T(8,128)(2,1)S(1)} %get-tuple-element.36.pair_ref, bf16[80,128]{1,0:T(8,128)(2,1)S(1)} %get-tuple-element.43.pack_own_ref, ...), custom_call_target="tpu_custom_call" | custom-call | flops 268435456 | bytes 1048576 | tf_op jit(solution)/shard_map/pallas_call | solution.py:405
  90.3 0.0 collective-permute-done.2.got_ref
  90.3 0.7 shard_map.123
  91.0 7.9 %all-to-all-done.1.packs_ref = bf16[16,120,128]{2,1,0:T(8,128)(2,1)S(1)} async-done(((bf16[16,120,128]{2,1,0:T(8,128)(2,1)}), bf16[16,120,128]{2,1,0:T(8,128)(2,1)S(1)}, u32[]{:S(2)}, u32[]{:S(2)}) %all-to-all-start.1) | async-done | bytes 491552 | tf_op jit(solution)/shard_map/all_to_all | solution.py:401
  98.9 5.7 %all-to-all-start.2 = ((bf16[8,8,1536]{2,1,0:T(8,128)(2,1)}), bf16[8,8,1536]{2,1,0:T(8,128)(2,1)S(1)}, u32[]{:S(2)}, u32[]{:S(2)}) async-start(bf16[8,8,1536]{2,1,0:T(8,128)(2,1)} %bitcast.11), calls=%async_computation.2 | async-start | bytes 393216 | tf_op jit(solution)/shard_map/all_to_all | solution.py:413
  104.6 6.4 %all-gather.3 = f32[112,128]{1,0:T(8,128)S(1)} all-gather(f32[56,128]{1,0:T(8,128)S(1)} %shard_map.124), channel_id=5, replica_groups=mesh['yh'=2,'z'=16,'chip'=8,'core'=2] {'yh'}, dimensions={0}, use_global_device_ids=true | all-gather | bytes 86016 | tf_op jit(solution)/shard_map/all_gather | solution.py:411
  111.0 0.7 shard_map.125
  111.7 0.0 all-to-all-done.2.parts_ref
  111.7 6.8 %all-to-all-start.3 = ((bf16[16,56,128]{2,1,0:T(8,128)(2,1)}), bf16[16,56,128]{2,1,0:T(8,128)(2,1)S(1)}, u32[]{:S(2)}, u32[]{:S(2)}) async-start(bf16[16,56,128]{2,1,0:T(8,128)(2,1)} %shard_map.125), calls=%async_computation.3 | async-start | bytes 458752 | tf_op jit(solution)/shard_map/all_to_all | solution.py:415
  118.6 2.4 %shard_map.127 = (f32[192,128]{1,0:T(8,128)S(1)}, bf16[192,128]{1,0:T(8,128)(2,1)S(1)}) custom-call(s32[6]{0:T(128)S(1)} %stack.19.place_ref, bf16[16,224,128]{2,1,0:T(8,128)(2,1)S(1)} %bitcast.18, bf16[16,120,128]{2,1,0:T(8,128)(2,1)S(1)} %all-to-all-done.1.packs_ref, bf16[192,128]{1,0:T(8,128)(2,1)S(1)} %pad_maximum_fusion.own_ref, ...), custom_call_target="tpu_custom_call" | custom-call | flops 536870912 | bytes 1048576 | tf_op jit(solution)/shard_map/pallas_call | solution.py:418
  121.0 6.3 %all-gather.4 = bf16[384,128]{1,0:T(8,128)(2,1)S(1)} all-gather(bf16[192,128]{1,0:T(8,128)(2,1)S(1)} %get-tuple-element.51), channel_id=6, replica_groups=mesh['yh'=2,'z'=16,'chip'=8,'core'=2] {'yh'}, dimensions={0}, use_global_device_ids=true | all-gather | bytes 147456 | tf_op jit(solution)/shard_map/all_gather | solution.py:421
  127.3 1.2 shard_map.128
  128.4 0.6 shard_map.126
  129.1 3.8 %all-to-all-done.3.parts_ref = bf16[16,56,128]{2,1,0:T(8,128)(2,1)S(1)} async-done(((bf16[16,56,128]{2,1,0:T(8,128)(2,1)}), bf16[16,56,128]{2,1,0:T(8,128)(2,1)S(1)}, u32[]{:S(2)}, u32[]{:S(2)}) %all-to-all-start.3) | async-done | bytes 229408 | tf_op jit(solution)/shard_map/all_to_all | solution.py:415
  132.8 0.8 shard_map.129
  (7 shorter events, 0.1 us)
Async XLA Ops:
  0.6 8.0 %collective-permute-start = (bf16[8,1536]{1,0:T(8,128)(2,1)}, bf16[8,1536]{1,0:T(8,128)(2,1)S(1)}, u32[]{:S(2)}, u32[]{:S(2)}) collective-permute-start(bf16[8,1536]{1,0:T(8,128)(2,1)} %own_ref.1), channel_id=1, source_target_pairs={{14,16},{16,14},{15,17},{17,15},{30,32},{32,30},{31,33},{33,31},{4... | collective-permute-start | bytes 73736 | tf_op jit(solution)/shard_map/ppermute | solution.py:359
  2.1 6.6 %copy-start.1 = (bf16[8,1536]{1,0:T(8,128)(2,1)S(1)}, bf16[8,1536]{1,0:T(8,128)(2,1)}, u32[]{:S(2)}) copy-start(bf16[8,1536]{1,0:T(8,128)(2,1)} %own_ref.1) | copy-start | bytes 73732
  9.6 49.6 %all-to-all-start = ((bf16[16,16,1536]{2,1,0:T(8,128)(2,1)}), bf16[16,16,1536]{2,1,0:T(8,128)(2,1)S(1)}, u32[]{:S(2)}, u32[]{:S(2)}) async-start(bf16[16,16,1536]{2,1,0:T(8,128)(2,1)} %shard_map.118), calls=%async_computation | async-start | bytes 1572864 | tf_op jit(solution)/shard_map/all_to_all | solution.py:370
  59.2 8.4 %copy-start = (bf16[64,1536]{1,0:T(8,128)(2,1)S(1)}, bf16[64,1536]{1,0:T(8,128)(2,1)}, u32[]{:S(2)}) copy-start(bf16[64,1536]{1,0:T(8,128)(2,1)} %weight_hbm.1) | copy-start | bytes 589828
  61.3 6.2 %copy-start.2 = (f32[32,64]{1,0:T(8,128)S(1)}, f32[32,64]{1,0:T(8,128)}, u32[]{:S(2)}) copy-start(f32[32,64]{1,0:T(8,128)} %taps_ref.1) | copy-start | bytes 24580
  70.5 28.4 %all-to-all-start.1 = ((bf16[16,120,128]{2,1,0:T(8,128)(2,1)}), bf16[16,120,128]{2,1,0:T(8,128)(2,1)S(1)}, u32[]{:S(2)}, u32[]{:S(2)}) async-start(bf16[16,120,128]{2,1,0:T(8,128)(2,1)} %get-tuple-element.42), calls=%async_computation.1 | async-start | bytes 983040 | tf_op jit(solution)/shard_map/all_to_all | solution.py:401
  79.0 11.3 %collective-permute-start.2 = (bf16[64,1536]{1,0:T(8,128)(2,1)S(1)}, bf16[64,1536]{1,0:T(8,128)(2,1)S(1)}, u32[]{:S(2)}, u32[]{:S(2)}) collective-permute-start(bf16[64,1536]{1,0:T(8,128)(2,1)S(1)} %get-tuple-element.45), channel_id=1, source_target_pairs={{0,1},{1,0},{2,3},{3,2},{4,5},{5,4},{6,7},{7,6},{8,9},{9,8},{10,11... | collective-permute-start | bytes 589832 | tf_op jit(solution)/shard_map/ppermute | solution.py:402
  80.9 7.2 %collective-permute-start.1 = (bf16[80,128]{1,0:T(8,128)(2,1)S(1)}, bf16[80,128]{1,0:T(8,128)(2,1)S(1)}, u32[]{:S(2)}, u32[]{:S(2)}) collective-permute-start(bf16[80,128]{1,0:T(8,128)(2,1)S(1)} %get-tuple-element.43.pack_own_ref), channel_id=1, source_target_pairs={{0,256},{256,0},{1,257},{257,1},{2,258},{258,2},{3,259},{259,3},{4... | collective-permute-start | bytes 61448 | tf_op jit(solution)/shard_map/ppermute | solution.py:404
  98.9 12.9 %all-to-all-start.2 = ((bf16[8,8,1536]{2,1,0:T(8,128)(2,1)}), bf16[8,8,1536]{2,1,0:T(8,128)(2,1)S(1)}, u32[]{:S(2)}, u32[]{:S(2)}) async-start(bf16[8,8,1536]{2,1,0:T(8,128)(2,1)} %bitcast.11), calls=%async_computation.2 | async-start | bytes 393216 | tf_op jit(solution)/shard_map/all_to_all | solution.py:413
  111.7 21.1 %all-to-all-start.3 = ((bf16[16,56,128]{2,1,0:T(8,128)(2,1)}), bf16[16,56,128]{2,1,0:T(8,128)(2,1)S(1)}, u32[]{:S(2)}, u32[]{:S(2)}) async-start(bf16[16,56,128]{2,1,0:T(8,128)(2,1)} %shard_map.125), calls=%async_computation.3 | async-start | bytes 458752 | tf_op jit(solution)/shard_map/all_to_all | solution.py:415

commit v10 on v9

--- a/solution.py
+++ b/solution.py
@@ -291,7 +291,11 @@
         ref[2 * head : 3 * head] = d_value[:, at : at + width].astype(kind)
 
 
-def finish(place_ref, mine_ref, got_ref, query_ref, key_ref, value_ref):
+def finish(place_ref, mine_ref, got_ref, parts_ref, query_ref, key_ref, value_ref, block_ref):
+    rows = jnp.zeros(block_ref.shape, F32)
+    for j in range(parts_ref.shape[0]):
+        rows = rows + parts_ref[j].astype(F32)
+    block_ref[...] = rows.astype(BF16)
     total = mine_ref[...] + got_ref[1 - place_ref[4]].astype(F32)
     query_ref[...] = total[0:64].astype(BF16)
     key_ref[...] = total[64:128].astype(BF16)
@@ -325,13 +329,6 @@
     tap = rows_of(len(pieces), 128, [(z, piece[share : share + 1]) for z, piece in enumerate(pieces)])
     taps_ref[0:16] = tap[:, 0:64]
     taps_ref[16:32] = tap[:, 64:128]
-
-
-def sum_blocks(parts_ref, out_ref):
-    total = jnp.zeros(out_ref.shape, F32)
-    for j in range(parts_ref.shape[0]):
-        total = total + parts_ref[j].astype(F32)
-    out_ref[...] = total.astype(BF16)
 
 
 def body(query_rows, key_rows, value_rows, valid_frames, depth_kernel, mix_weight, out_grad):
@@ -419,9 +416,10 @@
         place, everyone, packs, own, pair, d_query
     )
     got = lax.all_gather(other, "yh", axis=0)
-    d_query, d_key, d_value = call(finish, (block, block, block), 2 ** 20, scalars=1)(place, mine, got)
-
-    block_out = call(sum_blocks, jax.ShapeDtypeStruct((rows8, model), BF16), 2 ** 20)(block_parts)
+    d_query, d_key, d_value, block_out = call(
+        finish, (block, block, block, jax.ShapeDtypeStruct((rows8, model), BF16)), 2 ** 20, scalars=1
+    )(place, mine, got, block_parts)
+
     mix_grad, tap_total = call(
         functools.partial(mix_place, norm, share),
         (jax.ShapeDtypeStruct((head, model), F32), jax.ShapeDtypeStruct((KSIZE, head), F32)),

time: 134 us -> 134 us (level)
  no operation moved by 1% of the time
where the time goes in v10:
time: 134 us
  blocking collectives  64.9 us (48%)
  starting transfers between devices  35.4 us (26%)
  waiting for transfers between devices  16.3 us (12%)
  Pallas kernels  14.8 us (11%)
  between operations  1.36 us (1%)
    all_gather x1, blocking collectives, body(): everyone = lax.all_gather(front, 'z', axis=0)  39.5 us
    all_gather x2, blocking collectives, body(): got = lax.all_gather(other, 'yh', axis=0)  12.5 us
    all_to_all x1, starting transfers between devices, body(): shared = lax.all_to_all(grads, tp, 0, 0, tiled=True)  8.6 us
    all_to_all x1, starting transfers between devices, body(): packs = lax.all_to_all(copies, 'z', 0, 0, tiled=True)  8.48 us
    all_to_all x1, waiting for transfers between devices, body(): packs = lax.all_to_all(copies, 'z', 0, 0, tiled=True)  7.86 us
    all_to_all x1, starting transfers between devices, body(): pieces = lax.all_to_all(spread, 'z', 0, 0, tiled=True)  6.84 us
    all_gather x1, blocking collectives, body(): both = lax.all_gather(own, 'yh', axis=0)  6.56 us
    all_gather x1, blocking collectives, body(): mix_both = lax.all_gather(mix_mine, 'yh', axis=0)  6.41 us
  transfers between devices with their start and end apart: 7, of which 3 were waited for; matrix products, arithmetic and copies ran while one was open for 1% of the time, Pallas kernels for 6%

profile of v10, /device:TPU:56, one launch (start us, length us, event | category | flops | bytes accessed | tf_op | source)
XLA Modules:
  0.0 133.6 jit_solution(4120925335347723868)
XLA Ops:
  0.6 0.7 collective-permute-start
  1.3 0.8 pad_maximum_fusion.own_ref
  2.1 6.6 %all-gather = bf16[384,128]{1,0:T(8,128)(2,1)S(1)} all-gather(bf16[192,128]{1,0:T(8,128)(2,1)S(1)} %pad_maximum_fusion.own_ref), channel_id=2, replica_groups=mesh['yh'=2,'z'=16,'chip'=8,'core'=2] {'yh'}, dimensions={0}, use_global_device_ids=true | all-gather | bytes 147456 | tf_op jit(solution)/shard_map/all_gather | solution.py:358
  8.6 0.0 collective-permute-done.rim_ref
  8.6 1.0 shard_map.118
  9.6 8.6 %all-to-all-start = ((bf16[16,16,1536]{2,1,0:T(8,128)(2,1)}), bf16[16,16,1536]{2,1,0:T(8,128)(2,1)S(1)}, u32[]{:S(2)}, u32[]{:S(2)}) async-start(bf16[16,16,1536]{2,1,0:T(8,128)(2,1)} %shard_map.118), calls=%async_computation | async-start | bytes 1572864 | tf_op jit(solution)/shard_map/all_to_all | solution.py:367
  18.8 0.1 stack.19.place_ref
  18.9 0.7 shard_map.119
  19.6 39.5 %all-gather.1 = bf16[3584,128]{1,0:T(8,128)(2,1)S(1)} all-gather(bf16[224,128]{1,0:T(8,128)(2,1)S(1)} %get-tuple-element.35), channel_id=3, replica_groups=mesh['yh'=2,'z'=16,'chip'=8,'core'=2] {'z'}, dimensions={0}, use_global_device_ids=true | all-gather | bytes 974848 | tf_op jit(solution)/shard_map/all_gather | solution.py:368
  59.1 0.0 all-to-all-done.shared_ref
  59.2 2.2 %shard_map.120 = (f32[72,256]{1,0:T(8,128)S(1)}, bf16[80,256]{1,0:T(8,128)(2,1)S(1)}) custom-call(s32[6]{0:T(128)S(1)} %stack.19.place_ref, bf16[16,224,128]{2,1,0:T(8,128)(2,1)S(1)} %bitcast.16, bf16[192,128]{1,0:T(8,128)(2,1)S(1)} %pad_maximum_fusion.own_ref, bf16[192,128]{1,0:T(8,128)(2,1)S(1)} %get-tuple-element.37.pair_ref), custom_call_target="tpu_custom_call" | custom-call | flops 268435456 | bytes 1048576 | tf_op jit(solution)/shard_map/pallas_call | solution.py:373
  61.3 0.0 copy-start.2
  61.3 6.2 %all-gather.2 = bf16[160,256]{1,0:T(8,128)(2,1)S(1)} all-gather(bf16[80,256]{1,0:T(8,128)(2,1)S(1)} %get-tuple-element.41), channel_id=4, replica_groups=mesh['yh'=2,'z'=16,'chip'=8,'core'=2] {'yh'}, dimensions={0}, use_global_device_ids=true | all-gather | bytes 122880 | tf_op jit(solution)/shard_map/all_gather | solution.py:377
  67.5 2.9 %shard_map.121 = (bf16[64,1536]{1,0:T(8,128)(2,1)S(1)}, bf16[64,1536]{1,0:T(8,128)(2,1)S(1)}, bf16[80,128]{1,0:T(8,128)(2,1)S(1)}, bf16[16,120,128]{2,1,0:T(8,128)(2,1)}) custom-call(s32[6]{0:T(128)S(1)} %stack.19.place_ref, bf16[64,1536]{1,0:T(8,128)(2,1)S(1)} %copy-done, f32[72,256]{1,0:T(8,128)S(1)} %get-tuple-element.38.mine_ref, ...), custom_call_target="tpu_custom_call" | custom-call | flops 134217728 | bytes 1048576 | tf_op jit(solution)/shard_map/pallas_call | solution.py:380
  70.5 8.5 %all-to-all-start.1 = ((bf16[16,120,128]{2,1,0:T(8,128)(2,1)}), bf16[16,120,128]{2,1,0:T(8,128)(2,1)S(1)}, u32[]{:S(2)}, u32[]{:S(2)}) async-start(bf16[16,120,128]{2,1,0:T(8,128)(2,1)} %get-tuple-element.43), calls=%async_computation.1 | async-start | bytes 983040 | tf_op jit(solution)/shard_map/all_to_all | solution.py:398
  79.0 1.9 %collective-permute-start.2 = (bf16[64,1536]{1,0:T(8,128)(2,1)S(1)}, bf16[64,1536]{1,0:T(8,128)(2,1)S(1)}, u32[]{:S(2)}, u32[]{:S(2)}) collective-permute-start(bf16[64,1536]{1,0:T(8,128)(2,1)S(1)} %get-tuple-element.46), channel_id=1, source_target_pairs={{0,1},{1,0},{2,3},{3,2},{4,5},{5,4},{6,7},{7,6},{8,9},{9,8},{10,11... | collective-permute-start | bytes 589832 | tf_op jit(solution)/shard_map/ppermute | solution.py:399
  80.9 3.2 %collective-permute-start.1 = (bf16[80,128]{1,0:T(8,128)(2,1)S(1)}, bf16[80,128]{1,0:T(8,128)(2,1)S(1)}, u32[]{:S(2)}, u32[]{:S(2)}) collective-permute-start(bf16[80,128]{1,0:T(8,128)(2,1)S(1)} %get-tuple-element.44.pack_own_ref), channel_id=1, source_target_pairs={{0,256},{256,0},{1,257},{257,1},{2,258},{258,2},{3,259},{259,3},{4... | collective-permute-start | bytes 61448 | tf_op jit(solution)/shard_map/ppermute | solution.py:401
  84.0 4.0 %collective-permute-done.1.pack_pair_ref = bf16[80,128]{1,0:T(8,128)(2,1)S(1)} collective-permute-done((bf16[80,128]{1,0:T(8,128)(2,1)S(1)}, bf16[80,128]{1,0:T(8,128)(2,1)S(1)}, u32[]{:S(2)}, u32[]{:S(2)}) %collective-permute-start.1) | collective-permute-done | bytes 20512 | tf_op jit(solution)/shard_map/ppermute | solution.py:401
  88.0 2.2 %shard_map.122.d_query_ref = f32[64,256]{1,0:T(8,128)S(1)} custom-call(s32[6]{0:T(128)S(1)} %stack.19.place_ref, bf16[16,224,128]{2,1,0:T(8,128)(2,1)S(1)} %bitcast.17, bf16[192,128]{1,0:T(8,128)(2,1)S(1)} %pad_maximum_fusion.own_ref, bf16[192,128]{1,0:T(8,128)(2,1)S(1)} %get-tuple-element.37.pair_ref, bf16[80,128]{1,0:T(8,128)(2,1)S(1)} %get-tuple-element.44.pack_own_ref, ...), custom_call_target="tpu_custom_call" | custom-call | flops 268435456 | bytes 1048576 | tf_op jit(solution)/shard_map/pallas_call | solution.py:402
  90.3 0.0 collective-permute-done.2.got_ref
  90.3 0.7 shard_map.123
  91.0 7.9 %all-to-all-done.1.packs_ref = bf16[16,120,128]{2,1,0:T(8,128)(2,1)S(1)} async-done(((bf16[16,120,128]{2,1,0:T(8,128)(2,1)}), bf16[16,120,128]{2,1,0:T(8,128)(2,1)S(1)}, u32[]{:S(2)}, u32[]{:S(2)}) %all-to-all-start.1) | async-done | bytes 491552 | tf_op jit(solution)/shard_map/all_to_all | solution.py:398
  98.9 5.7 %all-to-all-start.2 = ((bf16[8,8,1536]{2,1,0:T(8,128)(2,1)}), bf16[8,8,1536]{2,1,0:T(8,128)(2,1)S(1)}, u32[]{:S(2)}, u32[]{:S(2)}) async-start(bf16[8,8,1536]{2,1,0:T(8,128)(2,1)} %bitcast.12), calls=%async_computation.2 | async-start | bytes 393216 | tf_op jit(solution)/shard_map/all_to_all | solution.py:410
  104.6 6.4 %all-gather.4 = f32[112,128]{1,0:T(8,128)S(1)} all-gather(f32[56,128]{1,0:T(8,128)S(1)} %shard_map.125), channel_id=6, replica_groups=mesh['yh'=2,'z'=16,'chip'=8,'core'=2] {'yh'}, dimensions={0}, use_global_device_ids=true | all-gather | bytes 86016 | tf_op jit(solution)/shard_map/all_gather | solution.py:408
  111.0 0.7 shard_map.126
  111.7 0.0 all-to-all-done.2.parts_ref
  111.7 6.8 %all-to-all-start.3 = ((bf16[16,56,128]{2,1,0:T(8,128)(2,1)}), bf16[16,56,128]{2,1,0:T(8,128)(2,1)S(1)}, u32[]{:S(2)}, u32[]{:S(2)}) async-start(bf16[16,56,128]{2,1,0:T(8,128)(2,1)} %shard_map.126), calls=%async_computation.3 | async-start | bytes 458752 | tf_op jit(solution)/shard_map/all_to_all | solution.py:412
  118.6 2.4 %shard_map.124 = (f32[192,128]{1,0:T(8,128)S(1)}, bf16[192,128]{1,0:T(8,128)(2,1)S(1)}) custom-call(s32[6]{0:T(128)S(1)} %stack.19.place_ref, bf16[16,224,128]{2,1,0:T(8,128)(2,1)S(1)} %bitcast.18, bf16[16,120,128]{2,1,0:T(8,128)(2,1)S(1)} %all-to-all-done.1.packs_ref, bf16[192,128]{1,0:T(8,128)(2,1)S(1)} %pad_maximum_fusion.own_ref, ...), custom_call_target="tpu_custom_call" | custom-call | flops 536870912 | bytes 1048576 | tf_op jit(solution)/shard_map/pallas_call | solution.py:415
  121.0 6.3 %all-gather.3 = bf16[384,128]{1,0:T(8,128)(2,1)S(1)} all-gather(bf16[192,128]{1,0:T(8,128)(2,1)S(1)} %get-tuple-element.50), channel_id=5, replica_groups=mesh['yh'=2,'z'=16,'chip'=8,'core'=2] {'yh'}, dimensions={0}, use_global_device_ids=true | all-gather | bytes 147456 | tf_op jit(solution)/shard_map/all_gather | solution.py:418
  127.3 1.2 shard_map.127
  128.5 4.4 %all-to-all-done.3.parts_ref = bf16[16,56,128]{2,1,0:T(8,128)(2,1)S(1)} async-done(((bf16[16,56,128]{2,1,0:T(8,128)(2,1)}), bf16[16,56,128]{2,1,0:T(8,128)(2,1)S(1)}, u32[]{:S(2)}, u32[]{:S(2)}) %all-to-all-start.3) | async-done | bytes 229408 | tf_op jit(solution)/shard_map/all_to_all | solution.py:412
  132.8 0.8 shard_map.128
  (6 shorter events, 0.0 us)
Async XLA Ops:
  0.6 8.0 %collective-permute-start = (bf16[8,1536]{1,0:T(8,128)(2,1)}, bf16[8,1536]{1,0:T(8,128)(2,1)S(1)}, u32[]{:S(2)}, u32[]{:S(2)}) collective-permute-start(bf16[8,1536]{1,0:T(8,128)(2,1)} %own_ref.1), channel_id=1, source_target_pairs={{14,16},{16,14},{15,17},{17,15},{30,32},{32,30},{31,33},{33,31},{4... | collective-permute-start | bytes 73736 | tf_op jit(solution)/shard_map/ppermute | solution.py:356
  2.1 6.6 %copy-start.1 = (bf16[8,1536]{1,0:T(8,128)(2,1)S(1)}, bf16[8,1536]{1,0:T(8,128)(2,1)}, u32[]{:S(2)}) copy-start(bf16[8,1536]{1,0:T(8,128)(2,1)} %own_ref.1) | copy-start | bytes 73732
  9.6 49.6 %all-to-all-start = ((bf16[16,16,1536]{2,1,0:T(8,128)(2,1)}), bf16[16,16,1536]{2,1,0:T(8,128)(2,1)S(1)}, u32[]{:S(2)}, u32[]{:S(2)}) async-start(bf16[16,16,1536]{2,1,0:T(8,128)(2,1)} %shard_map.118), calls=%async_computation | async-start | bytes 1572864 | tf_op jit(solution)/shard_map/all_to_all | solution.py:367
  59.2 8.4 %copy-start = (bf16[64,1536]{1,0:T(8,128)(2,1)S(1)}, bf16[64,1536]{1,0:T(8,128)(2,1)}, u32[]{:S(2)}) copy-start(bf16[64,1536]{1,0:T(8,128)(2,1)} %weight_hbm.1) | copy-start | bytes 589828
  61.3 6.2 %copy-start.2 = (f32[32,64]{1,0:T(8,128)S(1)}, f32[32,64]{1,0:T(8,128)}, u32[]{:S(2)}) copy-start(f32[32,64]{1,0:T(8,128)} %taps_ref.1) | copy-start | bytes 24580
  70.5 28.4 %all-to-all-start.1 = ((bf16[16,120,128]{2,1,0:T(8,128)(2,1)}), bf16[16,120,128]{2,1,0:T(8,128)(2,1)S(1)}, u32[]{:S(2)}, u32[]{:S(2)}) async-start(bf16[16,120,128]{2,1,0:T(8,128)(2,1)} %get-tuple-element.43), calls=%async_computation.1 | async-start | bytes 983040 | tf_op jit(solution)/shard_map/all_to_all | solution.py:398
  79.0 11.3 %collective-permute-start.2 = (bf16[64,1536]{1,0:T(8,128)(2,1)S(1)}, bf16[64,1536]{1,0:T(8,128)(2,1)S(1)}, u32[]{:S(2)}, u32[]{:S(2)}) collective-permute-start(bf16[64,1536]{1,0:T(8,128)(2,1)S(1)} %get-tuple-element.46), channel_id=1, source_target_pairs={{0,1},{1,0},{2,3},{3,2},{4,5},{5,4},{6,7},{7,6},{8,9},{9,8},{10,11... | collective-permute-start | bytes 589832 | tf_op jit(solution)/shard_map/ppermute | solution.py:399
  80.9 7.2 %collective-permute-start.1 = (bf16[80,128]{1,0:T(8,128)(2,1)S(1)}, bf16[80,128]{1,0:T(8,128)(2,1)S(1)}, u32[]{:S(2)}, u32[]{:S(2)}) collective-permute-start(bf16[80,128]{1,0:T(8,128)(2,1)S(1)} %get-tuple-element.44.pack_own_ref), channel_id=1, source_target_pairs={{0,256},{256,0},{1,257},{257,1},{2,258},{258,2},{3,259},{259,3},{4... | collective-permute-start | bytes 61448 | tf_op jit(solution)/shard_map/ppermute | solution.py:401
  98.9 12.9 %all-to-all-start.2 = ((bf16[8,8,1536]{2,1,0:T(8,128)(2,1)}), bf16[8,8,1536]{2,1,0:T(8,128)(2,1)S(1)}, u32[]{:S(2)}, u32[]{:S(2)}) async-start(bf16[8,8,1536]{2,1,0:T(8,128)(2,1)} %bitcast.12), calls=%async_computation.2 | async-start | bytes 393216 | tf_op jit(solution)/shard_map/all_to_all | solution.py:410
  111.7 21.1 %all-to-all-start.3 = ((bf16[16,56,128]{2,1,0:T(8,128)(2,1)}), bf16[16,56,128]{2,1,0:T(8,128)(2,1)S(1)}, u32[]{:S(2)}, u32[]{:S(2)}) async-start(bf16[16,56,128]{2,1,0:T(8,128)(2,1)} %shard_map.126), calls=%async_computation.3 | async-start | bytes 458752 | tf_op jit(solution)/shard_map/all_to_all | solution.py:412

commit v11 on v9

--- a/solution.py
+++ b/solution.py
@@ -126,24 +126,28 @@
     edges = jnp.where(middle, pltpu.roll(side_pair, width // 2, 1), side_own)
     query = jnp.concatenate([own_ref[0:head].astype(F32), pair_ref[0:head].astype(F32), edges], axis=1) * scale
     query = jnp.concatenate([query, rows_of(16, lanes, [(6, 1.0)])], axis=0).astype(BF16)
-    peak = jnp.full((1, lanes), LOW, F32)
+    peak = jnp.full((8, lanes), LOW, F32)
     for b in range(blocks):
         key = jnp.concatenate(
             [all_ref[b, head : 2 * head], rows_of(16, width, [(6, bias_of(place_ref, b, spot_rows))]).astype(BF16)], axis=0
         )
         score = dot00(key, query)
         score_ref[b] = score
-        peak = jnp.maximum(peak, jnp.max(score, axis=0, keepdims=True))
-    total = jnp.zeros((1, lanes), F32)
+        for at in range(0, width, 8):
+            peak = jnp.maximum(peak, score[at : at + 8])
+    peak = jnp.max(peak, axis=0, keepdims=True)
+    total = jnp.zeros((8, lanes), F32)
     out = jnp.zeros((head, lanes), F32)
     for b in range(0, blocks, 2):
         pair_weight = []
         for k in (b, b + 1):
             weight = jnp.exp(score_ref[k] - peak)
-            total = total + jnp.sum(weight, axis=0, keepdims=True)
+            for at in range(0, width, 8):
+                total = total + weight[at : at + 8]
             pair_weight.append(weight.astype(BF16))
         values = jnp.concatenate([all_ref[b, 2 * head : 3 * head], all_ref[b + 1, 2 * head : 3 * head]], axis=1)
         out = out + dot10(values, jnp.concatenate(pair_weight, axis=0))
+    total = jnp.sum(total, axis=0, keepdims=True)
     out = out / total
     lse = peak + jnp.log(total)
     both = jnp.concatenate([out, jnp.broadcast_to(lse, (8, lanes))], axis=0)

time: 134 us -> 134 us (level)
  no operation moved by 1% of the time
where the time goes in v11:
time: 134 us
  blocking collectives  64.9 us (48%)
  starting transfers between devices  35.4 us (26%)
  waiting for transfers between devices  15.7 us (12%)
  Pallas kernels  15.4 us (11%)
  between operations  1.36 us (1%)
    all_gather x1, blocking collectives, body(): everyone = lax.all_gather(front, 'z', axis=0)  39.5 us
    all_gather x2, blocking collectives, body(): got = lax.all_gather(other, 'yh', axis=0)  12.5 us
    all_to_all x1, starting transfers between devices, body(): shared = lax.all_to_all(grads, tp, 0, 0, tiled=True)  8.6 us
    all_to_all x1, starting transfers between devices, body(): packs = lax.all_to_all(copies, 'z', 0, 0, tiled=True)  8.49 us
    all_to_all x1, waiting for transfers between devices, body(): packs = lax.all_to_all(copies, 'z', 0, 0, tiled=True)  7.86 us
    all_to_all x1, starting transfers between devices, body(): pieces = lax.all_to_all(spread, 'z', 0, 0, tiled=True)  6.84 us
    all_gather x1, blocking collectives, body(): both = lax.all_gather(own, 'yh', axis=0)  6.56 us
    all_gather x1, blocking collectives, body(): mix_both = lax.all_gather(mix_mine, 'yh', axis=0)  6.41 us
  transfers between devices with their start and end apart: 7, of which 3 were waited for; matrix products, arithmetic and copies ran while one was open for 1% of the time, Pallas kernels for 6%

profile of v11, /device:TPU:56, one launch (start us, length us, event | category | flops | bytes accessed | tf_op | source)
XLA Modules:
  0.0 133.6 jit_solution(10279882520005653014)
XLA Ops:
  0.6 0.7 collective-permute-start
  1.3 0.8 pad_maximum_fusion.own_ref
  2.1 6.6 %all-gather = bf16[384,128]{1,0:T(8,128)(2,1)S(1)} all-gather(bf16[192,128]{1,0:T(8,128)(2,1)S(1)} %pad_maximum_fusion.own_ref), channel_id=2, replica_groups=mesh['yh'=2,'z'=16,'chip'=8,'core'=2] {'yh'}, dimensions={0}, use_global_device_ids=true | all-gather | bytes 147456 | tf_op jit(solution)/shard_map/all_gather | solution.py:365
  8.6 0.0 collective-permute-done.rim_ref
  8.6 1.0 shard_map.118
  9.6 8.6 %all-to-all-start = ((bf16[16,16,1536]{2,1,0:T(8,128)(2,1)}), bf16[16,16,1536]{2,1,0:T(8,128)(2,1)S(1)}, u32[]{:S(2)}, u32[]{:S(2)}) async-start(bf16[16,16,1536]{2,1,0:T(8,128)(2,1)} %shard_map.118), calls=%async_computation | async-start | bytes 1572864 | tf_op jit(solution)/shard_map/all_to_all | solution.py:374
  18.8 0.1 stack.19.place_ref
  18.9 0.7 shard_map.119
  19.6 39.5 %all-gather.1 = bf16[3584,128]{1,0:T(8,128)(2,1)S(1)} all-gather(bf16[224,128]{1,0:T(8,128)(2,1)S(1)} %get-tuple-element.34), channel_id=3, replica_groups=mesh['yh'=2,'z'=16,'chip'=8,'core'=2] {'z'}, dimensions={0}, use_global_device_ids=true | all-gather | bytes 974848 | tf_op jit(solution)/shard_map/all_gather | solution.py:375
  59.1 0.0 all-to-all-done.shared_ref
  59.2 2.1 %shard_map.120 = (f32[72,256]{1,0:T(8,128)S(1)}, bf16[80,256]{1,0:T(8,128)(2,1)S(1)}) custom-call(s32[6]{0:T(128)S(1)} %stack.19.place_ref, bf16[16,224,128]{2,1,0:T(8,128)(2,1)S(1)} %bitcast.16, bf16[192,128]{1,0:T(8,128)(2,1)S(1)} %pad_maximum_fusion.own_ref, bf16[192,128]{1,0:T(8,128)(2,1)S(1)} %get-tuple-element.36.pair_ref), custom_call_target="tpu_custom_call" | custom-call | flops 268435456 | bytes 1048576 | tf_op jit(solution)/shard_map/pallas_call | solution.py:380
  61.3 0.0 copy-start.2
  61.3 6.2 %all-gather.2 = bf16[160,256]{1,0:T(8,128)(2,1)S(1)} all-gather(bf16[80,256]{1,0:T(8,128)(2,1)S(1)} %get-tuple-element.40), channel_id=4, replica_groups=mesh['yh'=2,'z'=16,'chip'=8,'core'=2] {'yh'}, dimensions={0}, use_global_device_ids=true | all-gather | bytes 122880 | tf_op jit(solution)/shard_map/all_gather | solution.py:384
  67.5 2.9 %shard_map.121 = (bf16[64,1536]{1,0:T(8,128)(2,1)S(1)}, bf16[64,1536]{1,0:T(8,128)(2,1)S(1)}, bf16[80,128]{1,0:T(8,128)(2,1)S(1)}, bf16[16,120,128]{2,1,0:T(8,128)(2,1)}) custom-call(s32[6]{0:T(128)S(1)} %stack.19.place_ref, bf16[64,1536]{1,0:T(8,128)(2,1)S(1)} %copy-done, f32[72,256]{1,0:T(8,128)S(1)} %get-tuple-element.37.mine_ref, ...), custom_call_target="tpu_custom_call" | custom-call | flops 134217728 | bytes 1048576 | tf_op jit(solution)/shard_map/pallas_call | solution.py:387
  70.4 8.5 %all-to-all-start.1 = ((bf16[16,120,128]{2,1,0:T(8,128)(2,1)}), bf16[16,120,128]{2,1,0:T(8,128)(2,1)S(1)}, u32[]{:S(2)}, u32[]{:S(2)}) async-start(bf16[16,120,128]{2,1,0:T(8,128)(2,1)} %get-tuple-element.42), calls=%async_computation.1 | async-start | bytes 983040 | tf_op jit(solution)/shard_map/all_to_all | solution.py:405
  78.9 1.9 %collective-permute-start.2 = (bf16[64,1536]{1,0:T(8,128)(2,1)S(1)}, bf16[64,1536]{1,0:T(8,128)(2,1)S(1)}, u32[]{:S(2)}, u32[]{:S(2)}) collective-permute-start(bf16[64,1536]{1,0:T(8,128)(2,1)S(1)} %get-tuple-element.45), channel_id=1, source_target_pairs={{0,1},{1,0},{2,3},{3,2},{4,5},{5,4},{6,7},{7,6},{8,9},{9,8},{10,11... | collective-permute-start | bytes 589832 | tf_op jit(solution)/shard_map/ppermute | solution.py:406
  80.8 3.1 %collective-permute-start.1 = (bf16[80,128]{1,0:T(8,128)(2,1)S(1)}, bf16[80,128]{1,0:T(8,128)(2,1)S(1)}, u32[]{:S(2)}, u32[]{:S(2)}) collective-permute-start(bf16[80,128]{1,0:T(8,128)(2,1)S(1)} %get-tuple-element.43.pack_own_ref), channel_id=1, source_target_pairs={{0,256},{256,0},{1,257},{257,1},{2,258},{258,2},{3,259},{259,3},{4... | collective-permute-start | bytes 61448 | tf_op jit(solution)/shard_map/ppermute | solution.py:408
  84.0 4.0 %collective-permute-done.1.pack_pair_ref = bf16[80,128]{1,0:T(8,128)(2,1)S(1)} collective-permute-done((bf16[80,128]{1,0:T(8,128)(2,1)S(1)}, bf16[80,128]{1,0:T(8,128)(2,1)S(1)}, u32[]{:S(2)}, u32[]{:S(2)}) %collective-permute-start.1) | collective-permute-done | bytes 20512 | tf_op jit(solution)/shard_map/ppermute | solution.py:408
  88.0 2.2 %shard_map.122.d_query_ref = f32[64,256]{1,0:T(8,128)S(1)} custom-call(s32[6]{0:T(128)S(1)} %stack.19.place_ref, bf16[16,224,128]{2,1,0:T(8,128)(2,1)S(1)} %bitcast.17, bf16[192,128]{1,0:T(8,128)(2,1)S(1)} %pad_maximum_fusion.own_ref, bf16[192,128]{1,0:T(8,128)(2,1)S(1)} %get-tuple-element.36.pair_ref, bf16[80,128]{1,0:T(8,128)(2,1)S(1)} %get-tuple-element.43.pack_own_ref, ...), custom_call_target="tpu_custom_call" | custom-call | flops 268435456 | bytes 1048576 | tf_op jit(solution)/shard_map/pallas_call | solution.py:409
  90.2 0.0 collective-permute-done.2.got_ref
  90.2 0.7 shard_map.123
  91.0 7.9 %all-to-all-done.1.packs_ref = bf16[16,120,128]{2,1,0:T(8,128)(2,1)S(1)} async-done(((bf16[16,120,128]{2,1,0:T(8,128)(2,1)}), bf16[16,120,128]{2,1,0:T(8,128)(2,1)S(1)}, u32[]{:S(2)}, u32[]{:S(2)}) %all-to-all-start.1) | async-done | bytes 491552 | tf_op jit(solution)/shard_map/all_to_all | solution.py:405
  98.8 5.7 %all-to-all-start.2 = ((bf16[8,8,1536]{2,1,0:T(8,128)(2,1)}), bf16[8,8,1536]{2,1,0:T(8,128)(2,1)S(1)}, u32[]{:S(2)}, u32[]{:S(2)}) async-start(bf16[8,8,1536]{2,1,0:T(8,128)(2,1)} %bitcast.11), calls=%async_computation.2 | async-start | bytes 393216 | tf_op jit(solution)/shard_map/all_to_all | solution.py:417
  104.6 6.4 %all-gather.3 = f32[112,128]{1,0:T(8,128)S(1)} all-gather(f32[56,128]{1,0:T(8,128)S(1)} %shard_map.124), channel_id=5, replica_groups=mesh['yh'=2,'z'=16,'chip'=8,'core'=2] {'yh'}, dimensions={0}, use_global_device_ids=true | all-gather | bytes 86016 | tf_op jit(solution)/shard_map/all_gather | solution.py:415
  111.0 0.7 shard_map.125
  111.7 6.8 %all-to-all-start.3 = ((bf16[16,56,128]{2,1,0:T(8,128)(2,1)}), bf16[16,56,128]{2,1,0:T(8,128)(2,1)S(1)}, u32[]{:S(2)}, u32[]{:S(2)}) async-start(bf16[16,56,128]{2,1,0:T(8,128)(2,1)} %shard_map.125), calls=%async_computation.3 | async-start | bytes 458752 | tf_op jit(solution)/shard_map/all_to_all | solution.py:419
  118.5 2.4 %shard_map.127 = (f32[192,128]{1,0:T(8,128)S(1)}, bf16[192,128]{1,0:T(8,128)(2,1)S(1)}) custom-call(s32[6]{0:T(128)S(1)} %stack.19.place_ref, bf16[16,224,128]{2,1,0:T(8,128)(2,1)S(1)} %bitcast.18, bf16[16,120,128]{2,1,0:T(8,128)(2,1)S(1)} %all-to-all-done.1.packs_ref, bf16[192,128]{1,0:T(8,128)(2,1)S(1)} %pad_maximum_fusion.own_ref, ...), custom_call_target="tpu_custom_call" | custom-call | flops 536870912 | bytes 1048576 | tf_op jit(solution)/shard_map/pallas_call | solution.py:422
  121.0 6.3 %all-gather.4 = bf16[384,128]{1,0:T(8,128)(2,1)S(1)} all-gather(bf16[192,128]{1,0:T(8,128)(2,1)S(1)} %get-tuple-element.51), channel_id=6, replica_groups=mesh['yh'=2,'z'=16,'chip'=8,'core'=2] {'yh'}, dimensions={0}, use_global_device_ids=true | all-gather | bytes 147456 | tf_op jit(solution)/shard_map/all_gather | solution.py:425
  127.2 1.2 shard_map.128
  128.4 0.6 shard_map.126
  129.0 3.8 %all-to-all-done.3.parts_ref = bf16[16,56,128]{2,1,0:T(8,128)(2,1)S(1)} async-done(((bf16[16,56,128]{2,1,0:T(8,128)(2,1)}), bf16[16,56,128]{2,1,0:T(8,128)(2,1)S(1)}, u32[]{:S(2)}, u32[]{:S(2)}) %all-to-all-start.3) | async-done | bytes 229408 | tf_op jit(solution)/shard_map/all_to_all | solution.py:419
  132.8 0.8 shard_map.129
  (7 shorter events, 0.1 us)
Async XLA Ops:
  0.6 8.0 %collective-permute-start = (bf16[8,1536]{1,0:T(8,128)(2,1)}, bf16[8,1536]{1,0:T(8,128)(2,1)S(1)}, u32[]{:S(2)}, u32[]{:S(2)}) collective-permute-start(bf16[8,1536]{1,0:T(8,128)(2,1)} %own_ref.1), channel_id=1, source_target_pairs={{14,16},{16,14},{15,17},{17,15},{30,32},{32,30},{31,33},{33,31},{4... | collective-permute-start | bytes 73736 | tf_op jit(solution)/shard_map/ppermute | solution.py:363
  2.1 6.6 %copy-start.1 = (bf16[8,1536]{1,0:T(8,128)(2,1)S(1)}, bf16[8,1536]{1,0:T(8,128)(2,1)}, u32[]{:S(2)}) copy-start(bf16[8,1536]{1,0:T(8,128)(2,1)} %own_ref.1) | copy-start | bytes 73732
  9.6 49.6 %all-to-all-start = ((bf16[16,16,1536]{2,1,0:T(8,128)(2,1)}), bf16[16,16,1536]{2,1,0:T(8,128)(2,1)S(1)}, u32[]{:S(2)}, u32[]{:S(2)}) async-start(bf16[16,16,1536]{2,1,0:T(8,128)(2,1)} %shard_map.118), calls=%async_computation | async-start | bytes 1572864 | tf_op jit(solution)/shard_map/all_to_all | solution.py:374
  59.2 8.3 %copy-start = (bf16[64,1536]{1,0:T(8,128)(2,1)S(1)}, bf16[64,1536]{1,0:T(8,128)(2,1)}, u32[]{:S(2)}) copy-start(bf16[64,1536]{1,0:T(8,128)(2,1)} %weight_hbm.1) | copy-start | bytes 589828
  61.3 6.2 %copy-start.2 = (f32[32,64]{1,0:T(8,128)S(1)}, f32[32,64]{1,0:T(8,128)}, u32[]{:S(2)}) copy-start(f32[32,64]{1,0:T(8,128)} %taps_ref.1) | copy-start | bytes 24580
  70.4 28.4 %all-to-all-start.1 = ((bf16[16,120,128]{2,1,0:T(8,128)(2,1)}), bf16[16,120,128]{2,1,0:T(8,128)(2,1)S(1)}, u32[]{:S(2)}, u32[]{:S(2)}) async-start(bf16[16,120,128]{2,1,0:T(8,128)(2,1)} %get-tuple-element.42), calls=%async_computation.1 | async-start | bytes 983040 | tf_op jit(solution)/shard_map/all_to_all | solution.py:405
  78.9 11.3 %collective-permute-start.2 = (bf16[64,1536]{1,0:T(8,128)(2,1)S(1)}, bf16[64,1536]{1,0:T(8,128)(2,1)S(1)}, u32[]{:S(2)}, u32[]{:S(2)}) collective-permute-start(bf16[64,1536]{1,0:T(8,128)(2,1)S(1)} %get-tuple-element.45), channel_id=1, source_target_pairs={{0,1},{1,0},{2,3},{3,2},{4,5},{5,4},{6,7},{7,6},{8,9},{9,8},{10,11... | collective-permute-start | bytes 589832 | tf_op jit(solution)/shard_map/ppermute | solution.py:406
  80.8 7.2 %collective-permute-start.1 = (bf16[80,128]{1,0:T(8,128)(2,1)S(1)}, bf16[80,128]{1,0:T(8,128)(2,1)S(1)}, u32[]{:S(2)}, u32[]{:S(2)}) collective-permute-start(bf16[80,128]{1,0:T(8,128)(2,1)S(1)} %get-tuple-element.43.pack_own_ref), channel_id=1, source_target_pairs={{0,256},{256,0},{1,257},{257,1},{2,258},{258,2},{3,259},{259,3},{4... | collective-permute-start | bytes 61448 | tf_op jit(solution)/shard_map/ppermute | solution.py:408
  98.8 12.9 %all-to-all-start.2 = ((bf16[8,8,1536]{2,1,0:T(8,128)(2,1)}), bf16[8,8,1536]{2,1,0:T(8,128)(2,1)S(1)}, u32[]{:S(2)}, u32[]{:S(2)}) async-start(bf16[8,8,1536]{2,1,0:T(8,128)(2,1)} %bitcast.11), calls=%async_computation.2 | async-start | bytes 393216 | tf_op jit(solution)/shard_map/all_to_all | solution.py:417
  111.7 21.1 %all-to-all-start.3 = ((bf16[16,56,128]{2,1,0:T(8,128)(2,1)}), bf16[16,56,128]{2,1,0:T(8,128)(2,1)S(1)}, u32[]{:S(2)}, u32[]{:S(2)}) async-start(bf16[16,56,128]{2,1,0:T(8,128)(2,1)} %shard_map.125), calls=%async_computation.3 | async-start | bytes 458752 | tf_op jit(solution)/shard_map/all_to_all | solution.py:419
